TPU v7x, 32 devices: a whole 2x2x4 slice. The times are simulated.
32 devices in a mesh: slot: 4 (over y, x), seq: 8 (over z, core).
Axes of the slice: x: 2, y: 2, z: 4, core: 2. Of those that a mesh axis runs over, the one named last changes fastest.
Arguments:
- hidden_in: bfloat16 [6144, 2048], P(('slot', 'seq')), may hold values from -6 to 6
- seq_lens: int32 [4, 8], P('slot'), may hold values from 1 to 1216, as said below
- group_order: int32 [4, 16], P('slot'), may hold values from 0 to 15, as said below
- attn_gain: bfloat16 [2048], P(('slot', 'seq')), may hold values from 0.5 to 1.5
- wq_down: bfloat16 [2048, 1024], P(('slot', 'seq')), may hold values from -0.125 to 0.125
- q_gain: bfloat16 [1024], P(('slot', 'seq')), may hold values from 0.5 to 1.5
- wq_up: bfloat16 [1024, 4096], P(('slot', 'seq')), may hold values from -0.1875 to 0.1875
- w_key: bfloat16 [2048, 256], P(('slot', 'seq')), may hold values from -0.125 to 0.125
- w_value: bfloat16 [2048, 256], P(('slot', 'seq')), may hold values from -0.125 to 0.125
- w_out: bfloat16 [4096, 2048], P(('slot', 'seq')), may hold values from -0.375 to 0.375
- ffn_gain: bfloat16 [2048], P(('slot', 'seq')), may hold values from 0.5 to 1.5
- w_gate: bfloat16 [2048, 5632], P(('slot', 'seq')), may hold values from -0.125 to 0.125
- w_up: bfloat16 [2048, 5632], P(('slot', 'seq')), may hold values from -0.125 to 0.125
- w_down: bfloat16 [5632, 2048], P(('slot', 'seq')), may hold values from -0.078125 to 0.078125
- out_grad: bfloat16 [6144, 2048], P(('slot', 'seq')), may hold values from -6 to 6
Outputs:
- layer_out: bfloat16 [6144, 2048], P(('slot', 'seq'))
- in_grad: bfloat16 [6144, 2048], P(('slot', 'seq'))
- grad_attn_gain: float32 [2048], P(('slot', 'seq'))
- grad_wq_down: float32 [2048, 1024], P(('slot', 'seq'))
- grad_q_gain: float32 [1024], P(('slot', 'seq'))
- grad_wq_up: float32 [1024, 4096], P(('slot', 'seq'))
- grad_w_key: float32 [2048, 256], P(('slot', 'seq'))
- grad_w_value: float32 [2048, 256], P(('slot', 'seq'))
- grad_w_out: float32 [4096, 2048], P(('slot', 'seq'))
- grad_ffn_gain: float32 [2048], P(('slot', 'seq'))
- grad_w_gate: float32 [2048, 5632], P(('slot', 'seq'))
- grad_w_up: float32 [2048, 5632], P(('slot', 'seq'))
- grad_w_down: float32 [5632, 2048], P(('slot', 'seq'))
Inputs may be any that keep to these rules, and one draw needn't show every extreme that they name: `seq_lens`: sequences lie end to end from slot position 0; the rest of the slot is padding, under 1/16 of 1536 plus 8. The first is at least 1024 long and is the longest; in some slot it is exactly the most. `group_order`: row s lists, for the d-th device along seq, the two blocks of 96 slot positions that it stores, at entries 2 d and 2 d + 1: entry 2 d is d and entry 2 d + 1 lies in the upper half; each block appears once.
All inputs are finite; a program needn't handle non-finite values.
Results may differ from a plain program's by a relative error of at most 0.02.
Values may be sent and summed in bfloat16 or wider, within the bound.
No kernel may reach another device: no remote copies, remote signals or barrier semaphores. Data moves between devices by JAX's collectives and lax.ppermute only.
A program may use at most 384 MiB of HBM per device.

v0:
```python
import math

import jax
import jax.numpy as jnp
from jax import lax
from jax.sharding import PartitionSpec as P

H = 16
HD = 256
TOK_DEV = 192
GROUP = 96


EPS = 1e-05
ROPE_BASE = 10000.0


def norm_scale(values):
    return lax.rsqrt(jnp.mean(values * values, axis=-1, keepdims=True) + EPS)


def norm_back(values, scale, gain, upstream):
    scaled = gain * upstream
    gain_grad = jnp.sum(upstream * values * scale, axis=0)
    inner = jnp.mean(scaled * values, axis=-1, keepdims=True)
    return (gain_grad, scale * scaled - values * scale * scale * scale * inner)


def rope_tables(position, width):
    half = width // 2
    freq = ROPE_BASE ** (-2.0 * jnp.arange(half, dtype=jnp.float32) / width)
    angle = position.astype(jnp.float32)[:, None] * freq[None, :]
    return (jnp.cos(angle), jnp.sin(angle))


def rotate(values, cosine, sine):
    half = values.shape[-1] // 2
    first = values[..., :half]
    second = values[..., half:]
    return jnp.concatenate(
        [first * cosine - second * sine, first * sine + second * cosine], axis=-1
    )


def unrotate(grads, cosine, sine):
    half = grads.shape[-1] // 2
    first = grads[..., :half]
    second = grads[..., half:]
    return jnp.concatenate(
        [first * cosine + second * sine, second * cosine - first * sine], axis=-1
    )


def place_info(row_index, order, lengths):
    device = row_index // TOK_DEV
    local = row_index % TOK_DEV
    pick = 2 * device + local // GROUP
    table = jnp.arange(order.shape[0], dtype=jnp.int32)
    group_id = jnp.sum(jnp.where(pick[:, None] == table[None, :], order[None, :], 0), axis=1)
    slot_pos = group_id * GROUP + local % GROUP
    ends = jnp.cumsum(lengths)
    passed = slot_pos[:, None] >= ends[None, :]
    segment = jnp.sum(passed.astype(jnp.int32), axis=1)
    start = jnp.sum(jnp.where(passed, lengths[None, :], 0), axis=1)
    return (slot_pos, segment, slot_pos - start, segment < lengths.shape[0])


def block_size(count):
    size = min(512, count)
    while count % size:
        size -= 1
    return size


def contract_last(left, right):
    return lax.dot_general(
        left, right, (((1,), (1,)), ((), ())), preferred_element_type=jnp.float32
    )


def contract_first(left, right):
    return lax.dot_general(
        left, right, (((0,), (0,)), ((), ())), preferred_element_type=jnp.float32
    )


def body(
    hidden_in,
    seq_lens,
    group_order,
    attn_gain,
    wq_down,
    q_gain,
    wq_up,
    w_key,
    w_value,
    w_out,
    ffn_gain,
    w_gate,
    w_up,
    w_down,
    out_grad,
):
    lengths = seq_lens[0]
    order = group_order[0]
    tokens_here = hidden_in.shape[0]
    query_count = tokens_here * H
    scale = 1.0 / math.sqrt(HD)
    rows_here = lax.axis_index("seq") * tokens_here + jnp.arange(tokens_here, dtype=jnp.int32)
    slot_pos, segment, seq_pos, valid = place_info(rows_here, order, lengths)
    cosine, sine = rope_tables(seq_pos, HD)
    query_seg = jnp.repeat(segment, H)
    query_pos = jnp.repeat(slot_pos, H)
    attn_set = (
        lax.all_gather(attn_gain, ("slot", "seq"), axis=0, tiled=True),
        lax.all_gather(wq_down, ("slot", "seq"), axis=0, tiled=True),
        lax.all_gather(q_gain, ("slot", "seq"), axis=0, tiled=True),
        lax.all_gather(wq_up, ("slot", "seq"), axis=0, tiled=True),
        lax.all_gather(w_key, ("slot", "seq"), axis=0, tiled=True),
        lax.all_gather(w_value, ("slot", "seq"), axis=0, tiled=True),
        lax.all_gather(w_out, ("slot", "seq"), axis=0, tiled=True),
    )
    gain_one, down_q, gain_q, up_q, key_proj, value_proj, out_proj = attn_set
    inputs = hidden_in.astype(jnp.float32)
    scale_one = norm_scale(inputs)
    gain_one_f = gain_one.astype(jnp.float32)
    normed_one = (inputs * scale_one * gain_one_f).astype(jnp.bfloat16)
    query_low = jnp.dot(normed_one, down_q, preferred_element_type=jnp.float32)
    scale_q = norm_scale(query_low)
    gain_q_f = gain_q.astype(jnp.float32)
    query_normed = (query_low * scale_q * gain_q_f).astype(jnp.bfloat16)
    query_full = jnp.dot(query_normed, up_q, preferred_element_type=jnp.float32).reshape(
        tokens_here, H, HD
    )
    query_rows = (
        (rotate(query_full, cosine[:, None, :], sine[:, None, :]) * scale)
        .astype(jnp.bfloat16)
        .reshape(query_count, HD)
    )
    keys_rot = rotate(
        jnp.dot(normed_one, key_proj, preferred_element_type=jnp.float32), cosine, sine
    ).astype(jnp.bfloat16)
    values_here = jnp.dot(normed_one, value_proj, preferred_element_type=jnp.float32).astype(
        jnp.bfloat16
    )
    empty = (
        jnp.full((query_count,), -1e30, jnp.float32),
        jnp.zeros((query_count,), jnp.float32),
        jnp.zeros((query_count, HD), jnp.float32),
    )
    key_rows = lax.all_gather(keys_rot, "seq", axis=0, tiled=True)
    value_rows = lax.all_gather(values_here, "seq", axis=0, tiled=True)
    count = key_rows.shape[0]
    attend_size = block_size(count)

    def one_block(state, number):
        top, total, summed = state
        offset = number * attend_size
        key_block = lax.dynamic_slice_in_dim(key_rows, offset, attend_size, 0)
        value_block = lax.dynamic_slice_in_dim(value_rows, offset, attend_size, 0)
        key_index = offset + jnp.arange(attend_size, dtype=jnp.int32)
        key_pos, key_seg, _, _ = place_info(key_index, order, lengths)
        allowed = (query_seg[:, None] == key_seg[None, :]) & (
            key_pos[None, :] <= query_pos[:, None]
        )
        scores = jnp.where(allowed, contract_last(query_rows, key_block), -1e30)
        new_top = jnp.maximum(top, jnp.max(scores, axis=1))
        fade = jnp.exp(top - new_top)
        weights = jnp.where(allowed, jnp.exp(scores - new_top[:, None]), 0.0)
        total = total * fade + jnp.sum(weights, axis=1)
        summed = summed * fade[:, None] + jnp.dot(
            weights.astype(jnp.bfloat16), value_block, preferred_element_type=jnp.float32
        )
        return ((new_top, total, summed), None)

    state, _ = lax.scan(one_block, empty, jnp.arange(count // attend_size))
    top, total, summed = state
    log_total = top + jnp.log(total)
    attended = summed / total[:, None]
    att_low = attended.reshape(tokens_here, H * HD).astype(jnp.bfloat16)
    middle = inputs + jnp.dot(att_low, out_proj, preferred_element_type=jnp.float32)
    ffn_set = (
        lax.all_gather(ffn_gain, ("slot", "seq"), axis=0, tiled=True),
        lax.all_gather(w_gate, ("slot", "seq"), axis=0, tiled=True),
        lax.all_gather(w_up, ("slot", "seq"), axis=0, tiled=True),
        lax.all_gather(w_down, ("slot", "seq"), axis=0, tiled=True),
    )
    gain_two, gate_proj, up_proj, down_proj = ffn_set
    scale_two = norm_scale(middle)
    gain_two_f = gain_two.astype(jnp.float32)
    normed_two = (middle * scale_two * gain_two_f).astype(jnp.bfloat16)
    gate = jnp.dot(normed_two, gate_proj, preferred_element_type=jnp.float32)
    upward = jnp.dot(normed_two, up_proj, preferred_element_type=jnp.float32)
    sigma = jax.nn.sigmoid(gate)
    hidden = (gate * sigma * upward).astype(jnp.bfloat16)
    result = middle + jnp.dot(hidden, down_proj, preferred_element_type=jnp.float32)
    layer_out = result.astype(jnp.bfloat16)
    gain_two, gate_proj, up_proj, down_proj = (
        lax.all_gather(ffn_gain, ("slot", "seq"), axis=0, tiled=True),
        lax.all_gather(w_gate, ("slot", "seq"), axis=0, tiled=True),
        lax.all_gather(w_up, ("slot", "seq"), axis=0, tiled=True),
        lax.all_gather(w_down, ("slot", "seq"), axis=0, tiled=True),
    )
    out_cot = out_grad.astype(jnp.float32) * valid[:, None].astype(jnp.float32)
    cot_low = out_cot.astype(jnp.bfloat16)
    hidden_grad = contract_last(cot_low, down_proj)
    gate_grad = (hidden_grad * upward * sigma * (1.0 + gate * (1.0 - sigma))).astype(jnp.bfloat16)
    upward_grad = (hidden_grad * gate * sigma).astype(jnp.bfloat16)
    normed_two_grad = contract_last(gate_grad, gate_proj) + contract_last(upward_grad, up_proj)
    grad_gain_two, middle_part = norm_back(middle, scale_two, gain_two_f, normed_two_grad)
    middle_grad = out_cot + middle_part
    grad_down = contract_first(hidden, cot_low)
    grad_gate = contract_first(normed_two, gate_grad)
    grad_upward = contract_first(normed_two, upward_grad)
    ffn_out = (
        lax.psum_scatter(grad_gate, ("slot", "seq"), scatter_dimension=0, tiled=True),
        lax.psum_scatter(grad_upward, ("slot", "seq"), scatter_dimension=0, tiled=True),
        lax.psum_scatter(grad_down, ("slot", "seq"), scatter_dimension=0, tiled=True),
    )
    gain_one, down_q, gain_q, up_q, key_proj, value_proj, out_proj = (
        lax.all_gather(attn_gain, ("slot", "seq"), axis=0, tiled=True),
        lax.all_gather(wq_down, ("slot", "seq"), axis=0, tiled=True),
        lax.all_gather(q_gain, ("slot", "seq"), axis=0, tiled=True),
        lax.all_gather(wq_up, ("slot", "seq"), axis=0, tiled=True),
        lax.all_gather(w_key, ("slot", "seq"), axis=0, tiled=True),
        lax.all_gather(w_value, ("slot", "seq"), axis=0, tiled=True),
        lax.all_gather(w_out, ("slot", "seq"), axis=0, tiled=True),
    )
    middle_low = middle_grad.astype(jnp.bfloat16)
    grad_out = contract_first(att_low, middle_low)
    att_grad = contract_last(middle_low, out_proj).reshape(query_count, HD).astype(jnp.bfloat16)
    delta = jnp.sum(att_grad.astype(jnp.float32) * attended, axis=1)
    keys_all, values_all = (
        lax.all_gather(keys_rot, "seq", axis=0, tiled=True),
        lax.all_gather(values_here, "seq", axis=0, tiled=True),
    )
    slot_rows = keys_all.shape[0]
    size = block_size(slot_rows)

    def back_block(query_grad, number):
        offset = number * size
        key_block = lax.dynamic_slice_in_dim(keys_all, offset, size, 0)
        value_block = lax.dynamic_slice_in_dim(values_all, offset, size, 0)
        key_index = offset + jnp.arange(size, dtype=jnp.int32)
        key_pos, key_seg, _, _ = place_info(key_index, order, lengths)
        allowed = (query_seg[:, None] == key_seg[None, :]) & (
            key_pos[None, :] <= query_pos[:, None]
        )
        prob = jnp.where(
            allowed, jnp.exp(contract_last(query_rows, key_block) - log_total[:, None]), 0.0
        )
        prob_grad = contract_last(att_grad, value_block)
        score_grad = (prob * (prob_grad - delta[:, None])).astype(jnp.bfloat16)
        value_grad = contract_first(prob.astype(jnp.bfloat16), att_grad)
        key_grad = contract_first(score_grad, query_rows)
        query_grad = query_grad + jnp.dot(score_grad, key_block, preferred_element_type=jnp.float32)
        return (query_grad, (key_grad, value_grad))

    query_grad, (key_grads, value_grads) = lax.scan(
        back_block, jnp.zeros((query_count, HD), jnp.float32), jnp.arange(slot_rows // size)
    )
    key_sum, value_sum = (
        lax.psum_scatter(
            key_grads.reshape(slot_rows, HD).astype(jnp.bfloat16),
            "seq",
            scatter_dimension=0,
            tiled=True,
        ).astype(jnp.float32),
        lax.psum_scatter(
            value_grads.reshape(slot_rows, HD).astype(jnp.bfloat16),
            "seq",
            scatter_dimension=0,
            tiled=True,
        ).astype(jnp.float32),
    )
    key_pre = unrotate(key_sum, cosine, sine).astype(jnp.bfloat16)
    value_pre = value_sum.astype(jnp.bfloat16)
    query_pre = (
        unrotate(
            query_grad.reshape(tokens_here, H, HD) * scale, cosine[:, None, :], sine[:, None, :]
        )
        .reshape(tokens_here, H * HD)
        .astype(jnp.bfloat16)
    )
    grad_up_q = contract_first(query_normed, query_pre)
    normed_q_grad = contract_last(query_pre, up_q)
    grad_gain_q, low_part = norm_back(query_low, scale_q, gain_q_f, normed_q_grad)
    query_low_grad = low_part.astype(jnp.bfloat16)
    grad_down_q = contract_first(normed_one, query_low_grad)
    grad_key = contract_first(normed_one, key_pre)
    grad_value = contract_first(normed_one, value_pre)
    normed_one_grad = (
        contract_last(query_low_grad, down_q)
        + contract_last(key_pre, key_proj)
        + contract_last(value_pre, value_proj)
    )
    grad_gain_one, input_part = norm_back(inputs, scale_one, gain_one_f, normed_one_grad)
    in_grad = (middle_grad + input_part).astype(jnp.bfloat16)
    attn_out = (
        lax.psum_scatter(grad_gain_one, ("slot", "seq"), scatter_dimension=0, tiled=True),
        lax.psum_scatter(grad_down_q, ("slot", "seq"), scatter_dimension=0, tiled=True),
        lax.psum_scatter(grad_gain_q, ("slot", "seq"), scatter_dimension=0, tiled=True),
        lax.psum_scatter(grad_up_q, ("slot", "seq"), scatter_dimension=0, tiled=True),
        lax.psum_scatter(grad_key, ("slot", "seq"), scatter_dimension=0, tiled=True),
        lax.psum_scatter(grad_value, ("slot", "seq"), scatter_dimension=0, tiled=True),
        lax.psum_scatter(grad_out, ("slot", "seq"), scatter_dimension=0, tiled=True),
        lax.psum_scatter(grad_gain_two, ("slot", "seq"), scatter_dimension=0, tiled=True),
    )
    return (
        layer_out,
        in_grad,
        attn_out[0],
        attn_out[1],
        attn_out[2],
        attn_out[3],
        attn_out[4],
        attn_out[5],
        attn_out[6],
        attn_out[7],
        ffn_out[0],
        ffn_out[1],
        ffn_out[2],
    )


def solution(mesh):
    placed = (
        P(("slot", "seq"), None),
        P("slot", None),
        P("slot", None),
        P(("slot", "seq")),
        P(("slot", "seq"), None),
        P(("slot", "seq")),
        P(("slot", "seq"), None),
        P(("slot", "seq"), None),
        P(("slot", "seq"), None),
        P(("slot", "seq"), None),
        P(("slot", "seq")),
        P(("slot", "seq"), None),
        P(("slot", "seq"), None),
        P(("slot", "seq"), None),
        P(("slot", "seq"), None),
    )
    return jax.shard_map(
        body,
        mesh=mesh,
        in_specs=placed,
        out_specs=(
            P(("slot", "seq"), None),
            P(("slot", "seq"), None),
            P(("slot", "seq")),
            P(("slot", "seq"), None),
            P(("slot", "seq")),
            P(("slot", "seq"), None),
            P(("slot", "seq"), None),
            P(("slot", "seq"), None),
            P(("slot", "seq"), None),
            P(("slot", "seq")),
            P(("slot", "seq"), None),
            P(("slot", "seq"), None),
            P(("slot", "seq"), None),
        ),
        check_vma=False,
    )
```

profile of v0, /device:TPU:0, one launch (start us, length us, event | category | flops | bytes accessed | tf_op | source)
XLA Modules:
  0.0 3459.1 jit_solution(1133880235450454812)
XLA Ops:
  13.9 42.2 %all-reduce.7 = (bf16[2048]{0:T(1024)(128)(2,1)S(1)}, bf16[1024]{0:T(1024)(128)(2,1)S(1)}, bf16[2048]{0:T(1024)(128)(2,1)S(1)}) all-reduce(bf16[2048]{0:T(1024)(128)(2,1)S(1)} %dynamic-update-slice, bf16[1024]{0:T(1024)(128)(2,1)S(1)} %dynamic-update-slice.1, ...), channel_id=1, replica_groups=mesh['slot'=4,'seq'=8] {'slot','seq'}, use_global_device_ids=true, to_apply=%add | all-reduce | flops 5120 | bytes 20480
  69.8 53.6 %all-gather.15.cloned.1.call-done = bf16[2048,256]{1,0:T(8,128)(2,1)} async-done(((bf16[64,256]{1,0:T(8,128)(2,1)}), bf16[2048,256]{1,0:T(8,128)(2,1)}) %all-gather.15.cloned.1.call-update) | async-done | bytes 1048592 | tf_op jit(solution)/shard_map/all_gather | solution.py:120
  141.2 17.3 all_gather.56
  158.5 29.4 all-gather.11.cloned.1.call-done
  191.2 75.5 %all-gather.13.cloned.1.call-done = bf16[1024,4096]{1,0:T(8,128)(2,1)} async-done(((bf16[32,4096]{1,0:T(8,128)(2,1)}), bf16[1024,4096]{1,0:T(8,128)(2,1)}) %all-gather.13.cloned.1.call-update) | async-done | bytes 8388624 | tf_op jit(solution)/shard_map/all_gather | solution.py:118
  275.1 50.2 %while.36 = (s32[]{:T(128)}, f32[3072]{0:T(1024)S(1)}, f32[3072]{0:T(1024)S(1)}, f32[3072,256]{1,0:T(8,128)}, s32[3]{0:T(128)S(1)}, /*index=5*/s32[1,16]{1,0:T(1...) while((s32[]{:T(128)}, f32[3072]{0:T(1024)S(1)}, ...), condition=%wide.region_12.13_spmd.clone, body=%wide.region_7.12_spmd.clone.sunk | while | flops 1642927104 | bytes 52801388 | solution.py:176
  332.7 50.4 %all-gather.17.cloned.1.call-done = bf16[4096,2048]{1,0:T(8,128)(2,1)} async-done(((bf16[128,2048]{1,0:T(8,128)(2,1)}), bf16[4096,2048]{1,0:T(8,128)(2,1)}) %all-gather.17.cloned.1.call-update) | async-done | bytes 16777232 | tf_op jit(solution)/shard_map/all_gather | solution.py:121
  392.1 136.5 %all-gather.19.cloned.1.call-done = bf16[2048,5632]{1,0:T(8,128)(2,1)} async-done(((bf16[64,5632]{1,0:T(8,128)(2,1)}), bf16[2048,5632]{1,0:T(8,128)(2,1)}) %all-gather.19.cloned.1.call-update) | async-done | bytes 23068688 | tf_op jit(solution)/shard_map/all_gather | solution.py:184
  540.6 133.7 %all-gather.21.cloned.1.call-done = bf16[2048,5632]{1,0:T(8,128)(2,1)} async-done(((bf16[64,5632]{1,0:T(8,128)(2,1)}), bf16[2048,5632]{1,0:T(8,128)(2,1)}) %all-gather.21.cloned.1.call-update) | async-done | bytes 23068688 | tf_op jit(solution)/shard_map/all_gather | solution.py:185
  686.4 133.6 %all-gather.23.cloned.1.call-done = bf16[5632,2048]{1,0:T(8,128)(2,1)} async-done(((bf16[176,2048]{1,0:T(8,128)(2,1)}), bf16[5632,2048]{1,0:T(8,128)(2,1)}) %all-gather.23.cloned.1.call-update) | async-done | bytes 23068688 | tf_op jit(solution)/shard_map/all_gather | solution.py:186
  883.2 58.3 %while.37 = (s32[]{:T(128)}, f32[3072,256]{1,0:T(8,128)}, bf16[3,512,256]{2,1,0:T(8,128)(2,1)}, bf16[3,512,256]{2,1,0:T(8,128)(2,1)}, s32[3]{0:T(128)S(1)}, /*in...) while((s32[]{:T(128)}, f32[3072,256]{1,0:T(8,128)}, ...), condition=%wide.region_19.20_spmd.clone, body=%wide.region_16.19_spmd.clone.sunk | while | flops 4042315776 | bytes 124661888 | solution.py:259
  942.2 29.2 reduce-scatter.11.cloned.1.call-done
  974.8 29.1 reduce-scatter.13.cloned.1.call-done
  1047.1 19.5 fusion.123
  1066.6 19.5 fusion.124
  1087.3 19.5 fusion.78
  1125.3 38.2 %all-reduce.6 = (f32[2048]{0:T(1024)S(1)}, f32[1024]{0:T(1024)S(1)}, f32[2048]{0:T(1024)S(1)}) all-reduce(f32[2048]{0:T(1024)S(1)} %get-tuple-element.568, f32[1024]{0:T(1024)S(1)} %copy-done.56, f32[2048]{0:T(1024)S(1)} %copy-done.55), channel_id=4, replica_groups=mesh['slot'=4,'seq'=8] {'slot','seq'}, use_global_device_ids=true, to_apply=%region_25.26.clone | all-reduce | flops 5120 | bytes 40960
  1168.2 110.8 %reduce-scatter.21.cloned.1.call-done = f32[64,256]{1,0:T(8,128)} async-done(((f32[2048,256]{1,0:T(8,128)}), f32[64,256]{1,0:T(8,128)}) %reduce-scatter.21.cloned.1.call-update) | async-done | bytes 65552 | tf_op jit(solution)/shard_map/reduce_scatter | solution.py:305
  1278.9 150.6 %reduce-scatter.15.cloned.1.call-done = f32[64,1024]{1,0:T(8,128)} async-done(((f32[2048,1024]{1,0:T(8,128)}), f32[64,1024]{1,0:T(8,128)}) %reduce-scatter.15.cloned.1.call-update) | async-done | bytes 262160 | tf_op jit(solution)/shard_map/reduce_scatter | solution.py:301
  1429.5 187.2 %reduce-scatter.17.cloned.1.call-done = f32[32,4096]{1,0:T(8,128)} async-done(((f32[1024,4096]{1,0:T(8,128)}), f32[32,4096]{1,0:T(8,128)}) %reduce-scatter.17.cloned.1.call-update) | async-done | bytes 524304 | tf_op jit(solution)/shard_map/reduce_scatter | solution.py:303
  1616.7 361.5 %reduce-scatter.23.cloned.1.call-done = f32[128,2048]{1,0:T(8,128)} async-done(((f32[4096,2048]{1,0:T(8,128)}), f32[128,2048]{1,0:T(8,128)}) %reduce-scatter.23.cloned.1.call-update) | async-done | bytes 1048592 | tf_op jit(solution)/shard_map/reduce_scatter | solution.py:306
  1978.2 491.2 %reduce-scatter.25.cloned.1.call-done = f32[64,5632]{1,0:T(8,128)} async-done(((f32[2048,5632]{1,0:T(8,128)}), f32[64,5632]{1,0:T(8,128)}) %reduce-scatter.25.cloned.1.call-update) | async-done | bytes 1441808 | tf_op jit(solution)/shard_map/reduce_scatter | solution.py:216
  2469.4 491.2 %reduce-scatter.27.cloned.1.call-done = f32[64,5632]{1,0:T(8,128)} async-done(((f32[2048,5632]{1,0:T(8,128)}), f32[64,5632]{1,0:T(8,128)}) %reduce-scatter.27.cloned.1.call-update) | async-done | bytes 1441808 | tf_op jit(solution)/shard_map/reduce_scatter | solution.py:217
  2960.6 491.2 %reduce-scatter.29.cloned.1.call-done = f32[176,2048]{1,0:T(8,128)} async-done(((f32[5632,2048]{1,0:T(8,128)}), f32[176,2048]{1,0:T(8,128)}) %reduce-scatter.29.cloned.1.call-update) | async-done | bytes 1441808 | tf_op jit(solution)/shard_map/reduce_scatter | solution.py:218
  (374 shorter events, 328.0 us)
Async XLA Ops:
  7.2 60.4 %all-gather.9.cloned.1.call-start = ((), (), s32[]{:S(2)}) async-start(), calls=%async_computation.10 | async-start | bytes 1081344 | tf_op jit(solution)/shard_map/all_gather | solution.py:119
  8.0 115.4 %all-gather.15.cloned.1.call-start = ((), (), s32[]{:S(2)}) async-start(), calls=%async_computation.13 | async-start | bytes 1081344 | tf_op jit(solution)/shard_map/all_gather | solution.py:120
  8.7 179.1 %all-gather.11.cloned.1.call-start = ((), (), s32[]{:S(2)}) async-start(), calls=%async_computation.11 | async-start | bytes 4325376 | tf_op jit(solution)/shard_map/all_gather | solution.py:116
  9.5 257.2 %all-gather.13.cloned.1.call-start = ((), (), s32[]{:S(2)}) async-start(), calls=%async_computation.12 | async-start | bytes 8650752 | tf_op jit(solution)/shard_map/all_gather | solution.py:118
  10.0 373.0 %all-gather.17.cloned.1.call-start = ((), (), s32[]{:S(2)}) async-start(), calls=%async_computation.14 | async-start | bytes 17301504 | tf_op jit(solution)/shard_map/all_gather | solution.py:121
  10.6 518.0 %all-gather.19.cloned.1.call-start = ((), (), s32[]{:S(2)}) async-start(), calls=%async_computation.15 | async-start | bytes 23789568 | tf_op jit(solution)/shard_map/all_gather | solution.py:184
  11.2 663.1 %all-gather.21.cloned.1.call-start = ((), (), s32[]{:S(2)}) async-start(), calls=%async_computation.16 | async-start | bytes 23789568 | tf_op jit(solution)/shard_map/all_gather | solution.py:185
  11.9 808.1 %all-gather.23.cloned.1.call-start = ((), (), s32[]{:S(2)}) async-start(), calls=%async_computation.17 | async-start | bytes 23789568 | tf_op jit(solution)/shard_map/all_gather | solution.py:186
  12.7 958.7 %reduce-scatter.11.cloned.1.call-start = ((), (), s32[]{:S(2)}) async-start(), calls=%async_computation.18 | async-start | bytes 884736 | tf_op jit(solution)/shard_map/reduce_scatter | solution.py:263
  56.1 210.6 %copy-start.37 = (f32[1024]{0:T(1024)}, f32[1024]{0:T(1024)S(1)}, u32[]{:S(2)}) copy-start(f32[1024]{0:T(1024)S(1)} %convert_element_type.151) | copy-start | bytes 12292
  56.7 807.2 %copy-start.53 = (f32[192]{0:T(256)}, f32[192]{0:T(256)S(1)}, u32[]{:S(2)}) copy-start(f32[192]{0:T(256)S(1)} %compare_convert_fusion.1) | copy-start | bytes 2308
  69.7 203.4 %copy-start.29 = (f32[192,128]{1,0:T(8,128)}, f32[192,128]{1,0:T(8,128)S(1)}, u32[]{:S(2)}) copy-start(f32[192,128]{1,0:T(8,128)S(1)} %get-tuple-element.649) | copy-start | bytes 294916
  69.7 203.4 %copy-start.31 = (f32[192,128]{1,0:T(8,128)}, f32[192,128]{1,0:T(8,128)S(1)}, u32[]{:S(2)}) copy-start(f32[192,128]{1,0:T(8,128)S(1)} %get-tuple-element.650) | copy-start | bytes 294916
  392.1 282.2 %copy-start.14 = (bf16[192,2048]{1,0:T(8,128)(2,1)}, bf16[192,2048]{1,0:T(8,128)(2,1)S(1)}, u32[]{:S(2)}) copy-start(bf16[192,2048]{1,0:T(8,128)(2,1)S(1)} %multiply_convert_fusion.3) | copy-start | bytes 2359300
  540.6 279.4 %copy-start.22 = (bf16[192,2048]{1,0:T(8,128)(2,1)S(1)}, bf16[192,2048]{1,0:T(8,128)(2,1)}, u32[]{:S(2)}) copy-start(bf16[192,2048]{1,0:T(8,128)(2,1)} %param.33) | copy-start | bytes 2359300
  941.6 62.3 %reduce-scatter.13.cloned.1.call-start = ((), (), s32[]{:S(2)}) async-start(), calls=%async_computation.19 | async-start | bytes 884736 | tf_op jit(solution)/shard_map/reduce_scatter | solution.py:269
  942.1 226.0 %reduce-scatter.19.cloned.1.call-start = ((), (), s32[]{:S(2)}) async-start(), calls=%async_computation.22 | async-start | bytes 2162688 | tf_op jit(solution)/shard_map/reduce_scatter | solution.py:304
  974.8 304.2 %reduce-scatter.21.cloned.1.call-start = ((), (), s32[]{:S(2)}) async-start(), calls=%async_computation.23 | async-start | bytes 2162688 | tf_op jit(solution)/shard_map/reduce_scatter | solution.py:305
  1007.1 422.4 %reduce-scatter.15.cloned.1.call-start = ((), (), s32[]{:S(2)}) async-start(), calls=%async_computation.20 | async-start | bytes 8650752 | tf_op jit(solution)/shard_map/reduce_scatter | solution.py:301
  1020.8 595.8 %reduce-scatter.17.cloned.1.call-start = ((), (), s32[]{:S(2)}) async-start(), calls=%async_computation.21 | async-start | bytes 17301504 | tf_op jit(solution)/shard_map/reduce_scatter | solution.py:303
  1029.9 948.3 %reduce-scatter.23.cloned.1.call-start = ((), (), s32[]{:S(2)}) async-start(), calls=%async_computation.24 | async-start | bytes 34603008 | tf_op jit(solution)/shard_map/reduce_scatter | solution.py:306
  1046.0 1423.4 %reduce-scatter.25.cloned.1.call-start = ((), (), s32[]{:S(2)}) async-start(), calls=%async_computation.25 | async-start | bytes 47579136 | tf_op jit(solution)/shard_map/reduce_scatter | solution.py:216
  1066.6 1894.0 %reduce-scatter.27.cloned.1.call-start = ((), (), s32[]{:S(2)}) async-start(), calls=%async_computation.26 | async-start | bytes 47579136 | tf_op jit(solution)/shard_map/reduce_scatter | solution.py:217
  1086.2 2365.6 %reduce-scatter.29.cloned.1.call-start = ((), (), s32[]{:S(2)}) async-start(), calls=%async_computation.27 | async-start | bytes 47579136 | tf_op jit(solution)/shard_map/reduce_scatter | solution.py:218
  (79 other events, 1271.3 us)
Sparse Core Ops, SparseCore 0:
  11.1 56.4 all-gather.8
  70.6 52.7 all-gather.14
  126.4 61.3 all-gather.10
  190.7 75.9 all-gather.12
  269.5 113.4 all-gather.16
  385.8 142.7 all-gather.18
  531.5 142.7 all-gather.20
  677.2 142.7 all-gather.22
  941.7 29.6 reduce-scatter.10
  974.2 29.6 reduce-scatter.12
  1006.7 135.2 reduce-scatter.18
  1144.8 134.0 reduce-scatter.20
  1281.8 147.6 reduce-scatter.14
  1432.2 184.3 reduce-scatter.16
  1619.4 358.7 reduce-scatter.22
  1980.9 488.4 reduce-scatter.24
  2472.1 488.4 reduce-scatter.26
  2963.3 488.4 reduce-scatter.28
where the time goes:
time: 3470 us; the launch traced here: 3460 us
  waiting for transfers between devices  2970 us (86%)
  matrix products  292 us (8%)
  blocking collectives  114 us (3%)
    reduce_scatter x1, waiting for transfers between devices, body(): lax.psum_scatter(grad_gate, ('slot', 'seq'), scatter_dimension=0, tiled=T...  491 us
    reduce_scatter x1, waiting for transfers between devices, body(): lax.psum_scatter(grad_down, ('slot', 'seq'), scatter_dimension=0, tiled=T...  491 us
    reduce_scatter x1, waiting for transfers between devices, body(): lax.psum_scatter(grad_upward, ('slot', 'seq'), scatter_dimension=0, tiled...  491 us
    reduce_scatter x1, waiting for transfers between devices, body(): lax.psum_scatter(grad_out, ('slot', 'seq'), scatter_dimension=0, tiled=True)  362 us
    reduce_scatter x1, waiting for transfers between devices, body(): lax.psum_scatter(grad_up_q, ('slot', 'seq'), scatter_dimension=0, tiled=T...  187 us
    reduce_scatter x1, waiting for transfers between devices, body(): lax.psum_scatter(grad_down_q, ('slot', 'seq'), scatter_dimension=0, tiled...  151 us
    all_gather x1, waiting for transfers between devices, body(): lax.all_gather(w_gate, ('slot', 'seq'), axis=0, tiled=True)  136 us
    all_gather x1, waiting for transfers between devices, body(): lax.all_gather(w_up, ('slot', 'seq'), axis=0, tiled=True)  134 us
  transfers between devices with their start and end apart: 18, of which 17 were waited for; matrix products, arithmetic and copies ran while one was open for 6% of the time, Pallas kernels for 0%

commit v1 on v0

v1 whole, which is shorter than its diff:
```python
import functools
import math

import jax
import jax.numpy as jnp
from jax import lax
from jax.sharding import Mesh
from jax.sharding import PartitionSpec as P

H = 16
HD = 256
GROUP = 96

EPS = 1e-05
ROPE_BASE = 10000.0
BF = jnp.bfloat16
F32 = jnp.float32


def norm_scale(values):
    return lax.rsqrt(jnp.mean(values * values, axis=-1, keepdims=True) + EPS)


def norm_back(values, scale, gain, upstream):
    scaled = gain * upstream
    gain_grad = jnp.sum(upstream * values * scale, axis=0)
    inner = jnp.mean(scaled * values, axis=-1, keepdims=True)
    return (gain_grad, scale * scaled - values * scale * scale * scale * inner)


def rope_tables(position, width):
    half = width // 2
    freq = ROPE_BASE ** (-2.0 * jnp.arange(half, dtype=F32) / width)
    angle = position.astype(F32)[:, None] * freq[None, :]
    return (jnp.cos(angle), jnp.sin(angle))


def rotate(values, cosine, sine):
    half = values.shape[-1] // 2
    first = values[..., :half]
    second = values[..., half:]
    return jnp.concatenate(
        [first * cosine - second * sine, first * sine + second * cosine], axis=-1
    )


def unrotate(grads, cosine, sine):
    half = grads.shape[-1] // 2
    first = grads[..., :half]
    second = grads[..., half:]
    return jnp.concatenate(
        [first * cosine + second * sine, second * cosine - first * sine], axis=-1
    )


def place_info(row_index, order, lengths, tokens):
    device = row_index // tokens
    local = row_index % tokens
    pick = 2 * device + local // GROUP
    table = jnp.arange(order.shape[0], dtype=jnp.int32)
    group_id = jnp.sum(jnp.where(pick[:, None] == table[None, :], order[None, :], 0), axis=1)
    slot_pos = group_id * GROUP + local % GROUP
    ends = jnp.cumsum(lengths)
    passed = slot_pos[:, None] >= ends[None, :]
    segment = jnp.sum(passed.astype(jnp.int32), axis=1)
    start = jnp.sum(jnp.where(passed, lengths[None, :], 0), axis=1)
    return (slot_pos, segment, slot_pos - start, segment < lengths.shape[0])


def block_size(count):
    size = min(512, count)
    while count % size:
        size -= 1
    return size


def dot(left, right):
    return jnp.dot(left, right, preferred_element_type=F32)


def contract_last(left, right):
    return lax.dot_general(left, right, (((1,), (1,)), ((), ())), preferred_element_type=F32)


def contract_first(left, right):
    return lax.dot_general(left, right, (((0,), (0,)), ((), ())), preferred_element_type=F32)


class Net:
    def __init__(self, slots, depth):
        self.S = slots
        self.Z = depth

    def slot(self):
        return lax.axis_index("slot")

    def core(self):
        return lax.axis_index("c")

    def swap_c(self, a):
        return lax.ppermute(a, "c", [(0, 1), (1, 0)])

    def swap_x(self, a):
        return lax.ppermute(a, "slot", [(0, 1), (1, 0), (2, 3), (3, 2)])

    def swap_y(self, a):
        return lax.ppermute(a, "slot", [(0, 2), (2, 0), (1, 3), (3, 1)])

    def relative(self, number):
        return self.slot() ^ number if self.S == 4 else number

    def slots_gather(self, a):
        if self.S != 4:
            return lax.all_gather(a, "slot", axis=0, tiled=True)
        half = a.shape[0] // 2
        ax = self.swap_x(a)
        ay = self.swap_y(a)
        d0 = self.swap_y(ax[:half])
        d1 = self.swap_x(ay[half:])
        return jnp.concatenate([a, ax, ay, d0, d1], axis=0)

    def plane_gather(self, a):
        same = self.slots_gather(a)
        return same, self.swap_c(same)

    def plane_scatter(self, same, other):
        held = same.astype(F32) + self.swap_c(other).astype(F32)
        if self.S != 4:
            return lax.psum_scatter(
                held.astype(BF), "slot", scatter_dimension=0, tiled=True
            ).astype(F32)
        n = same.shape[0] // 4
        half = n // 2
        parts = held.reshape(4, n, -1)
        left = parts[:, :half]
        right = parts[:, half:]
        via_x = self.swap_x(jnp.concatenate([left[1], left[3]], axis=0).astype(BF)).astype(F32)
        via_y = self.swap_y(jnp.concatenate([right[2], right[3]], axis=0).astype(BF)).astype(F32)
        left_own = left[0] + via_x[:half]
        right_own = right[0] + via_y[: n - half]
        left_last = self.swap_y((left[2] + via_x[half:]).astype(BF)).astype(F32)
        right_last = self.swap_x((right[1] + via_y[n - half :]).astype(BF)).astype(F32)
        return jnp.concatenate([left_own + left_last, right_own + right_last], axis=0)

    def gather_all(self, w):
        r, n = w.shape
        same, other = self.plane_gather(lax.all_gather(w, "z", axis=0, tiled=True))
        first = self.core() == 0
        same = same.reshape(self.S, self.Z, 1, r, n)
        other = other.reshape(self.S, self.Z, 1, r, n)
        rows = []
        for number in range(self.S):
            place = self.relative(number)
            mine = lax.dynamic_slice_in_dim(same, place, 1, 0)
            theirs = lax.dynamic_slice_in_dim(other, place, 1, 0)
            rows.append(
                jnp.concatenate(
                    [jnp.where(first, mine, theirs), jnp.where(first, theirs, mine)], axis=2
                )
            )
        return jnp.concatenate(rows, axis=0).reshape(self.S * self.Z * 2 * r, n)

    def scatter_all(self, g):
        n = g.shape[1]
        r = g.shape[0] // (self.S * self.Z * 2)
        parts = g.astype(BF).reshape(self.S, self.Z, 2, r, n)

        def side(core):
            picked = lax.dynamic_slice_in_dim(parts, core, 1, 2)
            return jnp.concatenate(
                [
                    lax.dynamic_slice_in_dim(picked, self.relative(number), 1, 0)
                    for number in range(self.S)
                ],
                axis=0,
            ).reshape(self.S * self.Z * r, n)

        summed = self.plane_scatter(side(self.core()), side(1 - self.core()))
        return lax.psum_scatter(summed.astype(BF), "z", scatter_dimension=0, tiled=True).astype(F32)

    def rows_chunk(self, w):
        whole = lax.all_gather(w, ("z", "c"), axis=0, tiled=True)
        size = whole.shape[0] // 2
        return lax.dynamic_slice_in_dim(whole, self.core() * size, size, 0)

    def rows_scatter(self, g):
        n = g.shape[1]
        r = g.shape[0] // self.Z
        parts = g.astype(BF).reshape(self.Z // 2, 2, r, n)
        mine = lax.dynamic_slice_in_dim(parts, self.core(), 1, 1).reshape(-1, n)
        sent = lax.dynamic_slice_in_dim(parts, 1 - self.core(), 1, 1).reshape(-1, n)
        came = self.swap_c(sent)
        first = self.core() == 0
        joined = jnp.concatenate(
            [jnp.where(first, mine, came), jnp.where(first, came, mine)], axis=0
        )
        return lax.psum_scatter(joined, "z", scatter_dimension=0, tiled=True).astype(F32)

    def cols_chunk(self, w):
        r, n = w.shape
        ways = 2 * self.S
        parts = w.reshape(r, ways, n // ways).transpose(1, 0, 2)
        parts = lax.all_to_all(parts, ("slot", "c"), 0, 0, tiled=True)
        return lax.all_gather(parts.reshape(ways * r, n // ways), "z", axis=0, tiled=True)

    def cols_scatter(self, g):
        ways = 2 * self.S
        m = g.shape[1]
        r = g.shape[0] // (self.Z * ways)
        mine = lax.psum_scatter(g.astype(BF), "z", scatter_dimension=0, tiled=True)
        parts = lax.all_to_all(mine.reshape(ways, r, m), ("slot", "c"), 0, 0, tiled=True)
        return parts.transpose(1, 0, 2).reshape(r, ways * m).astype(F32)

    def by_z(self, a):
        t, n = a.shape
        piece = n // (self.S * self.Z)
        parts = [
            a[:, (s * self.Z + z) * piece : (s * self.Z + z + 1) * piece]
            for z in range(self.Z)
            for s in range(self.S)
        ]
        return jnp.concatenate(parts, axis=1)

    def from_z(self, a):
        t, n = a.shape
        piece = n // (self.S * self.Z)
        parts = [
            a[:, (z * self.S + s) * piece : (z * self.S + s + 1) * piece]
            for s in range(self.S)
            for z in range(self.Z)
        ]
        return jnp.concatenate(parts, axis=1)


def attend(query_rows, key_rows, value_rows, query_seg, query_pos, order, lengths, tokens):
    query_count = query_rows.shape[0]
    empty = (
        jnp.full((query_count,), -1e30, F32),
        jnp.zeros((query_count,), F32),
        jnp.zeros((query_count, HD), F32),
    )
    count = key_rows.shape[0]
    size = block_size(count)

    def one_block(state, number):
        top, total, summed = state
        offset = number * size
        key_block = lax.dynamic_slice_in_dim(key_rows, offset, size, 0)
        value_block = lax.dynamic_slice_in_dim(value_rows, offset, size, 0)
        key_index = offset + jnp.arange(size, dtype=jnp.int32)
        key_pos, key_seg, _, _ = place_info(key_index, order, lengths, tokens)
        allowed = (query_seg[:, None] == key_seg[None, :]) & (
            key_pos[None, :] <= query_pos[:, None]
        )
        scores = jnp.where(allowed, contract_last(query_rows, key_block), -1e30)
        new_top = jnp.maximum(top, jnp.max(scores, axis=1))
        fade = jnp.exp(top - new_top)
        weights = jnp.where(allowed, jnp.exp(scores - new_top[:, None]), 0.0)
        total = total * fade + jnp.sum(weights, axis=1)
        summed = summed * fade[:, None] + dot(weights.astype(BF), value_block)
        return ((new_top, total, summed), None)

    state, _ = lax.scan(one_block, empty, jnp.arange(count // size))
    top, total, summed = state
    return summed / total[:, None], top + jnp.log(total)


def attend_back(
    query_rows, keys_all, values_all, att_grad, attended, log_total,
    query_seg, query_pos, order, lengths, tokens,
):
    delta = jnp.sum(att_grad.astype(F32) * attended, axis=1)
    slot_rows = keys_all.shape[0]
    size = block_size(slot_rows)

    def back_block(query_grad, number):
        offset = number * size
        key_block = lax.dynamic_slice_in_dim(keys_all, offset, size, 0)
        value_block = lax.dynamic_slice_in_dim(values_all, offset, size, 0)
        key_index = offset + jnp.arange(size, dtype=jnp.int32)
        key_pos, key_seg, _, _ = place_info(key_index, order, lengths, tokens)
        allowed = (query_seg[:, None] == key_seg[None, :]) & (
            key_pos[None, :] <= query_pos[:, None]
        )
        prob = jnp.where(
            allowed, jnp.exp(contract_last(query_rows, key_block) - log_total[:, None]), 0.0
        )
        prob_grad = contract_last(att_grad, value_block)
        score_grad = (prob * (prob_grad - delta[:, None])).astype(BF)
        value_grad = contract_first(prob.astype(BF), att_grad)
        key_grad = contract_first(score_grad, query_rows)
        query_grad = query_grad + dot(score_grad, key_block)
        return (query_grad, (key_grad, value_grad))

    query_grad, (key_grads, value_grads) = lax.scan(
        back_block, jnp.zeros(query_rows.shape, F32), jnp.arange(slot_rows // size)
    )
    return query_grad, key_grads.reshape(slot_rows, HD), value_grads.reshape(slot_rows, HD)


def column(a, rows):
    return jnp.pad(a.reshape(-1, 1), ((0, rows - a.shape[0]), (0, 0)))


def body(
    net,
    hidden_in, seq_lens, group_order, attn_gain, wq_down, q_gain, wq_up, w_key, w_value, w_out,
    ffn_gain, w_gate, w_up, w_down, out_grad,
):
    lengths = seq_lens[0]
    order = group_order[0]
    tokens = hidden_in.shape[0]
    width = hidden_in.shape[1]
    low_rank = wq_up.shape[0] * net.S * net.Z * 2
    query_count = tokens * H
    scale = 1.0 / math.sqrt(HD)
    place = lax.axis_index("z") * 2 + lax.axis_index("c")
    rows_here = place * tokens + jnp.arange(tokens, dtype=jnp.int32)
    slot_pos, segment, seq_pos, valid = place_info(rows_here, order, lengths, tokens)
    cosine, sine = rope_tables(seq_pos, HD)
    query_seg = jnp.repeat(segment, H)
    query_pos = jnp.repeat(slot_pos, H)

    rows = wq_down.shape[0]
    gains = jnp.concatenate(
        [column(attn_gain, rows), column(ffn_gain, rows), column(q_gain, rows)], axis=1
    )
    gains = jnp.pad(gains, ((0, 0), (0, 128 - 3)))
    first_set = net.gather_all(jnp.concatenate([wq_down, w_key, w_value, gains], axis=1))
    down_q = first_set[:, :low_rank]
    key_proj = first_set[:, low_rank : low_rank + HD]
    value_proj = first_set[:, low_rank + HD : low_rank + 2 * HD]
    gains = first_set[:, low_rank + 2 * HD :].astype(F32)
    gain_one = gains[:, 0]
    gain_two = gains[:, 1]
    gain_q = gains[:, 2].reshape(-1, rows)[:, : q_gain.shape[0]].reshape(-1)
    up_q = net.gather_all(wq_up)
    out_chunk = net.rows_chunk(w_out)
    gate_chunk = net.cols_chunk(w_gate)
    up_chunk = net.cols_chunk(w_up)
    down_chunk = net.rows_chunk(w_down)

    out_cot = out_grad.astype(F32) * valid[:, None].astype(F32)
    cot_sides = net.plane_gather(out_cot.astype(BF))

    inputs = hidden_in.astype(F32)
    scale_one = norm_scale(inputs)
    normed_one = (inputs * scale_one * gain_one).astype(BF)
    query_low = dot(normed_one, down_q)
    scale_q = norm_scale(query_low)
    query_normed = (query_low * scale_q * gain_q).astype(BF)
    query_full = dot(query_normed, up_q).reshape(tokens, H, HD)
    query_rows = (
        (rotate(query_full, cosine[:, None, :], sine[:, None, :]) * scale)
        .astype(BF)
        .reshape(query_count, HD)
    )
    keys_rot = rotate(dot(normed_one, key_proj), cosine, sine).astype(BF)
    values_here = dot(normed_one, value_proj).astype(BF)
    both = lax.all_gather(
        jnp.concatenate([keys_rot, values_here], axis=1), ("z", "c"), axis=0, tiled=True
    )
    key_rows = both[:, :HD]
    value_rows = both[:, HD:]
    attended, log_total = attend(
        query_rows, key_rows, value_rows, query_seg, query_pos, order, lengths, tokens
    )
    ways = 2 * net.S
    att_low = attended.reshape(tokens, ways, H * HD // ways).astype(BF)

    def to_heads(a):
        got = lax.all_to_all(a.transpose(1, 0, 2), ("slot", "c"), 0, 0, tiled=True)
        got = got.reshape(net.S, 2, tokens, -1)

        def side(core):
            picked = lax.dynamic_slice_in_dim(got, core, 1, 1)
            return jnp.concatenate(
                [
                    lax.dynamic_slice_in_dim(picked, net.relative(number), 1, 0)
                    for number in range(net.S)
                ],
                axis=0,
            ).reshape(net.S * tokens, -1)

        return side(net.core()), side(1 - net.core())

    def to_rows(same, other):
        same = same.reshape(net.S, 1, tokens, -1)
        other = other.reshape(net.S, 1, tokens, -1)
        first = net.core() == 0
        pair = jnp.concatenate(
            [jnp.where(first, same, other), jnp.where(first, other, same)], axis=1
        )
        pair = jnp.concatenate(
            [
                lax.dynamic_slice_in_dim(pair, net.relative(number), 1, 0)
                for number in range(net.S)
            ],
            axis=0,
        ).reshape(ways, tokens, -1)
        return lax.all_to_all(pair, ("slot", "c"), 0, 0, tiled=True)

    att_sides = to_heads(att_low)
    mid_part = net.plane_scatter(*[dot(a, out_chunk).astype(BF) for a in att_sides])
    middle = inputs + mid_part

    scale_two = norm_scale(middle)
    normed_two = (middle * scale_two * gain_two).astype(BF)
    normed_sides = net.plane_gather(net.by_z(normed_two))
    gate = [dot(a, gate_chunk) for a in normed_sides]
    upward = [dot(a, up_chunk) for a in normed_sides]
    sigma = [jax.nn.sigmoid(g) for g in gate]
    hidden = [(g * s * u).astype(BF) for g, s, u in zip(gate, sigma, upward)]

    hidden_grad = [contract_last(a, down_chunk) for a in cot_sides]
    gate_grad = [
        (d * u * s * (1.0 + g * (1.0 - s))).astype(BF)
        for d, u, s, g in zip(hidden_grad, upward, sigma, gate)
    ]
    upward_grad = [
        (d * g * s).astype(BF) for d, g, s in zip(hidden_grad, gate, sigma)
    ]
    normed_two_grad = net.from_z(
        net.plane_scatter(
            *[
                (contract_last(a, gate_chunk) + contract_last(b, up_chunk)).astype(BF)
                for a, b in zip(gate_grad, upward_grad)
            ]
        )
    )
    result = middle + net.plane_scatter(*[dot(a, down_chunk).astype(BF) for a in hidden])
    layer_out = result.astype(BF)
    grad_down = sum(contract_first(a, b) for a, b in zip(hidden, cot_sides))
    grad_gate = sum(contract_first(a, b) for a, b in zip(normed_sides, gate_grad))
    grad_upward = sum(contract_first(a, b) for a, b in zip(normed_sides, upward_grad))
    grad_down = net.rows_scatter(grad_down)
    grad_gate = net.cols_scatter(grad_gate)
    grad_upward = net.cols_scatter(grad_upward)
    grad_gain_two, middle_back = norm_back(middle, scale_two, gain_two, normed_two_grad)
    middle_grad = out_cot + middle_back

    middle_sides = net.plane_gather(middle_grad.astype(BF))
    grad_out = sum(contract_first(a, b) for a, b in zip(att_sides, middle_sides))
    grad_out = net.rows_scatter(grad_out)
    att_grad = to_rows(*[contract_last(a, out_chunk).astype(BF) for a in middle_sides])
    att_grad = att_grad.transpose(1, 0, 2).reshape(query_count, HD)
    query_grad, key_grads, value_grads = attend_back(
        query_rows, key_rows, value_rows, att_grad, attended, log_total,
        query_seg, query_pos, order, lengths, tokens,
    )
    both_sum = lax.psum_scatter(
        jnp.concatenate([key_grads, value_grads], axis=1).astype(BF),
        ("z", "c"), scatter_dimension=0, tiled=True,
    ).astype(F32)
    key_pre = unrotate(both_sum[:, :HD], cosine, sine).astype(BF)
    value_pre = both_sum[:, HD:].astype(BF)
    query_pre = (
        unrotate(
            query_grad.reshape(tokens, H, HD) * scale, cosine[:, None, :], sine[:, None, :]
        )
        .reshape(tokens, H * HD)
        .astype(BF)
    )
    grad_up_q = net.scatter_all(contract_first(query_normed, query_pre))
    normed_q_grad = contract_last(query_pre, up_q)
    grad_gain_q, low_part = norm_back(query_low, scale_q, gain_q, normed_q_grad)
    query_low_grad = low_part.astype(BF)
    first_grad = jnp.concatenate([query_low_grad, key_pre, value_pre], axis=1)
    normed_one_grad = contract_last(first_grad, first_set[:, : low_rank + 2 * HD])
    grad_gain_one, input_part = norm_back(inputs, scale_one, gain_one, normed_one_grad)
    in_grad = (middle_grad + input_part).astype(BF)
    q_column = jnp.pad(
        grad_gain_q.reshape(-1, q_gain.shape[0]), ((0, 0), (0, rows - q_gain.shape[0]))
    ).reshape(-1)
    gain_grads = jnp.stack([grad_gain_one, grad_gain_two, q_column], axis=1)
    first_out = net.scatter_all(
        jnp.concatenate(
            [
                contract_first(normed_one, first_grad),
                jnp.pad(gain_grads, ((0, 0), (0, 128 - 3))),
            ],
            axis=1,
        )
    )
    last = low_rank + 2 * HD
    return (
        layer_out,
        in_grad,
        first_out[:, last],
        first_out[:, :low_rank],
        first_out[: q_gain.shape[0], last + 2],
        grad_up_q,
        first_out[:, low_rank : low_rank + HD],
        first_out[:, low_rank + HD : last],
        grad_out,
        first_out[:, last + 1],
        grad_gate,
        grad_upward,
        grad_down,
    )


def solution(mesh):
    slots, seq = mesh.devices.shape
    fine = Mesh(mesh.devices.reshape(slots, seq // 2, 2), ("slot", "z", "c"))
    every = ("slot", "z", "c")
    matrix = P(every, None)
    vector = P(every)
    net = Net(slots, seq // 2)
    return jax.shard_map(
        functools.partial(body, net),
        mesh=fine,
        in_specs=(
            matrix, P("slot", None), P("slot", None), vector, matrix, vector, matrix, matrix,
            matrix, matrix, vector, matrix, matrix, matrix, matrix,
        ),
        out_specs=(
            matrix, matrix, vector, matrix, vector, matrix, matrix, matrix, matrix, vector,
            matrix, matrix, matrix,
        ),
        check_vma=False,
    )
```

time: 3470 us -> 991 us (0.29)
  waiting for transfers between devices: 2970 us -> 416 us
  local copies, waits for them, and re-layouts: 27.7 us -> 111 us
  other arithmetic: 32.6 us -> 114 us
  matrix products: 292 us -> 215 us
  blocking collectives: 114 us -> 37.8 us
  starting transfers between devices: 1.47 us -> 65.4 us
    reduce_scatter x10 -> x7, waiting for transfers between devices: 2340 us -> 74.1 us  [the longest x2 49.8 us: scatter_all(): lax.psum_scatter(summed.astype(BF), 'z', scatter_dimension=0, tiled=True)]
    all_gather x8 -> x6, waiting for transfers between devices: 623 us -> 29.7 us  [the longest x2 29.7 us: rows_chunk(): whole = lax.all_gather(w, ('z', 'c'), axis=0, tiled=True)]
    ppermute x0 -> x52, waiting for transfers between devices: none -> 255 us  [the longest x20 175 us: swap_x(): return lax.ppermute(a, 'slot', [(0, 1), (1, 0), (2, 3), (3, 2)])]
    unnamed x2 -> x0, blocking collectives: 80.4 us -> none
    all_to_all x0 -> x5, waiting for transfers between devices: none -> 56.1 us  [the longest x1 20.9 us: to_rows(): return lax.all_to_all(pair, ('slot', 'c'), 0, 0, tiled=True)]
    dot_general x14 -> x16, matrix products: 108 us -> 57.6 us  [contract_first(): lax.dot_general(left, right, (((0,), (0,)), ((), ())), preferred_element_...]
    ppermute x0 -> x52, starting transfers between devices: none -> 43.5 us  [the longest x20 22.3 us: swap_x(): return lax.ppermute(a, 'slot', [(0, 1), (1, 0), (2, 3), (3, 2)])]
    concatenate x2 -> x31, other arithmetic: 0.19 us -> 35.8 us  [the longest x4 12.1 us: side(): jnp.concatenate([lax.dynamic_slice_in_dim(picked, self.relative(number),...]
  transfers between devices with their start and end apart: 18 -> 70, of which waited for: 17 -> 42; matrix products, arithmetic and copies ran while one was open for 6% -> 34% of each run, Pallas kernels for 0% -> 0%
where the time goes in v1:
time: 991 us; the launch traced here: 981 us
  waiting for transfers between devices  416 us (42%)
  matrix products  215 us (22%)
  other arithmetic  114 us (12%)
  local copies, waits for them, and re-layouts  111 us (11%)
  starting transfers between devices  65.4 us (7%)
  blocking collectives  37.8 us (4%)
  between operations  17.7 us (2%)
    ppermute x20, waiting for transfers between devices, swap_x(): return lax.ppermute(a, 'slot', [(0, 1), (1, 0), (2, 3), (3, 2)])  175 us
    dot_general x19, matrix products, contract_last(): lax.dot_general(left, right, (((1,), (1,)), ((), ())), preferred_element_...  79 us
    dot_general x18, matrix products, dot(): return jnp.dot(left, right, preferred_element_type=F32)  78 us
    ppermute x20, waiting for transfers between devices, swap_y(): return lax.ppermute(a, 'slot', [(0, 2), (2, 0), (1, 3), (3, 1)])  73.4 us
    dot_general x16, matrix products, contract_first(): lax.dot_general(left, right, (((0,), (0,)), ((), ())), preferred_element_...  57.6 us
    reduce_scatter x2, waiting for transfers between devices, scatter_all(): lax.psum_scatter(summed.astype(BF), 'z', scatter_dimension=0, tiled=True)  49.8 us
    unnamed x177, local copies, waits for them, and re-layouts  33.8 us
    all_gather x2, waiting for transfers between devices, rows_chunk(): whole = lax.all_gather(w, ('z', 'c'), axis=0, tiled=True)  29.7 us
  transfers between devices with their start and end apart: 70, of which 42 were waited for; matrix products, arithmetic and copies ran while one was open for 34% of the time, Pallas kernels for 0%

profile of v1, /device:TPU:0, one launch (start us, length us, event | category | flops | bytes accessed | tf_op | source)
XLA Modules:
  0.0 981.5 jit_solution(16484290695705637433)
XLA Ops:
  9.8 22.1 %all_gather.21 = bf16[256,1664]{1,0:T(8,128)(2,1)S(1)} all-gather(bf16[64,1664]{1,0:T(8,128)(2,1)S(1)} %fusion.132), channel_id=1, replica_groups=mesh['slot'=4,'z'=4,'c'=2] {'z'}, dimensions={0}, use_global_device_ids=true | all-gather | bytes 1064960 | tf_op jit(solution)/shard_map/all_gather | solution.py:147
  36.8 13.0 %collective-permute-done = bf16[256,1664]{1,0:T(8,128)(2,1)S(1)} collective-permute-done((bf16[256,1664]{1,0:T(8,128)(2,1)S(1)}, bf16[256,1664]{1,0:T(8,128)(2,1)S(1)}, u32[]{:S(2)}, u32[]{:S(2)}) %collective-permute-start) | collective-permute-done | bytes 852000 | tf_op jit(solution)/shard_map/ppermute | solution.py:104
  66.9 21.5 %collective-permute-done.5 = bf16[128,4096]{1,0:T(8,128)(2,1)S(1)} collective-permute-done((bf16[128,4096]{1,0:T(8,128)(2,1)}, bf16[128,4096]{1,0:T(8,128)(2,1)S(1)}, u32[]{:S(2)}, u32[]{:S(2)}) %collective-permute-start.5) | collective-permute-done | bytes 1048608 | tf_op jit(solution)/shard_map/ppermute | solution.py:104
  92.6 9.5 collective-permute-done.7
  133.6 12.0 %copy.100 = bf16[4096,1024]{1,0:T(8,128)(2,1)} copy(bf16[4096,1024]{0,1:T(8,128)(2,1)} %bitcast.341) | data formatting | bytes 16777216 | tf_op jit(solution)/shard_map/dot_general | solution.py:78
  159.2 48.1 %while.36 = (s32[]{:T(128)}, f32[3072]{0:T(1024)S(1)}, f32[3072]{0:T(1024)S(1)}, f32[3072,256]{1,0:T(8,128)S(1)}, s32[3]{0:T(128)S(1)}, /*index=5*/s32[1,16]{1,0...) while((s32[]{:T(128)}, f32[3072]{0:T(1024)S(1)}, ...), condition=%wide.region_12.13_spmd.clone, body=%wide.region_7.12_spmd.clone.sunk | while | flops 1642927104 | bytes 52801380 | solution.py:263
  220.8 20.4 %all-to-all-done = bf16[8,192,512]{2,1,0:T(8,128)(2,1)S(1)} async-done(((bf16[8,192,512]{2,1,0:T(8,128)(2,1)}), bf16[8,192,512]{2,1,0:T(8,128)(2,1)S(1)}, u32[]{:S(2)}, u32[]{:S(2)}) %all-to-all-start) | async-done | bytes 1572896 | tf_op jit(solution)/shard_map/all_to_all | solution.py:372
  247.6 15.7 %all_to_all.30 = bf16[8,64,704]{2,1,0:T(8,128)(2,1)} all-to-all(bf16[8,64,704]{2,1,0:T(8,128)(2,1)S(1)} %bitcast.374), channel_id=1, replica_groups=mesh['slot'=4,'z'=4,'c'=2] {'slot','c'}, dimensions={0} | all-to-all | bytes 1441792 | tf_op jit(solution)/shard_map/all_to_all | solution.py:203
  270.6 17.3 %collective-permute-done.11 = bf16[192,2048]{1,0:T(8,128)(2,1)S(1)} collective-permute-done((bf16[192,2048]{1,0:T(8,128)(2,1)S(1)}, bf16[192,2048]{1,0:T(8,128)(2,1)S(1)}, u32[]{:S(2)}, u32[]{:S(2)}) %collective-permute-start.11) | collective-permute-done | bytes 786464 | tf_op jit(solution)/shard_map/ppermute | solution.py:104
  289.3 8.4 collective-permute-done.12
  326.5 15.8 %collective-permute-done.15 = bf16[192,2048]{1,0:T(8,128)(2,1)S(1)} collective-permute-done((bf16[192,2048]{1,0:T(8,128)(2,1)S(1)}, bf16[192,2048]{1,0:T(8,128)(2,1)S(1)}, u32[]{:S(2)}, u32[]{:S(2)}) %collective-permute-start.15) | collective-permute-done | bytes 786464 | tf_op jit(solution)/shard_map/ppermute | solution.py:104
  381.2 29.6 %all-gather.17.cloned.1.call-done = bf16[1408,2048]{1,0:T(8,128)(2,1)} async-done(((bf16[176,2048]{1,0:T(8,128)(2,1)}), bf16[1408,2048]{1,0:T(8,128)(2,1)}) %all-gather.17.cloned.1.call-update) | async-done | bytes 5767184 | tf_op jit(solution)/shard_map/all_gather | solution.py:182
  468.9 15.7 %collective-permute-done.31 = bf16[192,2048]{1,0:T(8,128)(2,1)S(1)} collective-permute-done((bf16[192,2048]{1,0:T(8,128)(2,1)S(1)}, bf16[192,2048]{1,0:T(8,128)(2,1)S(1)}, u32[]{:S(2)}, u32[]{:S(2)}) %collective-permute-start.31) | collective-permute-done | bytes 786464 | tf_op jit(solution)/shard_map/ppermute | solution.py:104
  486.4 14.4 %collective-permute-done.21 = bf16[192,2048]{1,0:T(8,128)(2,1)S(1)} collective-permute-done((bf16[192,2048]{1,0:T(8,128)(2,1)S(1)}, bf16[192,2048]{1,0:T(8,128)(2,1)S(1)}, u32[]{:S(2)}, u32[]{:S(2)}) %collective-permute-start.21) | collective-permute-done | bytes 786464 | tf_op jit(solution)/shard_map/ppermute | solution.py:104
  535.9 14.3 %collective-permute-done.35 = bf16[192,2048]{1,0:T(8,128)(2,1)S(1)} collective-permute-done((bf16[192,2048]{1,0:T(8,128)(2,1)S(1)}, bf16[192,2048]{1,0:T(8,128)(2,1)S(1)}, u32[]{:S(2)}, u32[]{:S(2)}) %collective-permute-start.35) | collective-permute-done | bytes 786464 | tf_op jit(solution)/shard_map/ppermute | solution.py:104
  573.7 20.9 %all-to-all-done.3 = bf16[8,192,512]{2,1,0:T(8,128)(2,1)S(1)} async-done(((bf16[8,192,512]{2,1,0:T(8,128)(2,1)}), bf16[8,192,512]{2,1,0:T(8,128)(2,1)S(1)}, u32[]{:S(2)}, u32[]{:S(2)}) %all-to-all-start.3) | async-done | bytes 1572896 | tf_op jit(solution)/shard_map/all_to_all | solution.py:401
  599.6 63.1 %while.37 = (s32[]{:T(128)}, f32[3072,256]{1,0:T(8,128)}, bf16[3,512,256]{2,1,0:T(8,128)(2,1)}, bf16[3,512,256]{2,1,0:T(8,128)(2,1)}, s32[3]{0:T(128)S(1)}, /*in...) while((s32[]{:T(128)}, f32[3072,256]{1,0:T(8,128)}, ...), condition=%wide.region_19.20_spmd.clone, body=%wide.region_16.19_spmd.clone.sunk | while | flops 4042315776 | bytes 112079440 | solution.py:295
  758.1 19.1 %collective-permute-done.46 = bf16[128,4096]{1,0:T(8,128)(2,1)S(1)} collective-permute-done((bf16[128,4096]{1,0:T(8,128)(2,1)S(1)}, bf16[128,4096]{1,0:T(8,128)(2,1)S(1)}, u32[]{:S(2)}, u32[]{:S(2)}) %collective-permute-start.46) | collective-permute-done | bytes 1048608 | tf_op jit(solution)/shard_map/ppermute | solution.py:104
  785.3 9.1 collective-permute-done.47
  801.7 9.6 collective-permute-done.49
  813.1 14.7 %collective-permute-done.41 = bf16[256,1664]{1,0:T(8,128)(2,1)S(1)} collective-permute-done((bf16[256,1664]{1,0:T(8,128)(2,1)S(1)}, bf16[256,1664]{1,0:T(8,128)(2,1)S(1)}, u32[]{:S(2)}, u32[]{:S(2)}) %collective-permute-start.41) | collective-permute-done | bytes 852000 | tf_op jit(solution)/shard_map/ppermute | solution.py:104
  890.4 24.3 %reduce-scatter.14.cloned.1.call-done = bf16[128,2048]{1,0:T(8,128)(2,1)} async-done(((bf16[512,2048]{1,0:T(8,128)(2,1)}), bf16[128,2048]{1,0:T(8,128)(2,1)}) %reduce-scatter.14.cloned.1.call-update) | async-done | bytes 524304 | tf_op jit(solution)/shard_map/reduce_scatter | solution.py:197
  916.9 26.6 %reduce-scatter.12.cloned.1.call-done = bf16[32,4096]{1,0:T(8,128)(2,1)} async-done(((bf16[128,4096]{1,0:T(8,128)(2,1)}), bf16[32,4096]{1,0:T(8,128)(2,1)}) %reduce-scatter.12.cloned.1.call-update) | async-done | bytes 262160 | tf_op jit(solution)/shard_map/reduce_scatter | solution.py:179
  945.2 23.2 %reduce-scatter.10.cloned.1.call-done = bf16[64,1664]{1,0:T(8,128)(2,1)} async-done(((bf16[256,1664]{1,0:T(8,128)(2,1)}), bf16[64,1664]{1,0:T(8,128)(2,1)}) %reduce-scatter.10.cloned.1.call-update) | async-done | bytes 213008 | tf_op jit(solution)/shard_map/reduce_scatter | solution.py:179
  (678 shorter events, 582.1 us)
Async XLA Ops:
  8.0 54.6 %all-gather.9.cloned.1.call-start = ((), (), s32[]{:S(2)}) async-start(), calls=%async_computation.14 | async-start | bytes 1310720 | tf_op jit(solution)/shard_map/all_gather | solution.py:147
  35.0 121.6 %all-gather.7.cloned.1.call-start = ((), (), s32[]{:S(2)}) async-start(), calls=%async_computation.13 | async-start | bytes 1769472 | tf_op jit(solution)/shard_map/all_gather | solution.py:360
  62.3 42.0 %collective-permute-start.4 = (bf16[1024,1664]{1,0:T(8,128)(2,1)}, bf16[1024,1664]{1,0:T(8,128)(2,1)}, u32[]{:S(2)}, u32[]{:S(2)}) collective-permute-start(bf16[1024,1664]{1,0:T(8,128)(2,1)} %constant_dynamic-update-slice_fusion), channel_id=1, source_target_pairs={{0,1},{1,0},{2,3},{3,2},{4,5},{5,4},{6,7},{7,6},{8,9},{9,8},{10,11... | collective-permute-start | bytes 10223624 | tf_op jit(solution)/shard_map/ppermute | solution.py:101
  114.8 101.3 %all-to-all-start.1 = ((bf16[8,64,704]{2,1,0:T(8,128)(2,1)}), bf16[8,64,704]{2,1,0:T(8,128)(2,1)}, u32[]{:S(2)}, u32[]{:S(2)}) async-start(bf16[8,64,704]{2,1,0:T(8,128)(2,1)} %bitcast.280), calls=%async_computation.1 | async-start | bytes 1572864 | tf_op jit(solution)/shard_map/all_to_all | solution.py:203
  119.0 122.4 %all-gather.11.cloned.1.call-start = ((), (), s32[]{:S(2)}) async-start(), calls=%async_computation.15 | async-start | bytes 4718592 | tf_op jit(solution)/shard_map/all_gather | solution.py:182
  220.1 147.6 %all-gather.13.cloned.1.call-start = ((), (), s32[]{:S(2)}) async-start(), calls=%async_computation.16 | async-start | bytes 3932160 | tf_op jit(solution)/shard_map/all_gather | solution.py:204
  220.7 153.8 %all-gather.15.cloned.1.call-start = ((), (), s32[]{:S(2)}) async-start(), calls=%async_computation.17 | async-start | bytes 3932160 | tf_op jit(solution)/shard_map/all_gather | solution.py:204
  263.3 147.6 %all-gather.17.cloned.1.call-start = ((), (), s32[]{:S(2)}) async-start(), calls=%async_computation.18 | async-start | bytes 6488064 | tf_op jit(solution)/shard_map/all_gather | solution.py:182
  302.3 50.1 %collective-permute-start.25 = (bf16[192,2048]{1,0:T(8,128)(2,1)}, bf16[192,2048]{1,0:T(8,128)(2,1)}, u32[]{:S(2)}, u32[]{:S(2)}) collective-permute-start(bf16[192,2048]{1,0:T(8,128)(2,1)} %get-tuple-element.639), channel_id=1, source_target_pairs={{0,8},{8,0},{16,24},{24,16},{1,9},{9,1},{17,25},{25,17},{2,10},{10... | collective-permute-start | bytes 2359304 | tf_op jit(solution)/shard_map/ppermute | solution.py:104
  302.4 52.3 %collective-permute-start.26 = (bf16[192,2048]{1,0:T(8,128)(2,1)}, bf16[192,2048]{1,0:T(8,128)(2,1)}, u32[]{:S(2)}, u32[]{:S(2)}) collective-permute-start(bf16[192,2048]{1,0:T(8,128)(2,1)} %get-tuple-element.639), channel_id=1, source_target_pairs={{0,16},{16,0},{8,24},{24,8},{1,17},{17,1},{9,25},{25,9},{2,18},{18... | collective-permute-start | bytes 2359304 | tf_op jit(solution)/shard_map/ppermute | solution.py:107
  314.3 27.9 %collective-permute-start.15 = (bf16[192,2048]{1,0:T(8,128)(2,1)S(1)}, bf16[192,2048]{1,0:T(8,128)(2,1)S(1)}, u32[]{:S(2)}, u32[]{:S(2)}) collective-permute-start(bf16[192,2048]{1,0:T(8,128)(2,1)S(1)} %get-tuple-element.743), channel_id=1, source_target_pairs={{0,8},{8,0},{16,24},{24,16},{1,9},{9,1},{17,25},{25,17},{2,10},{10... | collective-permute-start | bytes 2359304 | tf_op jit(solution)/shard_map/ppermute | solution.py:104
  422.2 33.1 %collective-permute-start.20 = (bf16[768,2048]{1,0:T(8,128)(2,1)S(1)}, bf16[768,2048]{1,0:T(8,128)(2,1)S(1)}, u32[]{:S(2)}, u32[]{:S(2)}) collective-permute-start(bf16[768,2048]{1,0:T(8,128)(2,1)S(1)} %convolution_convert_fusion.4), channel_id=1, source_target_pairs={{0,1},{1,0},{2,3},{3,2},{4,5},{5,4},{6,7},{7,6},{8,9},{9,8},{10,11... | collective-permute-start | bytes 9437192 | tf_op jit(solution)/shard_map/ppermute | solution.py:101
  466.0 34.8 %collective-permute-start.21 = (bf16[192,2048]{1,0:T(8,128)(2,1)S(1)}, bf16[192,2048]{1,0:T(8,128)(2,1)S(1)}, u32[]{:S(2)}, u32[]{:S(2)}) collective-permute-start(bf16[192,2048]{1,0:T(8,128)(2,1)S(1)} %pad_maximum_fusion.18), channel_id=1, source_target_pairs={{0,8},{8,0},{16,24},{24,16},{1,9},{9,1},{17,25},{25,17},{2,10},{10... | collective-permute-start | bytes 2359304 | tf_op jit(solution)/shard_map/ppermute | solution.py:104
  466.7 35.9 %collective-permute-start.23 = (bf16[192,2048]{1,0:T(8,128)(2,1)S(1)}, bf16[192,2048]{1,0:T(8,128)(2,1)S(1)}, u32[]{:S(2)}, u32[]{:S(2)}) collective-permute-start(bf16[192,2048]{1,0:T(8,128)(2,1)S(1)} %pad_maximum_fusion.19), channel_id=1, source_target_pairs={{0,16},{16,0},{8,24},{24,8},{1,17},{17,1},{9,25},{25,9},{2,18},{18... | collective-permute-start | bytes 2359304 | tf_op jit(solution)/shard_map/ppermute | solution.py:107
  468.3 35.8 %collective-permute-start.33 = (bf16[192,2048]{1,0:T(8,128)(2,1)S(1)}, bf16[192,2048]{1,0:T(8,128)(2,1)S(1)}, u32[]{:S(2)}, u32[]{:S(2)}) collective-permute-start(bf16[192,2048]{1,0:T(8,128)(2,1)S(1)} %pad_maximum_fusion.21), channel_id=1, source_target_pairs={{0,16},{16,0},{8,24},{24,8},{1,17},{17,1},{9,25},{25,9},{2,18},{18... | collective-permute-start | bytes 2359304 | tf_op jit(solution)/shard_map/ppermute | solution.py:107
  573.6 158.2 %reduce-scatter.8.cloned.1.call-start = ((), (), s32[]{:S(2)}) async-start(), calls=%async_computation.19 | async-start | bytes 1769472 | tf_op jit(solution)/shard_map/reduce_scatter | solution.py:451
  665.5 178.7 %reduce-scatter.18.cloned.1.call-start = ((), (), s32[]{:S(2)}) async-start(), calls=%async_computation.24 | async-start | bytes 3604480 | tf_op jit(solution)/shard_map/reduce_scatter | solution.py:210
  676.0 174.8 %reduce-scatter.16.cloned.1.call-start = ((), (), s32[]{:S(2)}) async-start(), calls=%async_computation.23 | async-start | bytes 3604480 | tf_op jit(solution)/shard_map/reduce_scatter | solution.py:210
  686.7 199.7 %reduce-scatter.20.cloned.1.call-start = ((), (), s32[]{:S(2)}) async-start(), calls=%async_computation.25 | async-start | bytes 3604480 | tf_op jit(solution)/shard_map/reduce_scatter | solution.py:197
  701.2 213.5 %reduce-scatter.14.cloned.1.call-start = ((), (), s32[]{:S(2)}) async-start(), calls=%async_computation.22 | async-start | bytes 2621440 | tf_op jit(solution)/shard_map/reduce_scatter | solution.py:197
  724.0 30.3 %collective-permute-start.50 = (bf16[256,2048]{1,0:T(8,128)(2,1)}, bf16[256,2048]{1,0:T(8,128)(2,1)}, u32[]{:S(2)}, u32[]{:S(2)}) collective-permute-start(bf16[256,2048]{1,0:T(8,128)(2,1)} %bitcast.89), channel_id=1, source_target_pairs={{0,1},{1,0},{2,3},{3,2},{4,5},{5,4},{6,7},{7,6},{8,9},{9,8},{10,11... | collective-permute-start | bytes 3145736 | tf_op jit(solution)/shard_map/ppermute | solution.py:101
  754.3 43.1 %collective-permute-start.40 = (bf16[1024,1664]{1,0:T(8,128)(2,1)}, bf16[1024,1664]{1,0:T(8,128)(2,1)}, u32[]{:S(2)}, u32[]{:S(2)}) collective-permute-start(bf16[1024,1664]{1,0:T(8,128)(2,1)} %bitcast.65), channel_id=1, source_target_pairs={{0,1},{1,0},{2,3},{3,2},{4,5},{5,4},{6,7},{7,6},{8,9},{9,8},{10,11... | collective-permute-start | bytes 10223624 | tf_op jit(solution)/shard_map/ppermute | solution.py:101
  779.4 164.0 %reduce-scatter.12.cloned.1.call-start = ((), (), s32[]{:S(2)}) async-start(), calls=%async_computation.21 | async-start | bytes 1310720 | tf_op jit(solution)/shard_map/reduce_scatter | solution.py:179
  867.5 100.9 %reduce-scatter.10.cloned.1.call-start = ((), (), s32[]{:S(2)}) async-start(), calls=%async_computation.20 | async-start | bytes 1064960 | tf_op jit(solution)/shard_map/reduce_scatter | solution.py:179
  (137 other events, 1537.4 us)
Sparse Core Ops, SparseCore 0:
  35.1 25.1 all-gather.8
Sparse Core Ops, SparseCore 1:
  113.2 25.0 all-gather.6
  139.7 46.1 all-gather.10
  222.2 64.4 all-gather.12
  288.2 62.0 all-gather.14
  351.9 58.9 all-gather.16
  665.5 30.7 reduce-scatter.7
  698.5 54.4 reduce-scatter.17
  755.1 55.9 reduce-scatter.15
  813.2 55.9 reduce-scatter.19
  871.5 43.2 reduce-scatter.13
  917.0 26.4 reduce-scatter.11
  945.8 22.6 reduce-scatter.9

commit v2 on v0

v2 whole, which is shorter than its diff:
```python
import functools
import math

import jax
import jax.numpy as jnp
from jax import lax
from jax.experimental import pallas as pl
from jax.experimental.pallas import tpu as pltpu
from jax.sharding import Mesh
from jax.sharding import PartitionSpec as P

H = 16
HD = 256
GROUP = 96
TILE = 256
HG = 8
VMEM_BYTES = 60 << 20

EPS = 1e-05
ROPE_BASE = 10000.0
BF = jnp.bfloat16
F32 = jnp.float32


class Net:
    def __init__(self, slots, depth):
        self.S = slots
        self.Z = depth

    def me(self):
        return jnp.stack([lax.axis_index("slot"), lax.axis_index("c")]).astype(jnp.int32)

    def whole_pieces(self, rows):
        return self.S != 4

    def segments(self, n):
        if self.S != 4:
            return [(0, 0, n)]
        half = n // 2
        return [(0, 0, n), (1, 0, n), (2, 0, n), (3, 0, half), (3, half, n - half)]

    def swap_c(self, a):
        return lax.ppermute(a, "c", [(0, 1), (1, 0)])

    def swap_x(self, a):
        return lax.ppermute(a, "slot", [(0, 1), (1, 0), (2, 3), (3, 2)])

    def swap_y(self, a):
        return lax.ppermute(a, "slot", [(0, 2), (2, 0), (1, 3), (3, 1)])

    def spread(self, a, during=()):
        first, second = [*during, None, None][:2]
        if self.S != 4:
            a = lax.all_gather(a, "slot", axis=0, tiled=True)
            for step in (first, second):
                if step is not None:
                    (a,) = step(a)
            return [a]
        half = a.shape[0] // 2
        ax = self.swap_x(a)
        ay = self.swap_y(a)
        if first is not None:
            ax, ay = first(ax, ay)
        d0 = self.swap_y(ax[:half])
        d1 = self.swap_x(ay[half:])
        if second is not None:
            d0, d1 = second(d0, d1)
        return [a, ax, ay, d0, d1]

    def swap_all(self, pieces):
        return [self.swap_c(a) for a in pieces]

    def weight_pieces(self, same):
        other = self.swap_all(same)
        if self.S == 4:
            return [*same, *other]
        n = same[0].shape[1]
        r = same[0].shape[0] // (self.S * self.Z)
        first = lax.axis_index("c") == 0
        same = same[0].reshape(self.S, self.Z, 1, r, n)
        other = other[0].reshape(self.S, self.Z, 1, r, n)
        pair = [jnp.where(first, same, other), jnp.where(first, other, same)]
        return [jnp.concatenate(pair, axis=2).reshape(-1, n)]

    def weight_sides(self, parts):
        if self.S == 4:
            return parts[:4], parts[4:]
        n = parts[0].shape[1]
        whole = parts[0].reshape(self.S, self.Z, 2, -1, n)
        r = whole.shape[3]
        core = lax.axis_index("c")
        return tuple(
            [
                lax.dynamic_slice_in_dim(whole[slot], k, 1, 1).reshape(self.Z * r, n)
                for slot in range(self.S)
            ]
            for k in (core, 1 - core)
        )

    def collect(self, same, other, during=()):
        first, second, third = [*during, None, None, None][:3]
        came = self.swap_all(other)
        if first is not None:
            came = first(*came)
        held = [a.astype(F32) + b.astype(F32) for a, b in zip(same, came)]
        half = same[0].shape[0] // 2
        if self.S != 4:
            total = jnp.concatenate(held, axis=0).astype(BF)
            for step in (second, third):
                if step is not None:
                    (total,) = step(total)
            total = lax.psum_scatter(total, "slot", scatter_dimension=0, tiled=True)
            upper, lower = total[:half].astype(F32), total[half:].astype(F32)
            return [upper, jnp.zeros_like(total[:half]), lower, jnp.zeros_like(total[half:])]
        via_x = self.swap_x(jnp.concatenate([held[1][:half], held[3][:half]], axis=0).astype(BF))
        via_y = self.swap_y(jnp.concatenate([held[2][half:], held[3][half:]], axis=0).astype(BF))
        if second is not None:
            via_x, via_y = second(via_x, via_y)
        via_x, via_y = via_x.astype(F32), via_y.astype(F32)
        upper = held[0][:half] + via_x[:half]
        lower = held[0][half:] + via_y[: via_y.shape[0] // 2]
        upper_last = self.swap_y((held[2][:half] + via_x[half:]).astype(BF))
        lower_last = self.swap_x((held[1][half:] + via_y[via_y.shape[0] // 2 :]).astype(BF))
        if third is not None:
            upper_last, lower_last = third(upper_last, lower_last)
        return [upper, upper_last, lower, lower_last]

    def z_gather(self, w):
        return lax.all_gather(w, "z", axis=0, tiled=True)

    def z_scatter(self, g):
        return lax.psum_scatter(g.astype(BF), "z", scatter_dimension=0, tiled=True)

    def rows_gather(self, w):
        return lax.all_gather(w, ("z", "c"), axis=0, tiled=True)

    def rows_return(self, g):
        n = g.shape[1]
        r = g.shape[0] // self.Z
        core = lax.axis_index("c")
        parts = g.reshape(self.Z // 2, 2, r, n)
        mine = lax.dynamic_slice_in_dim(parts, core, 1, 1).reshape(-1, n)
        sent = lax.dynamic_slice_in_dim(parts, 1 - core, 1, 1).reshape(-1, n)
        came = self.swap_c(sent)
        first = core == 0
        return jnp.concatenate(
            [jnp.where(first, mine, came), jnp.where(first, came, mine)], axis=0
        )

    def cols_exchange(self, gate, up):
        r, n = gate.shape
        ways = 2 * self.S
        parts = jnp.concatenate(
            [gate.reshape(r, ways, n // ways), up.reshape(r, ways, n // ways)], axis=2
        ).transpose(1, 0, 2)
        return self.exchange(parts).reshape(ways * r, 2 * n // ways)

    def cols_return(self, mine):
        ways = 2 * self.S
        m = mine.shape[1] // 2
        parts = self.exchange(mine.reshape(ways, -1, 2 * m)).transpose(1, 0, 2)
        r = parts.shape[0]
        return (
            parts[:, :, :m].reshape(r, ways * m).astype(F32),
            parts[:, :, m:].reshape(r, ways * m).astype(F32),
        )

    def exchange(self, a):
        return lax.all_to_all(a, ("slot", "c"), 0, 0, tiled=True)


def tie(*arrays):
    return lax.optimization_barrier(arrays)


def column(a):
    return jnp.pad(a.reshape(-1, 1), ((0, 0), (0, 127)))


def place_info(row_index, order, lengths, tokens):
    device = row_index // tokens
    local = row_index % tokens
    pick = 2 * device + local // GROUP
    table = jnp.arange(order.shape[0], dtype=jnp.int32)
    group_id = jnp.sum(jnp.where(pick[:, None] == table[None, :], order[None, :], 0), axis=1)
    slot_pos = group_id * GROUP + local % GROUP
    ends = jnp.cumsum(lengths)
    passed = slot_pos[:, None] >= ends[None, :]
    segment = jnp.sum(passed.astype(jnp.int32), axis=1)
    start = jnp.sum(jnp.where(passed, lengths[None, :], 0), axis=1)
    return (slot_pos - start, segment < lengths.shape[0])


def rope_tables(position, width):
    half = width // 2
    freq = ROPE_BASE ** (-2.0 * jnp.arange(half, dtype=F32) / width)
    angle = position.astype(F32)[:, None] * freq[None, :]
    return (jnp.cos(angle), jnp.sin(angle))


def contract_first(left, right):
    return lax.dot_general(left, right, (((0,), (0,)), ((), ())), preferred_element_type=F32)


def _call(kernel, name, out_shape, args, scratch=(), memory=None):
    specs = [
        pl.BlockSpec(
            memory_space=pltpu.SMEM
            if a.dtype == jnp.int32 and a.ndim == 1
            else (memory or pltpu.VMEM)
        )
        for a in args
    ]
    many = isinstance(out_shape, (tuple, list))
    out_specs = [pl.BlockSpec(memory_space=memory or pltpu.VMEM)] * (len(out_shape) if many else 1)
    return pl.pallas_call(
        kernel,
        out_shape=out_shape,
        in_specs=specs,
        out_specs=out_specs if many else out_specs[0],
        scratch_shapes=list(scratch),
        compiler_params=pltpu.CompilerParams(vmem_limit_bytes=VMEM_BYTES),
        cost_estimate=pl.CostEstimate(flops=1, bytes_accessed=1, transcendentals=0),
        name=name,
    )(*args)


def _shape(*dims, dtype=BF):
    return jax.ShapeDtypeStruct(dims, dtype)


def _nt(a, b):
    return lax.dot_general(a, b, (((1,), (1,)), ((), ())), preferred_element_type=F32)


def _tn(a, b):
    return lax.dot_general(a, b, (((0,), (0,)), ((), ())), preferred_element_type=F32)


def _row_place(net, me, place, z, other, r):
    slot = jnp.bitwise_xor(me[0], place) if net.S == 4 else place
    core = 1 - me[1] if other else me[1]
    return pl.multiple_of(((slot * net.Z + z) * 2 + core) * r, r)


def _join(net, me, pieces, whole):
    if len(pieces) == 1:
        whole[...] = pieces[0][...]
        return
    r = whole.shape[0] // (net.S * net.Z * 2)
    for side in range(2):
        for (place, first, count), ref in zip(net.segments(net.Z * r), pieces[side * 5 : side * 5 + 5]):
            for k in range(count // r):
                at = _row_place(net, me, place, first // r + k, side == 1, r)
                whole[pl.ds(at, r), :] = ref[k * r : (k + 1) * r, :]


def _part(net, me, whole, pieces):
    if len(pieces) == 1:
        pieces[0][...] = whole[...]
        return
    r = whole.shape[0] // (net.S * net.Z * 2)
    for side in range(2):
        for place in range(net.S):
            for z in range(net.Z):
                at = _row_place(net, me, place, z, side == 1, r)
                pieces[side * net.S + place][z * r : (z + 1) * r, :] = whole[pl.ds(at, r), :]


def _mean_scale(values):
    return lax.rsqrt(jnp.mean(values * values, axis=1, keepdims=True) + EPS)


def project_kernel(net, count, me, x_ref, cos, sin, *refs):
    pieces, (low_out, kv_out, gain_out, whole) = refs[:count], refs[count:]
    _join(net, me, pieces, whole)
    width = whole.shape[0]
    low_rank = low_out.shape[1]
    last = low_rank + 2 * HD
    gains = jnp.transpose(whole[:, last:].astype(F32))
    gain_out[...] = gains[: gain_out.shape[0], :]
    x = x_ref[...].astype(F32)
    normed = (x * _mean_scale(x) * gains[:1, :]).astype(BF)
    low_out[...] = jnp.dot(normed, whole[:, :low_rank], preferred_element_type=F32)
    both = jnp.dot(normed, whole[:, low_rank:last], preferred_element_type=F32)
    half = HD // 2
    a, b = both[:, :half], both[:, half:HD]
    kv_out[:, :half] = (a * cos[...] - b * sin[...]).astype(BF)
    kv_out[:, half:HD] = (a * sin[...] + b * cos[...]).astype(BF)
    kv_out[:, HD:] = both[:, HD:].astype(BF)


def project(net, me, x, cos, sin, pieces, low_rank):
    tokens, width = x.shape
    wide = pieces[0].shape[1]
    return _call(
        functools.partial(project_kernel, net, len(pieces)),
        "project",
        (_shape(tokens, low_rank, dtype=F32), _shape(tokens, 2 * HD), _shape(8, width, dtype=F32)),
        [me, x, cos, sin, *pieces],
        [pltpu.VMEM((width, wide), BF)],
    )


def _starts(pos, table):
    start = jnp.zeros_like(pos)
    count = table.shape[0] // 2
    for k in range(count):
        start = start + jnp.where(pos >= table[k], table[count + k], 0)
    return start


def _start_of(pos, table):
    start = jnp.int32(0)
    count = table.shape[0] // 2
    for k in range(count):
        start = start + jnp.where(pos >= table[k], table[count + k], 0)
    return start


def _span(group, table):
    return _start_of(group * GROUP, table) // TILE, (group * GROUP + GROUP - 1) // TILE + 1


def _stack(ref, rows, first, heads):
    return jnp.concatenate(
        [ref[rows, (first + h) * HD : (first + h + 1) * HD] for h in range(heads)], axis=0
    )


def _sort_keys(order, kv, sorted_kv):
    for b in range(kv.shape[0] // GROUP):
        at = pl.ds(pl.multiple_of(order[b] * GROUP, GROUP), GROUP)
        sorted_kv[at, :] = kv[b * GROUP : (b + 1) * GROUP, :]


def attend_kernel(net, count, table, order, here, me, low, cos, sin, kv, *refs):
    pieces = refs[:count]
    cqn_out, q_out, att_out, chunk_out, lse_out, up_q, sorted_kv, scores = refs[count:]
    _join(net, me, pieces, up_q)
    _sort_keys(order, kv, sorted_kv)
    wide = H * HD
    gain = jnp.transpose(up_q[:, wide:].astype(F32))[:1, :]
    cqn_out[...] = (low[...] * _mean_scale(low[...]) * gain).astype(BF)
    scale = 1.0 / math.sqrt(HD)
    half = HD // 2
    per_chunk = chunk_out.shape[2] // HD
    for h in range(H):
        full = jnp.dot(
            cqn_out[...], up_q[:, h * HD : (h + 1) * HD], preferred_element_type=F32
        )
        a, b = full[:, :half], full[:, half:]
        q_out[:, h * HD : h * HD + half] = ((a * cos[...] - b * sin[...]) * scale).astype(BF)
        q_out[:, h * HD + half : (h + 1) * HD] = (
            (a * sin[...] + b * cos[...]) * scale
        ).astype(BF)
    for blk in range(2):
        rows = slice(blk * GROUP, (blk + 1) * GROUP)
        group = here[blk]
        lo, hi = _span(group, table)
        for hg in range(H // HG):
            q = _stack(q_out, rows, hg * HG, HG)
            width = HG * GROUP
            pos = group * GROUP + lax.rem(
                lax.broadcasted_iota(jnp.int32, (1, width), 1), GROUP
            )
            start = _starts(pos, table)

            def score(t, top):
                at = pl.ds(pl.multiple_of(t * TILE, TILE), TILE)
                s = _nt(sorted_kv[at, :HD], q)
                key = t * TILE + lax.broadcasted_iota(jnp.int32, (TILE, width), 0)
                s = jnp.where((key >= start) & (key <= pos), s, -1e30)
                scores[at, :] = s
                return jnp.maximum(top, jnp.max(s, axis=0, keepdims=True))

            top = lax.fori_loop(lo, hi, score, jnp.full((1, width), -1e30, F32))

            def weigh(t, carry):
                total, summed = carry
                at = pl.ds(pl.multiple_of(t * TILE, TILE), TILE)
                p = jnp.exp(scores[at, :] - top)
                total = total + jnp.sum(p, axis=0, keepdims=True)
                return total, summed + _tn(sorted_kv[at, HD:], p.astype(BF))

            total, summed = lax.fori_loop(
                lo, hi, weigh, (jnp.zeros((1, width), F32), jnp.zeros((HD, width), F32))
            )
            lse_out[blk, hg : hg + 1, :] = top + jnp.log(total)
            att = jnp.transpose(summed / total)
            for h in range(HG):
                head = hg * HG + h
                piece = att[h * GROUP : (h + 1) * GROUP, :]
                att_out[rows, head * HD : (head + 1) * HD] = piece
                lanes = slice((head % per_chunk) * HD, (head % per_chunk + 1) * HD)
                chunk_out[head // per_chunk, rows, lanes] = piece.astype(BF)


def attend(net, table, order, here, me, low, cos, sin, kv, pieces):
    tokens, low_rank = low.shape
    slot_rows = kv.shape[0]
    ways = 2 * net.S
    return _call(
        functools.partial(attend_kernel, net, len(pieces)),
        "attend",
        (
            _shape(tokens, low_rank),
            _shape(tokens, H * HD),
            _shape(tokens, H * HD, dtype=F32),
            _shape(ways, tokens, H * HD // ways),
            _shape(2, H // HG, HG * GROUP, dtype=F32),
        ),
        [table, order, here, me, low, cos, sin, kv, *pieces],
        [
            pltpu.VMEM((low_rank, pieces[0].shape[1]), BF),
            pltpu.VMEM((slot_rows, 2 * HD), BF),
            pltpu.VMEM((slot_rows, HG * GROUP), F32),
        ],
    )


def _owner(net, me, place, other):
    slot = jnp.bitwise_xor(me[0], place) if net.S == 4 else place
    return slot * 2 + (1 - me[1] if other else me[1])


def out_kernel(net, me, heads, out_rows, *parts):
    tokens, size = heads.shape[1:]
    weight = out_rows[pl.ds(pl.multiple_of(me[1] * size, size), size), :]
    for side in (1, 0):
        for first in range(0, net.S, 2):
            rows = jnp.concatenate(
                [heads[_owner(net, me, first + k, side == 1)] for k in range(2)], axis=0
            )
            got = jnp.dot(rows, weight, preferred_element_type=F32).astype(BF)
            for k in range(2):
                parts[side * net.S + first + k][...] = got[k * tokens : (k + 1) * tokens, :]


def out_forward(net, me, heads, out_rows):
    tokens = heads.shape[1]
    return _call(
        functools.partial(out_kernel, net),
        "out_forward",
        [_shape(tokens, out_rows.shape[1])] * (2 * net.S),
        [me, heads, out_rows],
    )


def _blocks(net, n):
    piece = n // (net.S * net.Z)
    return piece, [s * net.Z + z for z in range(net.Z) for s in range(net.S)]


def middle_kernel(net, x, gains, left, left_last, right, right_last, mid_out, h2_out):
    half = left.shape[0]
    for rows, one, two in ((slice(0, half), left, left_last), (slice(half, 2 * half), right, right_last)):
        mid = x[rows, :].astype(F32) + (one[...].astype(F32) + two[...].astype(F32))
        mid_out[rows, :] = mid
        h2 = (mid * _mean_scale(mid) * gains[1:2, :]).astype(BF)
        piece, places = _blocks(net, mid.shape[1])
        for k, place in enumerate(places):
            h2_out[rows, k * piece : (k + 1) * piece] = h2[:, place * piece : (place + 1) * piece]


def middle_forward(net, x, gains, parts):
    return _call(
        functools.partial(middle_kernel, net),
        "middle_forward",
        (_shape(*x.shape, dtype=F32), _shape(*x.shape)),
        [x, gains, *parts],
    )


def middle_back_kernel(net, mid_ref, gains, cot, left, left_last, right, right_last, grad_out, low_out, gain_out):
    half = left.shape[0]
    total = jnp.zeros((1, mid_ref.shape[1]), F32)
    gain = gains[1:2, :]
    for rows, one, two in ((slice(0, half), left, left_last), (slice(half, 2 * half), right, right_last)):
        came = one[...].astype(F32) + two[...].astype(F32)
        piece, places = _blocks(net, came.shape[1])
        back = [None] * len(places)
        for k, place in enumerate(places):
            back[place] = came[:, k * piece : (k + 1) * piece]
        upstream = jnp.concatenate(back, axis=1)
        mid = mid_ref[rows, :]
        scale = _mean_scale(mid)
        scaled = gain * upstream
        total = total + jnp.sum(upstream * mid * scale, axis=0, keepdims=True)
        inner = jnp.mean(scaled * mid, axis=1, keepdims=True)
        grad = cot[rows, :].astype(F32) + scale * scaled - mid * (scale * scale * scale * inner)
        grad_out[rows, :] = grad
        low_out[rows, :] = grad.astype(BF)
    gain_out[...] = jnp.broadcast_to(total, gain_out.shape)


def middle_back(net, mid, gains, cot, parts):
    return _call(
        functools.partial(middle_back_kernel, net),
        "middle_back",
        (_shape(*mid.shape, dtype=F32), _shape(*mid.shape), _shape(8, mid.shape[1], dtype=F32)),
        [mid, gains, cot, *parts],
    )


def _tiles(rows, size):
    tiles, held, left = [], [], size
    for k, n in enumerate(rows):
        first = 0
        while first < n:
            take = min(left, n - first)
            held.append((k, first, take))
            first, left = first + take, left - take
            if not left:
                tiles.append(held)
                held, left = [], size
    assert not held
    return tiles


def ffn_kernel(net, tiles, splits, me, *refs):
    count = len({k for tile in tiles for k, _, _ in tile})
    results = len({k for tile in splits for k, _, _ in tile})
    h, d = refs[:count], refs[count : 2 * count]
    gu_w, down_rows = refs[2 * count : 2 * count + 2]
    outs = refs[2 * count + 2 : 2 * count + 2 + results]
    h_out, d_out, hid_out, dgu_out = refs[2 * count + 2 + results : 2 * count + 6 + results]
    hv, dv, gv, wv, xv, hidv, dguv, sem_in, sem_out = refs[2 * count + 6 + results :]
    wide = hid_out.shape[1]
    size = hv.shape[1]

    def fetch(t, sources, target, sem):
        copies, at = [], 0
        for n, (k, first, rows) in enumerate(tiles[t]):
            copies.append(
                pltpu.make_async_copy(
                    sources[k].at[pl.ds(first, rows)], target.at[t, pl.ds(at, rows)], sem.at[n]
                )
            )
            at += rows
        return copies

    gu_copy = pltpu.make_async_copy(gu_w, gv, sem_in.at[0, 0, 0])
    down_copy = pltpu.make_async_copy(
        down_rows.at[pl.ds(pl.multiple_of(me[1] * wide, 16), wide)], wv, sem_in.at[0, 0, 1]
    )
    h_copies = [fetch(t, h, hv, sem_in.at[1, t]) for t in range(len(tiles))]
    d_copies = [fetch(t, d, dv, sem_in.at[2, t]) for t in range(len(tiles))]
    for c in d_copies[0] + [down_copy] + h_copies[0] + [gu_copy]:
        c.start()
    for t in range(1, len(tiles)):
        for c in d_copies[t] + h_copies[t]:
            c.start()
    sent = []

    def send(source, target, sem):
        copy = pltpu.make_async_copy(source, target, sem)
        copy.start()
        sent.append(copy)

    for t in range(len(tiles)):
        rows = pl.ds(t * size, size)
        for c in d_copies[t] + ([down_copy] if t == 0 else []):
            c.wait()
        send(dv.at[t], d_out.at[rows], sem_out.at[t, 0])
        grad = _nt(dv[t], wv[...])
        for c in h_copies[t] + ([gu_copy] if t == 0 else []):
            c.wait()
        send(hv.at[t], h_out.at[rows], sem_out.at[t, 1])
        both = jnp.dot(hv[t], gv[...], preferred_element_type=F32)
        gate = both[:, :wide]
        up = both[:, wide:]
        sigma = jax.nn.sigmoid(gate)
        silu = gate * sigma
        hidv[t] = (silu * up).astype(BF)
        send(hidv.at[t], hid_out.at[rows], sem_out.at[t, 2])
        dguv[t] = jnp.concatenate(
            [grad * up * sigma * (1.0 + gate * (1.0 - sigma)), grad * silu], axis=1
        ).astype(BF)
        send(dguv.at[t], dgu_out.at[rows], sem_out.at[t, 3])
        xv[t] = _nt(dguv[t], gv[...]).astype(BF)
        at = 0
        for n, (k, first, take) in enumerate(splits[t]):
            send(xv.at[t, pl.ds(at, take)], outs[k].at[pl.ds(first, take)], sem_out.at[t, 4 + n])
            at += take
    for copy in sent:
        copy.wait()


def ffn(net, me, h, d, gu_w, down_rows, tokens):
    width = gu_w.shape[0]
    wide = gu_w.shape[1] // 2
    size = 2 * tokens
    tiles = _tiles([a.shape[0] for a in h], size)
    out_rows = [tokens] * (2 * net.S)
    splits = _tiles(out_rows, size)
    steps = len(tiles)
    every = steps * size
    return _call(
        functools.partial(ffn_kernel, net, tiles, splits),
        "ffn",
        [_shape(n, width) for n in out_rows]
        + [_shape(every, n) for n in (width, width, wide, 2 * wide)],
        [me, *h, *d, gu_w, down_rows],
        [
            pltpu.VMEM((steps, size, width), BF),
            pltpu.VMEM((steps, size, width), BF),
            pltpu.VMEM((width, 2 * wide), BF),
            pltpu.VMEM((wide, width), BF),
            pltpu.VMEM((steps, size, width), BF),
            pltpu.VMEM((steps, size, wide), BF),
            pltpu.VMEM((steps, size, 2 * wide), BF),
            pltpu.SemaphoreType.DMA((3, steps, 5)),
            pltpu.SemaphoreType.DMA((steps, 8)),
        ],
        memory=pl.ANY,
    )


def out_back_kernel(net, count, me, out_rows, *refs):
    rows_in, (heads_out,) = refs[:count], refs[count:]
    ways, tokens, size = heads_out.shape
    weight = out_rows[pl.ds(pl.multiple_of(me[1] * size, size), size), :]
    group = count // 2
    for side in range(2):
        rows = jnp.concatenate([ref[...] for ref in rows_in[side * group : (side + 1) * group]], axis=0)
        got = _nt(rows, weight).astype(BF)
        for place in range(net.S):
            heads_out[_owner(net, me, place, side == 0)] = got[place * tokens : (place + 1) * tokens, :]


def out_back(net, me, out_rows, rows, tokens):
    ways = 2 * net.S
    return _call(
        functools.partial(out_back_kernel, net, len(rows)),
        "out_back",
        _shape(ways, tokens, out_rows.shape[0] // 2),
        [me, out_rows, *rows],
    )


def out_grad_kernel(net, count, me, heads, *refs):
    rows_in, (grad_out,) = refs[:count], refs[count:]
    group = count // 2
    total = None
    for side in range(2):
        left = jnp.concatenate(
            [heads[_owner(net, me, place, side == 0)] for place in range(net.S)], axis=0
        )
        right = jnp.concatenate([ref[...] for ref in rows_in[side * group : (side + 1) * group]], axis=0)
        part = _tn(left, right)
        total = part if total is None else total + part
    grad_out[...] = total.astype(BF)


def out_weight_grad(net, me, heads, rows):
    return _call(
        functools.partial(out_grad_kernel, net, len(rows)),
        "out_weight_grad",
        _shape(heads.shape[2], rows[0].shape[1]),
        [me, heads, *rows],
    )


def back_kernel(table, order, here, q_in, grad, att, lse, cos, sin, kv, dq_out, dkv_out, sorted_kv, dk, dv):
    _sort_keys(order, kv, sorted_kv)
    dk[...] = jnp.zeros_like(dk)
    dv[...] = jnp.zeros_like(dv)
    scale = 1.0 / math.sqrt(HD)
    half = HD // 2
    per_chunk = grad.shape[2] // HD
    for blk in range(2):
        rows = slice(blk * GROUP, (blk + 1) * GROUP)
        group = here[blk]
        lo, hi = _span(group, table)
        cosine, sine = cos[rows, :], sin[rows, :]
        for hg in range(H // HG):
            width = HG * GROUP
            q = _stack(q_in, rows, hg * HG, HG)
            da = jnp.concatenate(
                [
                    grad[
                        head // per_chunk,
                        rows,
                        (head % per_chunk) * HD : (head % per_chunk + 1) * HD,
                    ]
                    for head in range(hg * HG, (hg + 1) * HG)
                ],
                axis=0,
            )
            kept = _stack(att, rows, hg * HG, HG)
            delta = jnp.sum(da.astype(F32) * kept, axis=1, keepdims=True)
            delta = jnp.transpose(jnp.broadcast_to(delta, (width, 128)))[:1, :]
            shift = lse[blk, hg : hg + 1, :]
            pos = group * GROUP + lax.rem(
                lax.broadcasted_iota(jnp.int32, (1, width), 1), GROUP
            )
            start = _starts(pos, table)

            def step(t, dq):
                at = pl.ds(pl.multiple_of(t * TILE, TILE), TILE)
                k = sorted_kv[at, :HD]
                s = _nt(k, q)
                key = t * TILE + lax.broadcasted_iota(jnp.int32, (TILE, width), 0)
                p = jnp.where((key >= start) & (key <= pos), jnp.exp(s - shift), 0.0)
                dp = _nt(sorted_kv[at, HD:], da)
                ds = (p * (dp - delta)).astype(BF)
                dv[at, :] += jnp.dot(p.astype(BF), da, preferred_element_type=F32)
                dk[at, :] += jnp.dot(ds, q, preferred_element_type=F32)
                return dq + _tn(k, ds)

            dq = jnp.transpose(lax.fori_loop(lo, hi, step, jnp.zeros((HD, width), F32)))
            dq = dq * scale
            for h in range(HG):
                head = hg * HG + h
                a = dq[h * GROUP : (h + 1) * GROUP, :half]
                b = dq[h * GROUP : (h + 1) * GROUP, half:]
                dq_out[rows, head * HD : head * HD + half] = (a * cosine + b * sine).astype(BF)
                dq_out[rows, head * HD + half : (head + 1) * HD] = (
                    b * cosine - a * sine
                ).astype(BF)
    for b in range(kv.shape[0] // GROUP):
        at = pl.ds(pl.multiple_of(order[b] * GROUP, GROUP), GROUP)
        dkv_out[b * GROUP : (b + 1) * GROUP, :HD] = dk[at, :].astype(BF)
        dkv_out[b * GROUP : (b + 1) * GROUP, HD:] = dv[at, :].astype(BF)


def attend_back(table, order, here, q, grad, att, lse, cos, sin, kv):
    slot_rows = kv.shape[0]
    return _call(
        back_kernel,
        "attend_back",
        (_shape(*q.shape), _shape(slot_rows, 2 * HD)),
        [table, order, here, q, grad, att, lse, cos, sin, kv],
        [
            pltpu.VMEM((slot_rows, 2 * HD), BF),
            pltpu.VMEM((slot_rows, HD), F32),
            pltpu.VMEM((slot_rows, HD), F32),
        ],
    )


def up_back_kernel(net, count, results, me, dq, cqn, low_ref, *refs):
    pieces, outs = refs[:count], refs[count : count + results]
    low_grad_out, up_q, grad = refs[count + results :]
    _join(net, me, pieces, up_q)
    wide = dq.shape[1]
    gain = jnp.transpose(up_q[:, wide:].astype(F32))[:1, :]
    upstream = _nt(dq[...], up_q[:, :wide])
    low = low_ref[...]
    scale = _mean_scale(low)
    gain_grad = jnp.sum(upstream * low * scale, axis=0, keepdims=True)
    scaled = gain * upstream
    inner = jnp.mean(scaled * low, axis=1, keepdims=True)
    low_grad_out[...] = (scale * scaled - low * (scale * scale * scale * inner)).astype(BF)
    step = 1024
    for first in range(0, wide, step):
        grad[:, first : first + step] = _tn(cqn[...], dq[:, first : first + step]).astype(BF)
    grad[:, wide:] = jnp.transpose(
        jnp.broadcast_to(gain_grad, (128, gain_grad.shape[1]))
    ).astype(BF)
    _part(net, me, grad, outs)


def up_back(net, me, dq, cqn, low, pieces):
    tokens, low_rank = low.shape
    wide = pieces[0].shape[1]
    outs = _out_pieces(net, low_rank, wide)
    *parts, grad = _call(
        functools.partial(up_back_kernel, net, len(pieces), len(outs)),
        "up_back",
        outs + [_shape(tokens, low_rank)],
        [me, dq, cqn, low, *pieces],
        [pltpu.VMEM((low_rank, wide), BF), pltpu.VMEM((low_rank, wide), BF)],
    )
    return parts, grad


def _out_pieces(net, rows, wide):
    if not net.whole_pieces(rows):
        return [_shape(rows // (2 * net.S), wide)] * (2 * net.S)
    return [_shape(rows, wide)]


def project_back_kernel(net, count, results, me, x_ref, low_grad, both, cos, sin, mid_grad, gains, mid_gain, *refs):
    pieces, outs = refs[:count], refs[count : count + results]
    in_out, whole, grad = refs[count + results :]
    _join(net, me, pieces, whole)
    width = whole.shape[0]
    low_rank = low_grad.shape[1]
    last = low_rank + 2 * HD
    half = HD // 2
    a, b = both[:, :half].astype(F32), both[:, half:HD].astype(F32)
    upstream_parts = jnp.concatenate(
        [
            low_grad[...],
            (a * cos[...] + b * sin[...]).astype(BF),
            (b * cos[...] - a * sin[...]).astype(BF),
            both[:, HD:].astype(BF),
        ],
        axis=1,
    )
    x = x_ref[...].astype(F32)
    scale = _mean_scale(x)
    gain = gains[:1, :]
    normed = (x * scale * gain).astype(BF)
    for first in range(0, last, 512):
        grad[:, first : first + 512] = _tn(normed, upstream_parts[:, first : first + 512]).astype(BF)
    upstream = _nt(upstream_parts, whole[:, :last])
    gain_grad = jnp.sum(upstream * x * scale, axis=0, keepdims=True)
    scaled = gain * upstream
    inner = jnp.mean(scaled * x, axis=1, keepdims=True)
    in_out[...] = (mid_grad[...] + scale * scaled - x * (scale * scale * scale * inner)).astype(BF)
    tall = lax.broadcasted_iota(jnp.int32, (128, width), 0)
    both_gains = jnp.where(
        tall == 0, jnp.broadcast_to(gain_grad, (128, width)),
        jnp.broadcast_to(mid_gain[:1, :], (128, width)),
    )
    grad[:, last:] = jnp.transpose(both_gains).astype(BF)
    _part(net, me, grad, outs)


def project_back(net, me, x, low_grad, both, cos, sin, mid_grad, gains, mid_gain, pieces):
    tokens, width = x.shape
    wide = pieces[0].shape[1]
    outs = _out_pieces(net, width, wide)
    *parts, in_grad = _call(
        functools.partial(project_back_kernel, net, len(pieces), len(outs)),
        "project_back",
        outs + [_shape(tokens, width)],
        [me, x, low_grad, both, cos, sin, mid_grad, gains, mid_gain, *pieces],
        [pltpu.VMEM((width, wide), BF), pltpu.VMEM((width, wide), BF)],
    )
    return parts, in_grad


def share_kernel(net, me, hidden, down_rows, *parts):
    tokens = parts[0].shape[0]
    wide = hidden.shape[1]
    weight = down_rows[pl.ds(pl.multiple_of(me[1] * wide, 16), wide), :]
    for first in range(0, len(parts), 2):
        rows = hidden[first * tokens : (first + 2) * tokens, :]
        got = jnp.dot(rows, weight, preferred_element_type=F32).astype(BF)
        for k in range(2):
            parts[first + k][...] = got[k * tokens : (k + 1) * tokens, :]


def down_share(net, me, hidden, down_rows, tokens):
    return _call(
        functools.partial(share_kernel, net),
        "down_share",
        [_shape(tokens, down_rows.shape[1])] * (2 * net.S),
        [me, hidden, down_rows],
    )


def body(
    net,
    hidden_in, seq_lens, group_order, attn_gain, wq_down, q_gain, wq_up, w_key, w_value, w_out,
    ffn_gain, w_gate, w_up, w_down, out_grad,
):
    lengths = seq_lens[0]
    order = group_order[0]
    tokens = hidden_in.shape[0]
    low_rank = wq_up.shape[0] * net.S * net.Z * 2
    last = low_rank + 2 * HD
    me = net.me()
    place = lax.axis_index("z") * 2 + lax.axis_index("c")
    rows_here = place * tokens + jnp.arange(tokens, dtype=jnp.int32)
    seq_pos, valid = place_info(rows_here, order, lengths, tokens)
    cosine, sine = rope_tables(seq_pos, HD)
    table = jnp.concatenate([jnp.cumsum(lengths), lengths]).astype(jnp.int32)
    here = lax.dynamic_slice_in_dim(order, 2 * place, 2, 0)
    kept = {}

    gains = column(attn_gain) + jnp.roll(column(ffn_gain), 1, axis=1)
    first_z = net.z_gather(jnp.concatenate([wq_down, w_key, w_value, gains], axis=1))
    up_z = net.z_gather(jnp.concatenate([wq_up, column(q_gain)], axis=1))
    out_rows = net.rows_gather(w_out)
    down_rows = net.rows_gather(w_down)

    def first_one(*moved):
        *moved, kept["up_z"] = tie(*moved, up_z)
        return moved

    first_pieces = net.weight_pieces(net.spread(first_z, (first_one,)))

    w_gate, w_up, *_ = tie(w_gate, w_up, *first_pieces)
    gu_mine = net.cols_exchange(w_gate, w_up)

    def up_one(*moved):
        kept["gu_mine"], *moved = tie(gu_mine, *moved)
        return moved

    up_pieces = net.weight_pieces(net.spread(kept["up_z"], (up_one,)))

    query_low, kv, gains = project(net, me, hidden_in, cosine, sine, first_pieces, low_rank)
    kv, out_rows = tie(kv, out_rows)
    both = net.rows_gather(kv)
    gu_chunk = net.z_gather(kept["gu_mine"])
    cot = (out_grad.astype(F32) * valid[:, None].astype(F32)).astype(BF)
    cot, *_ = tie(cot, *up_pieces)

    def cot_one(*moved):
        kept["attend"] = attend(
            net, table, order, here, me, query_low, cosine, sine, both, up_pieces
        )
        *kept["attend"], a, b = tie(*kept["attend"], *moved, *moved[: 2 - len(moved)])
        return [a, b][: len(moved)]

    def cot_two(*moved):
        heads = net.exchange(kept["attend"][3])
        parts = out_forward(net, me, heads, out_rows)
        kept["heads"] = heads
        done = tie(*moved, *parts)
        kept["out_parts"] = done[len(moved) :]
        return done[: len(moved)]

    cot_same = net.spread(cot, (cot_one, cot_two))
    cot_other = net.swap_all(cot_same)
    query_normed, query_rows, attended, _, log_total = kept["attend"]
    heads = kept["heads"]
    out_parts = kept["out_parts"]
    middle, normed_two = middle_forward(
        net, hidden_in, gains, net.collect(out_parts[: net.S], out_parts[net.S :])
    )

    two_same = net.spread(normed_two)
    two_all = [*net.swap_all(two_same), *two_same]
    cot_all = [*cot_other, *cot_same]
    *back_parts, two_rows, cot_rows, hidden, gu_grad = ffn(
        net, me, two_all, cot_all, gu_chunk, down_rows, tokens
    )

    def back_one(*came):
        *_, kept["hidden"], kept["gu_grad"] = tie(*came, hidden, gu_grad)
        kept["grad_down"] = net.rows_return(contract_first(kept["hidden"], cot_rows).astype(BF))
        return came

    def back_two(*moved):
        *moved, kept["grad_down"] = tie(*moved, kept["grad_down"])
        gu_grad, *_ = tie(kept["gu_grad"], *moved)
        kept["grad_gu"] = contract_first(two_rows, gu_grad).astype(BF)
        return moved

    def back_three(*moved):
        *moved, kept["grad_gu"] = tie(*moved, kept["grad_gu"])
        return moved

    middle_grad, middle_low, middle_gain = middle_back(
        net,
        middle,
        gains,
        cot,
        net.collect(
            back_parts[net.S :], back_parts[: net.S], (back_one, back_two, back_three)
        ),
    )
    grad_down = net.z_scatter(kept["grad_down"])
    grad_gu = net.z_scatter(kept["grad_gu"])

    def middle_one(*moved):
        hidden, *_ = tie(kept["hidden"], middle_low)
        shares = down_share(net, me, hidden, down_rows, tokens)
        done = tie(*moved, *shares)
        kept["shares"] = done[len(moved) :]
        return done[: len(moved)]

    def middle_two(*moved):
        *moved, kept["grad_down"] = tie(*moved, grad_down)
        return moved

    middle_same = net.spread(middle_low, (middle_one, middle_two))
    grad_down = kept["grad_down"].astype(F32)
    middle_all = [*net.swap_all(middle_same), *middle_same]
    heads_grad = net.exchange(out_back(net, me, out_rows, middle_all, tokens))
    grad_out = net.rows_return(out_weight_grad(net, me, heads, middle_all))
    heads_grad, grad_out, *shares = tie(heads_grad, grad_out, *kept["shares"])
    grad_out = net.z_scatter(grad_out)

    def result_two(*moved):
        backs = attend_back(
            table, order, here, query_rows, heads_grad, attended, log_total, cosine, sine, both
        )
        *moved, kept["query_pre"], kept["both_grads"], kept["grad_gu"] = tie(
            *moved, *backs, grad_gu
        )
        return moved

    upper, upper_last, lower, lower_last = net.collect(
        shares[net.S :], shares[: net.S], (None, result_two)
    )
    layer_out = (
        middle
        + jnp.concatenate(
            [upper + upper_last.astype(F32), lower + lower_last.astype(F32)], axis=0
        )
    ).astype(BF)
    both_sum = lax.psum_scatter(kept["both_grads"], ("z", "c"), scatter_dimension=0, tiled=True)
    up_parts, low_grad = up_back(net, me, kept["query_pre"], query_normed, query_low, up_pieces)

    def whole(parts):
        upper, upper_last, lower, lower_last = parts
        return net.z_scatter(
            jnp.concatenate(
                [upper + upper_last.astype(F32), lower + lower_last.astype(F32)], axis=0
            )
        ).astype(F32)

    up_out = whole(net.collect(*net.weight_sides(up_parts)))
    first_parts, in_grad = project_back(
        net, me, hidden_in, low_grad, both_sum, cosine, sine, middle_grad, gains, middle_gain,
        first_pieces,
    )

    def first_two(*moved):
        *moved, kept["grad_out"] = tie(*moved, grad_out)
        return moved

    first_out = whole(net.collect(*net.weight_sides(first_parts), (None, first_two)))
    grad_out = kept["grad_out"].astype(F32)
    grad_gate, grad_upward = net.cols_return(kept["grad_gu"])
    return (
        layer_out,
        in_grad,
        first_out[:, last],
        first_out[:, :low_rank],
        up_out[:, H * HD],
        up_out[:, : H * HD],
        first_out[:, low_rank : low_rank + HD],
        first_out[:, low_rank + HD : last],
        grad_out,
        first_out[:, last + 1],
        grad_gate,
        grad_upward,
        grad_down,
    )


def solution(mesh):
    slots, seq = mesh.devices.shape
    fine = Mesh(mesh.devices.reshape(slots, seq // 2, 2), ("slot", "z", "c"))
    every = ("slot", "z", "c")
    matrix = P(every, None)
    vector = P(every)
    net = Net(slots, seq // 2)
    return jax.shard_map(
        functools.partial(body, net),
        mesh=fine,
        in_specs=(
            matrix, P("slot", None), P("slot", None), vector, matrix, vector, matrix, matrix,
            matrix, matrix, vector, matrix, matrix, matrix, matrix,
        ),
        out_specs=(
            matrix, matrix, vector, matrix, vector, matrix, matrix, matrix, matrix, vector,
            matrix, matrix, matrix,
        ),
        check_vma=False,
    )
```

time: 3470 us -> 727 us (0.21)
  waiting for transfers between devices: 2970 us -> 326 us
  matrix products: 292 us -> 22 us
  Pallas kernels: 0 us -> 149 us
  blocking collectives: 114 us -> 32 us
  starting transfers between devices: 1.47 us -> 71.1 us
    reduce_scatter x10 -> x6, waiting for transfers between devices: 2340 us -> 37.7 us  [the longest x5 37.7 us: z_scatter(): return lax.psum_scatter(g.astype(BF), 'z', scatter_dimension=0, tiled=True)]
    all_gather x8 -> x5, waiting for transfers between devices: 623 us -> 12.1 us  [the longest x3 12 us: rows_gather(): return lax.all_gather(w, ('z', 'c'), axis=0, tiled=True)]
    ppermute x0 -> x87, waiting for transfers between devices: none -> 241 us  [the longest x20 149 us: swap_x(): return lax.ppermute(a, 'slot', [(0, 1), (1, 0), (2, 3), (3, 2)])]
    dot_general x31 -> x0, matrix products: 184 us -> none  [the longest x17 100 us: contract_last(): lax.dot_general(left, right, (((1,), (1,)), ((), ())), preferred_element_...]
    pallas_call x0 -> x12, Pallas kernels: none -> 149 us  [_call(): pl.pallas_call(kernel, out_shape=out_shape, in_specs=specs, out_specs=out...]
    dot_general x14 -> x2, matrix products: 108 us -> 22 us  [contract_first(): lax.dot_general(left, right, (((0,), (0,)), ((), ())), preferred_element_...]
    unnamed x2 -> x0, blocking collectives: 80.4 us -> none
    ppermute x0 -> x87, starting transfers between devices: none -> 53.8 us  [the longest x20 23.7 us: swap_y(): return lax.ppermute(a, 'slot', [(0, 2), (2, 0), (1, 3), (3, 1)])]
  transfers between devices with their start and end apart: 18 -> 102, of which waited for: 17 -> 45; matrix products, arithmetic and copies ran while one was open for 6% -> 13% of each run, Pallas kernels for 0% -> 16%
where the time goes in v2:
time: 727 us; the launch traced here: 717 us
  waiting for transfers between devices  326 us (45%)
  Pallas kernels  149 us (20%)
  starting transfers between devices  71.1 us (10%)
  other arithmetic  62.7 us (9%)
  local copies, waits for them, and re-layouts  39.4 us (5%)
  blocking collectives  32 us (4%)
  matrix products  22 us (3%)
  between operations  15.6 us (2%)
    ppermute x20, waiting for transfers between devices, swap_x(): return lax.ppermute(a, 'slot', [(0, 1), (1, 0), (2, 3), (3, 2)])  149 us
    pallas_call x12, Pallas kernels, _call(): pl.pallas_call(kernel, out_shape=out_shape, in_specs=specs, out_specs=out...  149 us
    ppermute x20, waiting for transfers between devices, swap_y(): return lax.ppermute(a, 'slot', [(0, 2), (2, 0), (1, 3), (3, 1)])  80.4 us
    reduce_scatter x5, waiting for transfers between devices, z_scatter(): return lax.psum_scatter(g.astype(BF), 'z', scatter_dimension=0, tiled=True)  37.7 us
    all_to_all x4, waiting for transfers between devices, exchange(): return lax.all_to_all(a, ('slot', 'c'), 0, 0, tiled=True)  33.6 us
    all_gather x1, blocking collectives, z_gather(): return lax.all_gather(w, 'z', axis=0, tiled=True)  32 us
    ppermute x20, starting transfers between devices, swap_y(): return lax.ppermute(a, 'slot', [(0, 2), (2, 0), (1, 3), (3, 1)])  23.7 us
    dot_general x2, matrix products, contract_first(): lax.dot_general(left, right, (((0,), (0,)), ((), ())), preferred_element_...  22 us
  transfers between devices with their start and end apart: 102, of which 45 were waited for; matrix products, arithmetic and copies ran while one was open for 13% of the time, Pallas kernels for 16%

profile of v2, /device:TPU:0, one launch (start us, length us, event | category | flops | bytes accessed | tf_op | source)
XLA Modules:
  0.0 717.4 jit_solution(9502578517171617658)
XLA Ops:
  13.1 32.0 %all_gather.18.refs_0_ = bf16[256,1664]{1,0:T(8,128)(2,1)S(1)} all-gather(bf16[64,1664]{1,0:T(8,128)(2,1)S(1)} %pad_maximum_fusion.14), channel_id=1, replica_groups=mesh['slot'=4,'z'=4,'c'=2] {'z'}, dimensions={0}, use_global_device_ids=true | all-gather | bytes 1064960 | tf_op jit(solution)/shard_map/all_gather | solution.py:129
  48.2 14.4 %collective-permute-done.refs_1_ = bf16[256,1664]{1,0:T(8,128)(2,1)S(1)} collective-permute-done((bf16[256,1664]{1,0:T(8,128)(2,1)S(1)}, bf16[256,1664]{1,0:T(8,128)(2,1)S(1)}, u32[]{:S(2)}, u32[]{:S(2)}) %collective-permute-start) | collective-permute-done | bytes 852000 | tf_op jit(solution)/shard_map/ppermute | solution.py:46
  67.0 9.0 %collective-permute-done.2.refs_3_ = bf16[128,1664]{1,0:T(8,128)(2,1)S(1)} collective-permute-done((bf16[128,1664]{1,0:T(8,128)(2,1)S(1)}, bf16[128,1664]{1,0:T(8,128)(2,1)S(1)}, u32[]{:S(2)}, u32[]{:S(2)}) %collective-permute-start.2) | collective-permute-done | bytes 426016 | tf_op jit(solution)/shard_map/ppermute | solution.py:49
  87.3 12.0 %all-gather.8.cloned.1.call-done.out_rows = bf16[1024,2048]{1,0:T(8,128)(2,1)} async-done(((bf16[128,2048]{1,0:T(8,128)(2,1)}), bf16[1024,2048]{1,0:T(8,128)(2,1)}) %all-gather.8.cloned.1.call-update) | async-done | bytes 4194320 | tf_op jit(solution)/shard_map/all_gather | solution.py:135
  112.1 38.4 %collective-permute-done.9.refs_1_ = bf16[128,4224]{1,0:T(8,128)(2,1)S(1)} collective-permute-done((bf16[128,4224]{1,0:T(8,128)(2,1)}, bf16[128,4224]{1,0:T(8,128)(2,1)S(1)}, u32[]{:S(2)}, u32[]{:S(2)}) %collective-permute-start.9) | collective-permute-done | bytes 1081376 | tf_op jit(solution)/shard_map/ppermute | solution.py:46
  153.3 11.3 %collective-permute-done.11.refs_3_ = bf16[64,4224]{1,0:T(8,128)(2,1)S(1)} collective-permute-done((bf16[64,4224]{1,0:T(8,128)(2,1)S(1)}, bf16[64,4224]{1,0:T(8,128)(2,1)S(1)}, u32[]{:S(2)}, u32[]{:S(2)}) %collective-permute-start.11) | collective-permute-done | bytes 540704 | tf_op jit(solution)/shard_map/ppermute | solution.py:49
  172.1 21.0 %attend.1 = (bf16[192,1024]{1,0:T(8,128)(2,1)}, bf16[192,4096]{1,0:T(8,128)(2,1)}, f32[192,4096]{1,0:T(8,128)}, bf16[8,192,512]{2,1,0:T(8,128)(2,1)}, f32[2,2,768]{2,1,0:T(2,128)}) custom-call(s32[16]{0:T(128)} %pad_add_fusion.2.table, s32[16]{0:T(128)} %bitcast.33, s32[2]{0:T(128)} %fusion.29.here, s32[2]{0:T(128)} %pad_add_fusion.1.me, ...), custom_call_target="tpu_custom_call" | custom-call | flops 1 | bytes 1 | tf_op jit(solution)/shard_map/attend/pallas_call | solution.py:216
  203.5 15.8 %all-to-all-done.1.heads = bf16[8,192,512]{2,1,0:T(8,128)(2,1)S(1)} async-done(((bf16[8,192,512]{2,1,0:T(8,128)(2,1)}), bf16[8,192,512]{2,1,0:T(8,128)(2,1)S(1)}, u32[]{:S(2)}, u32[]{:S(2)}) %all-to-all-start.1) | async-done | bytes 1572896 | tf_op jit(solution)/shard_map/all_to_all | solution.py:169
  235.0 17.1 %collective-permute-done.28 = bf16[192,2048]{1,0:T(8,128)(2,1)S(1)} collective-permute-done((bf16[192,2048]{1,0:T(8,128)(2,1)S(1)}, bf16[192,2048]{1,0:T(8,128)(2,1)S(1)}, u32[]{:S(2)}, u32[]{:S(2)}) %collective-permute-start.28) | collective-permute-done | bytes 786464 | tf_op jit(solution)/shard_map/ppermute | solution.py:49
  256.3 9.3 %collective-permute-done.27.left_last = bf16[96,2048]{1,0:T(8,128)(2,1)S(1)} collective-permute-done((bf16[96,2048]{1,0:T(8,128)(2,1)S(1)}, bf16[96,2048]{1,0:T(8,128)(2,1)S(1)}, u32[]{:S(2)}, u32[]{:S(2)}) %collective-permute-start.27) | collective-permute-done | bytes 393248 | tf_op jit(solution)/shard_map/ppermute | solution.py:49
  272.8 15.8 %collective-permute-done.31.refs_6_ = bf16[192,2048]{1,0:T(8,128)(2,1)S(1)} collective-permute-done((bf16[192,2048]{1,0:T(8,128)(2,1)}, bf16[192,2048]{1,0:T(8,128)(2,1)S(1)}, u32[]{:S(2)}, u32[]{:S(2)}) %collective-permute-start.31) | collective-permute-done | bytes 786464 | tf_op jit(solution)/shard_map/ppermute | solution.py:46
  306.1 35.5 %ffn.1 = (bf16[192,2048]{1,0:T(8,128)(2,1)}, bf16[192,2048]{1,0:T(8,128)(2,1)}, bf16[192,2048]{1,0:T(8,128)(2,1)}, bf16[192,2048]{1,0:T(8,128)(2,1)}, bf16[192,2...) custom-call(s32[2]{0:T(128)} %pad_add_fusion.1.me, ...), custom_call_target="tpu_custom_call" | custom-call | flops 1 | bytes 1 | tf_op jit(solution)/shard_map/ffn/pallas_call | solution.py:216
  364.6 14.2 %collective-permute-done.47 = bf16[192,2048]{1,0:T(8,128)(2,1)} collective-permute-done((bf16[192,2048]{1,0:T(8,128)(2,1)}, bf16[192,2048]{1,0:T(8,128)(2,1)}, u32[]{:S(2)}, u32[]{:S(2)}) %collective-permute-start.47) | collective-permute-done | bytes 786464 | tf_op jit(solution)/shard_map/ppermute | solution.py:46
  388.9 14.2 %convolution_convert_fusion = bf16[2048,1408]{1,0:T(8,128)(2,1)} fusion(bf16[1536,2048]{1,0:T(8,128)(2,1)S(1)} %bitcast.45, bf16[1536,1408]{1,0:T(8,128)(2,1)} %get-tuple-element.201), kind=kOutput, calls=%fused_computation | convolution fusion | flops 8861253632 | bytes 16384000 | tf_op jit(solution)/shard_map/dot_general | solution.py:202
  411.4 9.5 %down_share.1 = (bf16[192,2048]{1,0:T(8,128)(2,1)}, bf16[192,2048]{1,0:T(8,128)(2,1)}, bf16[192,2048]{1,0:T(8,128)(2,1)}, bf16[192,2048]{1,0:T(8,128)(2,1)}, bf1...) custom-call(s32[2]{0:T(128)} %pad_add_fusion.1.me, ...), custom_call_target="tpu_custom_call" | custom-call | flops 1 | bytes 1 | tf_op jit(solution)/shard_map/down_share/pallas_call | solution.py:216
  451.9 8.5 %out_back.1 = bf16[8,192,512]{2,1,0:T(8,128)(2,1)} custom-call(s32[2]{0:T(128)} %pad_add_fusion.1.me, bf16[1024,2048]{1,0:T(8,128)(2,1)} %all-gather.8.cloned.1.call-done.out_rows, bf16[192,2048]{1,0:T(8,128)(2,1)} %copy-done.29, bf16[192,2048]{1,0:T(8,128)(2,1)} %collective-permute-done.56.refs_1_, bf16[192,2048]{1,0:T(8,128)(2,1)} %collective-permute-done.57.refs_2_, ...), custom_call_target="tpu_custom_call" | custom-call | flops 1 | bytes 1 | tf_op jit(solution)/shard_map/out_back/pallas_call | solution.py:216
  467.2 17.7 %all-to-all-done.2.grad = bf16[8,192,512]{2,1,0:T(8,128)(2,1)S(1)} async-done(((bf16[8,192,512]{2,1,0:T(8,128)(2,1)}), bf16[8,192,512]{2,1,0:T(8,128)(2,1)S(1)}, u32[]{:S(2)}, u32[]{:S(2)}) %all-to-all-start.2) | async-done | bytes 1572896 | tf_op jit(solution)/shard_map/all_to_all | solution.py:169
  492.7 18.4 %attend_back.1 = (bf16[192,4096]{1,0:T(8,128)(2,1)}, bf16[1536,512]{1,0:T(8,128)(2,1)}) custom-call(s32[16]{0:T(128)} %pad_add_fusion.2.table, s32[16]{0:T(128)} %bitcast.34, s32[2]{0:T(128)} %fusion.29.here, bf16[192,4096]{1,0:T(8,128)(2,1)} %get-tuple-element.235.q_in, bf16[8,192,512]{2,1,0:T(8,128)(2,1)} %copy-done.8, ...), custom_call_target="tpu_custom_call" | custom-call | flops 1 | bytes 1 | tf_op jit(solution)/shard_map/attend_back/pallas_call | solution.py:216
  511.8 29.5 %reduce-scatter.9.cloned.1.call-done = bf16[512,1408]{1,0:T(8,128)(2,1)} async-done(((bf16[2048,1408]{1,0:T(8,128)(2,1)}), bf16[512,1408]{1,0:T(8,128)(2,1)}) %reduce-scatter.9.cloned.1.call-update) | async-done | bytes 1441808 | tf_op jit(solution)/shard_map/reduce_scatter | solution.py:132
  541.6 13.8 %up_back.1 = (bf16[128,4224]{1,0:T(8,128)(2,1)}, bf16[128,4224]{1,0:T(8,128)(2,1)}, bf16[128,4224]{1,0:T(8,128)(2,1)}, bf16[128,4224]{1,0:T(8,128)(2,1)}, bf16[1...) custom-call(s32[2]{0:T(128)} %pad_add_fusion.1.me, ...), custom_call_target="tpu_custom_call" | custom-call | flops 1 | bytes 1 | tf_op jit(solution)/shard_map/up_back/pallas_call | solution.py:216
  580.3 33.2 %collective-permute-done.82 = bf16[128,4224]{1,0:T(8,128)(2,1)S(1)} collective-permute-done((bf16[128,4224]{1,0:T(8,128)(2,1)S(1)}, bf16[128,4224]{1,0:T(8,128)(2,1)S(1)}, u32[]{:S(2)}, u32[]{:S(2)}) %collective-permute-start.82) | collective-permute-done | bytes 1081376 | tf_op jit(solution)/shard_map/ppermute | solution.py:46
  615.3 11.6 %project_back.1 = (bf16[256,1664]{1,0:T(8,128)(2,1)}, bf16[256,1664]{1,0:T(8,128)(2,1)}, bf16[256,1664]{1,0:T(8,128)(2,1)}, bf16[256,1664]{1,0:T(8,128)(2,1)}, b...) custom-call(s32[2]{0:T(128)} %pad_add_fusion.1.me, ...), custom_call_target="tpu_custom_call" | custom-call | flops 1 | bytes 1 | tf_op jit(solution)/shard_map/project_back/pallas_call | solution.py:216
  636.8 8.3 %collective-permute-done.84 = bf16[64,4224]{1,0:T(8,128)(2,1)S(1)} collective-permute-done((bf16[64,4224]{1,0:T(8,128)(2,1)S(1)}, bf16[64,4224]{1,0:T(8,128)(2,1)S(1)}, u32[]{:S(2)}, u32[]{:S(2)}) %collective-permute-start.84) | collective-permute-done | bytes 540704 | tf_op jit(solution)/shard_map/ppermute | solution.py:49
  649.0 16.5 %collective-permute-done.74 = bf16[256,1664]{1,0:T(8,128)(2,1)S(1)} collective-permute-done((bf16[256,1664]{1,0:T(8,128)(2,1)}, bf16[256,1664]{1,0:T(8,128)(2,1)S(1)}, u32[]{:S(2)}, u32[]{:S(2)}) %collective-permute-start.74) | collective-permute-done | bytes 852000 | tf_op jit(solution)/shard_map/ppermute | solution.py:46
  (509 shorter events, 274.7 us)
Async XLA Ops:
  7.2 56.3 %all-gather.6.cloned.1.call-start = ((), (), s32[]{:S(2)}) async-start(), calls=%async_computation.10 | async-start | bytes 1351680 | tf_op jit(solution)/shard_map/all_gather | solution.py:129
  9.7 89.6 %all-gather.8.cloned.1.call-start = ((), (), s32[]{:S(2)}) async-start(), calls=%async_computation.11 | async-start | bytes 4718592 | tf_op jit(solution)/shard_map/all_gather | solution.py:135
  10.4 161.7 %all-gather.10.cloned.1.call-start = ((), (), s32[]{:S(2)}) async-start(), calls=%async_computation.12 | async-start | bytes 1769472 | tf_op jit(solution)/shard_map/all_gather | solution.py:135
  47.8 30.6 %collective-permute-start.4 = (bf16[256,1664]{1,0:T(8,128)(2,1)S(1)}, bf16[256,1664]{1,0:T(8,128)(2,1)S(1)}, u32[]{:S(2)}, u32[]{:S(2)}) collective-permute-start(bf16[256,1664]{1,0:T(8,128)(2,1)S(1)} %all_gather.18.refs_0_), channel_id=1, source_target_pairs={{0,1},{1,0},{2,3},{3,2},{4,5},{5,4},{6,7},{7,6},{8,9},{9,8},{10,11... | collective-permute-start | bytes 2555912 | tf_op jit(solution)/shard_map/ppermute | solution.py:43
  99.3 204.9 %all-gather.14.cloned.1.call-start = ((), (), s32[]{:S(2)}) async-start(), calls=%async_computation.14 | async-start | bytes 6488064 | tf_op jit(solution)/shard_map/all_gather | solution.py:135
  104.4 46.1 %all-to-all-start = ((bf16[8,64,1408]{2,1,0:T(8,128)(2,1)}), bf16[8,64,1408]{2,1,0:T(8,128)(2,1)}, u32[]{:S(2)}, u32[]{:S(2)}) async-start(bf16[8,64,1408]{2,1,0:T(8,128)(2,1)} %maximum_bitcast_fusion), calls=%async_computation | async-start | bytes 2883584 | tf_op jit(solution)/shard_map/all_to_all | solution.py:169
  108.7 195.6 %all-gather.12.cloned.1.call-start = ((), (), s32[]{:S(2)}) async-start(), calls=%async_computation.13 | async-start | bytes 7208960 | tf_op jit(solution)/shard_map/all_gather | solution.py:129
  108.7 41.8 %collective-permute-start.9 = (bf16[128,4224]{1,0:T(8,128)(2,1)}, bf16[128,4224]{1,0:T(8,128)(2,1)S(1)}, u32[]{:S(2)}, u32[]{:S(2)}) collective-permute-start(bf16[128,4224]{1,0:T(8,128)(2,1)} %all-gather.6.cloned.1.call-done.refs_0_), channel_id=1, source_target_pairs={{0,8},{8,0},{16,24},{24,16},{1,9},{9,1},{17,25},{25,17},{2,10},{10... | collective-permute-start | bytes 3244040 | tf_op jit(solution)/shard_map/ppermute | solution.py:46
  110.6 39.9 %collective-permute-start.10 = (bf16[128,4224]{1,0:T(8,128)(2,1)}, bf16[128,4224]{1,0:T(8,128)(2,1)S(1)}, u32[]{:S(2)}, u32[]{:S(2)}) collective-permute-start(bf16[128,4224]{1,0:T(8,128)(2,1)} %all-gather.6.cloned.1.call-done.refs_0_), channel_id=1, source_target_pairs={{0,16},{16,0},{8,24},{24,8},{1,17},{17,1},{9,25},{25,9},{2,18},{18... | collective-permute-start | bytes 3244040 | tf_op jit(solution)/shard_map/ppermute | solution.py:49
  194.3 25.1 %all-to-all-start.1 = ((bf16[8,192,512]{2,1,0:T(8,128)(2,1)}), bf16[8,192,512]{2,1,0:T(8,128)(2,1)S(1)}, u32[]{:S(2)}, u32[]{:S(2)}) async-start(bf16[8,192,512]{2,1,0:T(8,128)(2,1)} %get-tuple-element.162), calls=%async_computation.1 | async-start | bytes 3145728 | tf_op jit(solution)/shard_map/all_to_all | solution.py:169
  197.9 240.2 %reduce-scatter.7.cloned.1.call-start = ((), (), s32[]{:S(2)}) async-start(), calls=%async_computation.15 | async-start | bytes 3604480 | tf_op jit(solution)/shard_map/reduce_scatter | solution.py:132
  199.0 29.0 %collective-permute-start.20 = (bf16[96,2048]{1,0:T(8,128)(2,1)S(1)}, bf16[96,2048]{1,0:T(8,128)(2,1)S(1)}, u32[]{:S(2)}, u32[]{:S(2)}) collective-permute-start(bf16[96,2048]{1,0:T(8,128)(2,1)S(1)} %slice.268), channel_id=1, source_target_pairs={{0,16},{16,0},{8,24},{24,8},{1,17},{17,1},{9,25},{25,9},{2,18},{18... | collective-permute-start | bytes 1179656 | tf_op jit(solution)/shard_map/ppermute | solution.py:49
  202.0 26.0 %collective-permute-start.21 = (bf16[96,2048]{1,0:T(8,128)(2,1)S(1)}, bf16[96,2048]{1,0:T(8,128)(2,1)}, u32[]{:S(2)}, u32[]{:S(2)}) collective-permute-start(bf16[96,2048]{1,0:T(8,128)(2,1)S(1)} %slice.269), channel_id=1, source_target_pairs={{0,8},{8,0},{16,24},{24,16},{1,9},{9,1},{17,25},{25,17},{2,10},{10... | collective-permute-start | bytes 1179656 | tf_op jit(solution)/shard_map/ppermute | solution.py:46
  381.5 159.8 %reduce-scatter.9.cloned.1.call-start = ((), (), s32[]{:S(2)}) async-start(), calls=%async_computation.16 | async-start | bytes 7208960 | tf_op jit(solution)/shard_map/reduce_scatter | solution.py:132
  464.0 151.3 %reduce-scatter.11.cloned.1.call-start = ((), (), s32[]{:S(2)}) async-start(), calls=%async_computation.17 | async-start | bytes 1769472 | tf_op jit(solution)/shard_map/reduce_scatter | solution.py:999
  541.3 124.2 %reduce-scatter.13.cloned.1.call-start = ((), (), s32[]{:S(2)}) async-start(), calls=%async_computation.18 | async-start | bytes 2621440 | tf_op jit(solution)/shard_map/reduce_scatter | solution.py:132
  557.8 123.6 %collective-permute-start.63 = (bf16[192,2048]{1,0:T(8,128)(2,1)}, bf16[192,2048]{1,0:T(8,128)(2,1)}, u32[]{:S(2)}, u32[]{:S(2)}) collective-permute-start(bf16[192,2048]{1,0:T(8,128)(2,1)} %get-tuple-element.228), channel_id=1, source_target_pairs={{0,1},{1,0},{2,3},{3,2},{4,5},{5,4},{6,7},{7,6},{8,9},{9,8},{10,11... | collective-permute-start | bytes 2359304 | tf_op jit(solution)/shard_map/ppermute | solution.py:43
  559.7 123.6 %collective-permute-start.69 = (bf16[96,2048]{1,0:T(8,128)(2,1)S(1)}, bf16[96,2048]{1,0:T(8,128)(2,1)}, u32[]{:S(2)}, u32[]{:S(2)}) collective-permute-start(bf16[96,2048]{1,0:T(8,128)(2,1)S(1)} %fusion.15), channel_id=1, source_target_pairs={{0,16},{16,0},{8,24},{24,8},{1,17},{17,1},{9,25},{25,9},{2,18},{18... | collective-permute-start | bytes 1179656 | tf_op jit(solution)/shard_map/ppermute | solution.py:49
  563.9 119.5 %collective-permute-start.70 = (bf16[96,2048]{1,0:T(8,128)(2,1)}, bf16[96,2048]{1,0:T(8,128)(2,1)}, u32[]{:S(2)}, u32[]{:S(2)}) collective-permute-start(bf16[96,2048]{1,0:T(8,128)(2,1)} %fusion.13), channel_id=1, source_target_pairs={{0,8},{8,0},{16,24},{24,16},{1,9},{9,1},{17,25},{25,17},{2,10},{10... | collective-permute-start | bytes 1179656 | tf_op jit(solution)/shard_map/ppermute | solution.py:46
  565.3 120.9 %all-to-all-start.3 = ((bf16[8,64,1408]{2,1,0:T(8,128)(2,1)}), bf16[8,64,1408]{2,1,0:T(8,128)(2,1)}, u32[]{:S(2)}, u32[]{:S(2)}) async-start(bf16[8,64,1408]{2,1,0:T(8,128)(2,1)} %bitcast.18), calls=%async_computation.9 | async-start | bytes 2883584 | tf_op jit(solution)/shard_map/all_to_all | solution.py:169
  569.6 124.7 %reduce-scatter.17.cloned.1.call-start = ((), (), s32[]{:S(2)}) async-start(), calls=%async_computation.20 | async-start | bytes 1351680 | tf_op jit(solution)/shard_map/reduce_scatter | solution.py:132
  575.1 38.4 %collective-permute-start.82 = (bf16[128,4224]{1,0:T(8,128)(2,1)S(1)}, bf16[128,4224]{1,0:T(8,128)(2,1)S(1)}, u32[]{:S(2)}, u32[]{:S(2)}) collective-permute-start(bf16[128,4224]{1,0:T(8,128)(2,1)S(1)} %pad_maximum_fusion.2), channel_id=1, source_target_pairs={{0,8},{8,0},{16,24},{24,16},{1,9},{9,1},{17,25},{25,17},{2,10},{10... | collective-permute-start | bytes 3244040 | tf_op jit(solution)/shard_map/ppermute | solution.py:46
  577.1 36.7 %collective-permute-start.85 = (bf16[128,4224]{1,0:T(8,128)(2,1)S(1)}, bf16[128,4224]{1,0:T(8,128)(2,1)S(1)}, u32[]{:S(2)}, u32[]{:S(2)}) collective-permute-start(bf16[128,4224]{1,0:T(8,128)(2,1)S(1)} %pad_maximum_fusion.3), channel_id=1, source_target_pairs={{0,16},{16,0},{8,24},{24,8},{1,17},{17,1},{9,25},{25,9},{2,18},{18... | collective-permute-start | bytes 3244040 | tf_op jit(solution)/shard_map/ppermute | solution.py:49
  648.8 57.2 %reduce-scatter.15.cloned.1.call-start = ((), (), s32[]{:S(2)}) async-start(), calls=%async_computation.19 | async-start | bytes 1064960 | tf_op jit(solution)/shard_map/reduce_scatter | solution.py:132
  (167 other events, 1522.5 us)
Sparse Core Ops, SparseCore 0:
  10.2 40.8 all-gather.5
  52.7 46.6 all-gather.7
  101.5 23.7 all-gather.9
  126.8 59.9 all-gather.13
  188.3 105.3 all-gather.11
  381.6 55.2 reduce-scatter.6
  439.1 102.0 reduce-scatter.8
  543.6 34.4 reduce-scatter.10
  580.4 42.3 reduce-scatter.12
  648.9 27.7 reduce-scatter.16
  681.5 24.4 reduce-scatter.14

commit v3 on v2

--- a/solution.py
+++ b/solution.py
@@ -134,15 +134,17 @@
     def rows_gather(self, w):
         return lax.all_gather(w, ("z", "c"), axis=0, tiled=True)
 
-    def rows_return(self, g):
+    def rows_parted(self, g):
         n = g.shape[1]
-        r = g.shape[0] // self.Z
         core = lax.axis_index("c")
-        parts = g.reshape(self.Z // 2, 2, r, n)
-        mine = lax.dynamic_slice_in_dim(parts, core, 1, 1).reshape(-1, n)
-        sent = lax.dynamic_slice_in_dim(parts, 1 - core, 1, 1).reshape(-1, n)
+        parts = g.reshape(self.Z // 2, 2, -1, n)
+        return [
+            lax.dynamic_slice_in_dim(parts, k, 1, 1).reshape(-1, n) for k in (core, 1 - core)
+        ]
+
+    def rows_return(self, mine, sent):
         came = self.swap_c(sent)
-        first = core == 0
+        first = lax.axis_index("c") == 0
         return jnp.concatenate(
             [jnp.where(first, mine, came), jnp.where(first, came, mine)], axis=0
         )
@@ -167,6 +169,23 @@
 
     def exchange(self, a):
         return lax.all_to_all(a, ("slot", "c"), 0, 0, tiled=True)
+
+    def exchange_pieces(self, pieces):
+        if self.S == 4:
+            ways = 2 * self.S
+            moved = [pieces[0]]
+            for number in range(1, ways):
+                step = 2 * (number % self.S) + number // self.S
+                moved.append(
+                    lax.ppermute(pieces[number], ("slot", "c"), [(i, i ^ step) for i in range(ways)])
+                )
+            return moved
+        first = lax.axis_index("c") == 0
+        same, other = jnp.stack(pieces[: self.S]), jnp.stack(pieces[self.S :])
+        pair = jnp.stack([jnp.where(first, same, other), jnp.where(first, other, same)], axis=1)
+        pair = self.exchange(pair.reshape(2 * self.S, *pieces[0].shape))
+        low, high = pair[0::2], pair[1::2]
+        return [*jnp.where(first, low, high), *jnp.where(first, high, low)]
 
 
 def tie(*arrays):
@@ -196,10 +215,6 @@
     freq = ROPE_BASE ** (-2.0 * jnp.arange(half, dtype=F32) / width)
     angle = position.astype(F32)[:, None] * freq[None, :]
     return (jnp.cos(angle), jnp.sin(angle))
-
-
-def contract_first(left, right):
-    return lax.dot_general(left, right, (((0,), (0,)), ((), ())), preferred_element_type=F32)
 
 
 def _call(kernel, name, out_shape, args, scratch=(), memory=None):
@@ -334,14 +349,23 @@
         sorted_kv[at, :] = kv[b * GROUP : (b + 1) * GROUP, :]
 
 
-def attend_kernel(net, count, table, order, here, me, low, cos, sin, kv, *refs):
-    pieces = refs[:count]
-    cqn_out, q_out, att_out, chunk_out, lse_out, up_q, sorted_kv, scores = refs[count:]
+def _key_blocks(net, me, order):
+    for side in range(2):
+        core = me[1] if side == 0 else 1 - me[1]
+        for k in range(2 * net.Z):
+            group = order[2 * (2 * (k // 2) + core) + k % 2]
+            at = pl.ds(pl.multiple_of(group * GROUP, GROUP), GROUP)
+            yield side, slice(k * GROUP, (k + 1) * GROUP), at
+
+
+def attend_kernel(net, count, table, order, here, me, low, gain, cos, sin, kv, *refs):
+    pieces, parts = refs[:count], refs[count : count + 2 * net.S]
+    cqn_out, q_out, att_out, lse_out, up_q, sorted_kv, scores, chunk_out = refs[
+        count + 2 * net.S :
+    ]
     _join(net, me, pieces, up_q)
     _sort_keys(order, kv, sorted_kv)
-    wide = H * HD
-    gain = jnp.transpose(up_q[:, wide:].astype(F32))[:1, :]
-    cqn_out[...] = (low[...] * _mean_scale(low[...]) * gain).astype(BF)
+    cqn_out[...] = (low[...] * _mean_scale(low[...]) * gain[...]).astype(BF)
     scale = 1.0 / math.sqrt(HD)
     half = HD // 2
     per_chunk = chunk_out.shape[2] // HD
@@ -394,27 +418,30 @@
                 att_out[rows, head * HD : (head + 1) * HD] = piece
                 lanes = slice((head % per_chunk) * HD, (head % per_chunk + 1) * HD)
                 chunk_out[head // per_chunk, rows, lanes] = piece.astype(BF)
-
-
-def attend(net, table, order, here, me, low, cos, sin, kv, pieces):
+    for number, part in enumerate(parts):
+        part[...] = chunk_out[_owner(net, me, number % net.S, number >= net.S)]
+
+
+def attend(net, table, order, here, me, low, gain, cos, sin, kv, pieces):
     tokens, low_rank = low.shape
     slot_rows = kv.shape[0]
     ways = 2 * net.S
     return _call(
         functools.partial(attend_kernel, net, len(pieces)),
         "attend",
-        (
+        [_shape(tokens, H * HD // ways)] * ways
+        + [
             _shape(tokens, low_rank),
             _shape(tokens, H * HD),
             _shape(tokens, H * HD, dtype=F32),
-            _shape(ways, tokens, H * HD // ways),
             _shape(2, H // HG, HG * GROUP, dtype=F32),
-        ),
-        [table, order, here, me, low, cos, sin, kv, *pieces],
+        ],
+        [table, order, here, me, low, gain, cos, sin, kv, *pieces],
         [
-            pltpu.VMEM((low_rank, pieces[0].shape[1]), BF),
+            pltpu.VMEM((low_rank, H * HD), BF),
             pltpu.VMEM((slot_rows, 2 * HD), BF),
             pltpu.VMEM((slot_rows, HG * GROUP), F32),
+            pltpu.VMEM((ways, tokens, H * HD // ways), BF),
         ],
     )
 
@@ -424,26 +451,25 @@
     return slot * 2 + (1 - me[1] if other else me[1])
 
 
-def out_kernel(net, me, heads, out_rows, *parts):
-    tokens, size = heads.shape[1:]
+def out_kernel(net, me, out_rows, *refs):
+    heads, parts = refs[: 2 * net.S], refs[2 * net.S :]
+    tokens, size = heads[0].shape
     weight = out_rows[pl.ds(pl.multiple_of(me[1] * size, size), size), :]
     for side in (1, 0):
-        for first in range(0, net.S, 2):
-            rows = jnp.concatenate(
-                [heads[_owner(net, me, first + k, side == 1)] for k in range(2)], axis=0
-            )
+        for first in range(side * net.S, (side + 1) * net.S, 2):
+            rows = jnp.concatenate([heads[first][...], heads[first + 1][...]], axis=0)
             got = jnp.dot(rows, weight, preferred_element_type=F32).astype(BF)
             for k in range(2):
-                parts[side * net.S + first + k][...] = got[k * tokens : (k + 1) * tokens, :]
+                parts[first + k][...] = got[k * tokens : (k + 1) * tokens, :]
 
 
 def out_forward(net, me, heads, out_rows):
-    tokens = heads.shape[1]
+    tokens = heads[0].shape[0]
     return _call(
         functools.partial(out_kernel, net),
         "out_forward",
         [_shape(tokens, out_rows.shape[1])] * (2 * net.S),
-        [me, heads, out_rows],
+        [me, out_rows, *heads],
     )
 
 
@@ -518,134 +544,234 @@
     return tiles
 
 
-def ffn_kernel(net, tiles, splits, me, *refs):
+def hidden_back_kernel(net, count, me, down_rows, *refs):
+    rows_in, (all_out, grad_out) = refs[:count], refs[count:]
+    wide = grad_out.shape[1]
+    weight = down_rows[pl.ds(pl.multiple_of(me[1] * wide, 16), wide), :]
+    at = 0
+    for ref in rows_in:
+        all_out[at : at + ref.shape[0], :] = ref[...]
+        at += ref.shape[0]
+    step = at // 4
+    for first in range(0, at, step):
+        rows = slice(first, first + step)
+        grad_out[rows, :] = _nt(all_out[rows, :], weight)
+
+
+def hidden_back(net, me, d, down_rows):
+    rows = sum(a.shape[0] for a in d)
+    return _call(
+        functools.partial(hidden_back_kernel, net, len(d)),
+        "hidden_back",
+        (
+            _shape(rows, down_rows.shape[1]),
+            _shape(rows, down_rows.shape[0] // 2, dtype=F32),
+        ),
+        [me, down_rows, *d],
+    )
+
+
+def _send(copies, source, target, sem):
+    copy = pltpu.make_async_copy(source, target, sem)
+    copy.start()
+    copies.append(copy)
+
+
+def ffn_forward_kernel(tiles, *refs):
     count = len({k for tile in tiles for k, _, _ in tile})
-    results = len({k for tile in splits for k, _, _ in tile})
-    h, d = refs[:count], refs[count : 2 * count]
-    gu_w, down_rows = refs[2 * count : 2 * count + 2]
-    outs = refs[2 * count + 2 : 2 * count + 2 + results]
-    h_out, d_out, hid_out, dgu_out = refs[2 * count + 2 + results : 2 * count + 6 + results]
-    hv, dv, gv, wv, xv, hidv, dguv, sem_in, sem_out = refs[2 * count + 6 + results :]
+    h, gu_w = refs[:count], refs[count]
+    h_out, hid_out, slope_out, hv, gv, hidv, slopev, sem_in, sem_out = refs[count + 1 :]
     wide = hid_out.shape[1]
     size = hv.shape[1]
-
-    def fetch(t, sources, target, sem):
-        copies, at = [], 0
-        for n, (k, first, rows) in enumerate(tiles[t]):
-            copies.append(
-                pltpu.make_async_copy(
-                    sources[k].at[pl.ds(first, rows)], target.at[t, pl.ds(at, rows)], sem.at[n]
-                )
+    gu_copy = pltpu.make_async_copy(gu_w, gv, sem_in.at[len(tiles), 0])
+    copies = []
+    for t, tile in enumerate(tiles):
+        at = 0
+        copies.append([])
+        for n, (k, first, rows) in enumerate(tile):
+            _send(
+                copies[t], h[k].at[pl.ds(first, rows)], hv.at[t, pl.ds(at, rows)], sem_in.at[t, n]
             )
             at += rows
-        return copies
-
-    gu_copy = pltpu.make_async_copy(gu_w, gv, sem_in.at[0, 0, 0])
-    down_copy = pltpu.make_async_copy(
-        down_rows.at[pl.ds(pl.multiple_of(me[1] * wide, 16), wide)], wv, sem_in.at[0, 0, 1]
-    )
-    h_copies = [fetch(t, h, hv, sem_in.at[1, t]) for t in range(len(tiles))]
-    d_copies = [fetch(t, d, dv, sem_in.at[2, t]) for t in range(len(tiles))]
-    for c in d_copies[0] + [down_copy] + h_copies[0] + [gu_copy]:
-        c.start()
-    for t in range(1, len(tiles)):
-        for c in d_copies[t] + h_copies[t]:
-            c.start()
+        if t == 0:
+            gu_copy.start()
     sent = []
-
-    def send(source, target, sem):
-        copy = pltpu.make_async_copy(source, target, sem)
-        copy.start()
-        sent.append(copy)
-
     for t in range(len(tiles)):
         rows = pl.ds(t * size, size)
-        for c in d_copies[t] + ([down_copy] if t == 0 else []):
+        for c in copies[t] + ([gu_copy] if t == 0 else []):
             c.wait()
-        send(dv.at[t], d_out.at[rows], sem_out.at[t, 0])
-        grad = _nt(dv[t], wv[...])
-        for c in h_copies[t] + ([gu_copy] if t == 0 else []):
-            c.wait()
-        send(hv.at[t], h_out.at[rows], sem_out.at[t, 1])
+        _send(sent, hv.at[t], h_out.at[rows], sem_out.at[t, 0])
         both = jnp.dot(hv[t], gv[...], preferred_element_type=F32)
         gate = both[:, :wide]
         up = both[:, wide:]
         sigma = jax.nn.sigmoid(gate)
         silu = gate * sigma
         hidv[t] = (silu * up).astype(BF)
-        send(hidv.at[t], hid_out.at[rows], sem_out.at[t, 2])
-        dguv[t] = jnp.concatenate(
-            [grad * up * sigma * (1.0 + gate * (1.0 - sigma)), grad * silu], axis=1
+        _send(sent, hidv.at[t], hid_out.at[rows], sem_out.at[t, 1])
+        slopev[t] = jnp.concatenate(
+            [up * sigma * (1.0 + gate * (1.0 - sigma)), silu], axis=1
         ).astype(BF)
-        send(dguv.at[t], dgu_out.at[rows], sem_out.at[t, 3])
-        xv[t] = _nt(dguv[t], gv[...]).astype(BF)
-        at = 0
-        for n, (k, first, take) in enumerate(splits[t]):
-            send(xv.at[t, pl.ds(at, take)], outs[k].at[pl.ds(first, take)], sem_out.at[t, 4 + n])
-            at += take
+        _send(sent, slopev.at[t], slope_out.at[rows], sem_out.at[t, 2])
     for copy in sent:
         copy.wait()
 
 
-def ffn(net, me, h, d, gu_w, down_rows, tokens):
+def ffn_forward(h, gu_w, tokens):
     width = gu_w.shape[0]
     wide = gu_w.shape[1] // 2
     size = 2 * tokens
     tiles = _tiles([a.shape[0] for a in h], size)
-    out_rows = [tokens] * (2 * net.S)
-    splits = _tiles(out_rows, size)
     steps = len(tiles)
-    every = steps * size
-    return _call(
-        functools.partial(ffn_kernel, net, tiles, splits),
-        "ffn",
-        [_shape(n, width) for n in out_rows]
-        + [_shape(every, n) for n in (width, width, wide, 2 * wide)],
-        [me, *h, *d, gu_w, down_rows],
+    return _call(
+        functools.partial(ffn_forward_kernel, tiles),
+        "ffn_forward",
+        [_shape(steps * size, n) for n in (width, wide, 2 * wide)],
+        [*h, gu_w],
         [
             pltpu.VMEM((steps, size, width), BF),
-            pltpu.VMEM((steps, size, width), BF),
             pltpu.VMEM((width, 2 * wide), BF),
-            pltpu.VMEM((wide, width), BF),
-            pltpu.VMEM((steps, size, width), BF),
             pltpu.VMEM((steps, size, wide), BF),
             pltpu.VMEM((steps, size, 2 * wide), BF),
-            pltpu.SemaphoreType.DMA((3, steps, 5)),
-            pltpu.SemaphoreType.DMA((steps, 8)),
+            pltpu.SemaphoreType.DMA((steps + 1, 5)),
+            pltpu.SemaphoreType.DMA((steps, 3)),
         ],
         memory=pl.ANY,
     )
 
 
+def down_grad_kernel(net, me, hidden, rows, mine, sent, grad):
+    wide = hidden.shape[1]
+    step = 512
+    for first in range(0, rows.shape[1], step):
+        grad[:, first : first + step] = _tn(hidden[...], rows[:, first : first + step]).astype(BF)
+    r = wide // net.Z
+    for k in range(net.Z // 2):
+        low = grad[2 * k * r : (2 * k + 1) * r, :]
+        high = grad[(2 * k + 1) * r : (2 * k + 2) * r, :]
+        here = slice(k * r, (k + 1) * r)
+        mine[here, :] = jnp.where(me[1] == 0, low, high)
+        sent[here, :] = jnp.where(me[1] == 0, high, low)
+
+
+def down_grad(net, me, hidden, rows):
+    half = _shape(hidden.shape[1] // 2, rows.shape[1])
+    return _call(
+        functools.partial(down_grad_kernel, net),
+        "down_grad",
+        (half, half),
+        [me, hidden, rows],
+        [pltpu.VMEM((hidden.shape[1], rows.shape[1]), BF)],
+    )
+
+
+def gu_grad_kernel(rows, grad, out):
+    out[...] = _tn(rows[...], grad[...]).astype(BF)
+
+
+def gu_weight_grad(rows, grad):
+    count, width = rows.shape
+    wide = grad.shape[1]
+    size = 512
+    return pl.pallas_call(
+        gu_grad_kernel,
+        grid=(width // size,),
+        out_shape=_shape(width, wide),
+        in_specs=[
+            pl.BlockSpec((count, size), lambda i: (0, i)),
+            pl.BlockSpec((count, wide), lambda i: (0, 0)),
+        ],
+        out_specs=pl.BlockSpec((size, wide), lambda i: (i, 0)),
+        compiler_params=pltpu.CompilerParams(vmem_limit_bytes=VMEM_BYTES),
+        cost_estimate=pl.CostEstimate(flops=1, bytes_accessed=1, transcendentals=0),
+        name="gu_weight_grad",
+    )(rows, grad)
+
+
+def ffn_back_kernel(splits, grad, slope, gu_w, *refs):
+    results = len({k for tile in splits for k, _, _ in tile})
+    outs = refs[:results]
+    dgu_out, gradv, slopev, gv, dguv, xv, sem_in, sem_out = refs[results:]
+    size, wide = gradv.shape[1:]
+    gu_copy = pltpu.make_async_copy(gu_w, gv, sem_in.at[len(splits), 0])
+    copies = []
+    for t in range(len(splits)):
+        rows = pl.ds(t * size, size)
+        copies.append([])
+        _send(copies[t], grad.at[rows], gradv.at[t], sem_in.at[t, 0])
+        _send(copies[t], slope.at[rows], slopev.at[t], sem_in.at[t, 1])
+        if t == 0:
+            gu_copy.start()
+    sent = []
+    for t, split in enumerate(splits):
+        for c in copies[t]:
+            c.wait()
+        up = gradv[t]
+        dguv[t] = (jnp.concatenate([up, up], axis=1) * slopev[t].astype(F32)).astype(BF)
+        _send(sent, dguv.at[t], dgu_out.at[pl.ds(t * size, size)], sem_out.at[t, 0])
+        if t == 0:
+            gu_copy.wait()
+        xv[t] = _nt(dguv[t], gv[...]).astype(BF)
+        at = 0
+        for n, (k, first, take) in enumerate(split):
+            _send(sent, xv.at[t, pl.ds(at, take)], outs[k].at[pl.ds(first, take)], sem_out.at[t, 1 + n])
+            at += take
+    for copy in sent:
+        copy.wait()
+
+
+def ffn_back(net, grad, slope, gu_w, tokens):
+    width = gu_w.shape[0]
+    rows, wide = grad.shape
+    size = 2 * tokens
+    splits = _tiles([tokens] * (2 * net.S), size)
+    steps = len(splits)
+    return _call(
+        functools.partial(ffn_back_kernel, splits),
+        "ffn_back",
+        [_shape(tokens, width)] * (2 * net.S) + [_shape(rows, 2 * wide)],
+        [grad, slope, gu_w],
+        [
+            pltpu.VMEM((steps, size, wide), F32),
+            pltpu.VMEM((steps, size, 2 * wide), BF),
+            pltpu.VMEM((width, 2 * wide), BF),
+            pltpu.VMEM((steps, size, 2 * wide), BF),
+            pltpu.VMEM((steps, size, width), BF),
+            pltpu.SemaphoreType.DMA((steps + 1, 2)),
+            pltpu.SemaphoreType.DMA((steps, 6)),
+        ],
+        memory=pl.ANY,
+    )
+
+
 def out_back_kernel(net, count, me, out_rows, *refs):
-    rows_in, (heads_out,) = refs[:count], refs[count:]
-    ways, tokens, size = heads_out.shape
+    rows_in, parts = refs[:count], refs[count:]
+    tokens, size = parts[0].shape
     weight = out_rows[pl.ds(pl.multiple_of(me[1] * size, size), size), :]
     group = count // 2
     for side in range(2):
         rows = jnp.concatenate([ref[...] for ref in rows_in[side * group : (side + 1) * group]], axis=0)
         got = _nt(rows, weight).astype(BF)
         for place in range(net.S):
-            heads_out[_owner(net, me, place, side == 0)] = got[place * tokens : (place + 1) * tokens, :]
+            part = parts[(1 - side) * net.S + place]
+            part[...] = got[place * tokens : (place + 1) * tokens, :]
 
 
 def out_back(net, me, out_rows, rows, tokens):
-    ways = 2 * net.S
     return _call(
         functools.partial(out_back_kernel, net, len(rows)),
         "out_back",
-        _shape(ways, tokens, out_rows.shape[0] // 2),
+        [_shape(tokens, out_rows.shape[0] // 2)] * (2 * net.S),
         [me, out_rows, *rows],
     )
 
 
-def out_grad_kernel(net, count, me, heads, *refs):
-    rows_in, (grad_out,) = refs[:count], refs[count:]
+def out_grad_kernel(net, count, *refs):
+    heads, rows_in, grad_out = refs[: 2 * net.S], refs[2 * net.S : -1], refs[-1]
     group = count // 2
     total = None
     for side in range(2):
         left = jnp.concatenate(
-            [heads[_owner(net, me, place, side == 0)] for place in range(net.S)], axis=0
+            [ref[...] for ref in heads[(1 - side) * net.S : (2 - side) * net.S]], axis=0
         )
         right = jnp.concatenate([ref[...] for ref in rows_in[side * group : (side + 1) * group]], axis=0)
         part = _tn(left, right)
@@ -653,16 +779,20 @@
     grad_out[...] = total.astype(BF)
 
 
-def out_weight_grad(net, me, heads, rows):
+def out_weight_grad(net, heads, rows):
     return _call(
         functools.partial(out_grad_kernel, net, len(rows)),
         "out_weight_grad",
-        _shape(heads.shape[2], rows[0].shape[1]),
-        [me, heads, *rows],
-    )
-
-
-def back_kernel(table, order, here, q_in, grad, att, lse, cos, sin, kv, dq_out, dkv_out, sorted_kv, dk, dv):
+        _shape(heads[0].shape[1], rows[0].shape[1]),
+        [*heads, *rows],
+    )
+
+
+def back_kernel(net, table, order, here, me, q_in, att, lse, cos, sin, kv, *refs):
+    parts = refs[: 2 * net.S]
+    dq_out, dkv_same, dkv_other, sorted_kv, dk, dv, grad = refs[2 * net.S :]
+    for number, part in enumerate(parts):
+        grad[_owner(net, me, number % net.S, number >= net.S)] = part[...]
     _sort_keys(order, kv, sorted_kv)
     dk[...] = jnp.zeros_like(dk)
     dv[...] = jnp.zeros_like(dv)
@@ -719,34 +849,36 @@
                 dq_out[rows, head * HD + half : (head + 1) * HD] = (
                     b * cosine - a * sine
                 ).astype(BF)
-    for b in range(kv.shape[0] // GROUP):
-        at = pl.ds(pl.multiple_of(order[b] * GROUP, GROUP), GROUP)
-        dkv_out[b * GROUP : (b + 1) * GROUP, :HD] = dk[at, :].astype(BF)
-        dkv_out[b * GROUP : (b + 1) * GROUP, HD:] = dv[at, :].astype(BF)
-
-
-def attend_back(table, order, here, q, grad, att, lse, cos, sin, kv):
+    for side, rows, at in _key_blocks(net, me, order):
+        target = (dkv_same, dkv_other)[side]
+        target[rows, :HD] = dk[at, :].astype(BF)
+        target[rows, HD:] = dv[at, :].astype(BF)
+
+
+def attend_back(net, table, order, here, me, q, grads, att, lse, cos, sin, kv):
     slot_rows = kv.shape[0]
-    return _call(
-        back_kernel,
+    half = _shape(slot_rows // 2, 2 * HD)
+    return _call(
+        functools.partial(back_kernel, net),
         "attend_back",
-        (_shape(*q.shape), _shape(slot_rows, 2 * HD)),
-        [table, order, here, q, grad, att, lse, cos, sin, kv],
+        (_shape(*q.shape), half, half),
+        [table, order, here, me, q, att, lse, cos, sin, kv, *grads],
         [
             pltpu.VMEM((slot_rows, 2 * HD), BF),
             pltpu.VMEM((slot_rows, HD), F32),
             pltpu.VMEM((slot_rows, HD), F32),
+            pltpu.VMEM((len(grads), *grads[0].shape), BF),
         ],
     )
 
 
-def up_back_kernel(net, count, results, me, dq, cqn, low_ref, *refs):
+def up_back_kernel(net, count, results, me, dq, cqn, low_ref, gain_ref, *refs):
     pieces, outs = refs[:count], refs[count : count + results]
     low_grad_out, up_q, grad = refs[count + results :]
     _join(net, me, pieces, up_q)
     wide = dq.shape[1]
-    gain = jnp.transpose(up_q[:, wide:].astype(F32))[:1, :]
-    upstream = _nt(dq[...], up_q[:, :wide])
+    gain = gain_ref[...]
+    upstream = _nt(dq[...], up_q[...])
     low = low_ref[...]
     scale = _mean_scale(low)
     gain_grad = jnp.sum(upstream * low * scale, axis=0, keepdims=True)
@@ -762,16 +894,16 @@
     _part(net, me, grad, outs)
 
 
-def up_back(net, me, dq, cqn, low, pieces):
+def up_back(net, me, dq, cqn, low, gain, pieces):
     tokens, low_rank = low.shape
-    wide = pieces[0].shape[1]
+    wide = H * HD + 128
     outs = _out_pieces(net, low_rank, wide)
     *parts, grad = _call(
         functools.partial(up_back_kernel, net, len(pieces), len(outs)),
         "up_back",
         outs + [_shape(tokens, low_rank)],
-        [me, dq, cqn, low, *pieces],
-        [pltpu.VMEM((low_rank, wide), BF), pltpu.VMEM((low_rank, wide), BF)],
+        [me, dq, cqn, low, gain, *pieces],
+        [pltpu.VMEM((low_rank, H * HD), BF), pltpu.VMEM((low_rank, wide), BF)],
     )
     return parts, grad
 
@@ -832,6 +964,29 @@
         [pltpu.VMEM((width, wide), BF), pltpu.VMEM((width, wide), BF)],
     )
     return parts, in_grad
+
+
+def finish_kernel(got, low_out, key_out, value_out, gains_out):
+    low_rank = low_out.shape[1]
+    low_out[...] = got[:, :low_rank].astype(F32)
+    key_out[...] = got[:, low_rank : low_rank + HD].astype(F32)
+    value_out[...] = got[:, low_rank + HD : low_rank + 2 * HD].astype(F32)
+    gains_out[...] = jnp.transpose(got[:, low_rank + 2 * HD :].astype(F32))[: gains_out.shape[0], :]
+
+
+def finish(got, low_rank):
+    rows = got.shape[0]
+    return _call(
+        finish_kernel,
+        "finish",
+        (
+            _shape(rows, low_rank, dtype=F32),
+            _shape(rows, HD, dtype=F32),
+            _shape(rows, HD, dtype=F32),
+            _shape(8, rows, dtype=F32),
+        ),
+        [got],
+    )
 
 
 def share_kernel(net, me, hidden, down_rows, *parts):
@@ -873,43 +1028,50 @@
     here = lax.dynamic_slice_in_dim(order, 2 * place, 2, 0)
     kept = {}
 
-    gains = column(attn_gain) + jnp.roll(column(ffn_gain), 1, axis=1)
-    first_z = net.z_gather(jnp.concatenate([wq_down, w_key, w_value, gains], axis=1))
-    up_z = net.z_gather(jnp.concatenate([wq_up, column(q_gain)], axis=1))
+    rows = wq_down.shape[0]
+    q_column = jnp.pad(column(q_gain), ((0, rows - q_gain.shape[0]), (0, 0)))
+    gains = (
+        column(attn_gain)
+        + jnp.roll(column(ffn_gain), 1, axis=1)
+        + jnp.roll(q_column, 2, axis=1)
+    )
+    up_z = net.z_gather(wq_up)
     out_rows = net.rows_gather(w_out)
     down_rows = net.rows_gather(w_down)
-
-    def first_one(*moved):
+    gu_mine = net.cols_exchange(w_gate, w_up)
+    first_z = net.z_gather(jnp.concatenate([wq_down, w_key, w_value, gains], axis=1))
+    first_z, gu_mine = tie(first_z, gu_mine)
+
+    def first_two(*moved):
         *moved, kept["up_z"] = tie(*moved, up_z)
         return moved
 
-    first_pieces = net.weight_pieces(net.spread(first_z, (first_one,)))
-
-    w_gate, w_up, *_ = tie(w_gate, w_up, *first_pieces)
-    gu_mine = net.cols_exchange(w_gate, w_up)
-
-    def up_one(*moved):
-        kept["gu_mine"], *moved = tie(gu_mine, *moved)
-        return moved
-
-    up_pieces = net.weight_pieces(net.spread(kept["up_z"], (up_one,)))
-
+    first_pieces = net.weight_pieces(net.spread(first_z, (None, first_two)))
     query_low, kv, gains = project(net, me, hidden_in, cosine, sine, first_pieces, low_rank)
     kv, out_rows = tie(kv, out_rows)
     both = net.rows_gather(kv)
-    gu_chunk = net.z_gather(kept["gu_mine"])
+
+    def up_two(*moved):
+        *moved, kept["both"] = tie(*moved, both)
+        return moved
+
+    up_z = kept["up_z"]
+    up_pieces = net.weight_pieces(net.spread(up_z, (None, up_two)))
+    both = kept["both"]
+    gain_q = gains[2:3].reshape(-1, rows)[:, : q_gain.shape[0]].reshape(1, low_rank)
     cot = (out_grad.astype(F32) * valid[:, None].astype(F32)).astype(BF)
     cot, *_ = tie(cot, *up_pieces)
 
     def cot_one(*moved):
         kept["attend"] = attend(
-            net, table, order, here, me, query_low, cosine, sine, both, up_pieces
+            net, table, order, here, me, query_low, gain_q, cosine, sine, both, up_pieces
         )
-        *kept["attend"], a, b = tie(*kept["attend"], *moved, *moved[: 2 - len(moved)])
-        return [a, b][: len(moved)]
+        count = len(moved)
+        *kept["attend"], a, b = tie(*kept["attend"], *moved, *moved[: 2 - count])
+        return [a, b][:count]
 
     def cot_two(*moved):
-        heads = net.exchange(kept["attend"][3])
+        heads = net.exchange_pieces(kept["attend"][: 2 * net.S])
         parts = out_forward(net, me, heads, out_rows)
         kept["heads"] = heads
         done = tie(*moved, *parts)
@@ -918,7 +1080,8 @@
 
     cot_same = net.spread(cot, (cot_one, cot_two))
     cot_other = net.swap_all(cot_same)
-    query_normed, query_rows, attended, _, log_total = kept["attend"]
+    gu_chunk = net.z_gather(gu_mine)
+    query_normed, query_rows, attended, log_total = kept["attend"][2 * net.S :]
     heads = kept["heads"]
     out_parts = kept["out_parts"]
     middle, normed_two = middle_forward(
@@ -927,24 +1090,27 @@
 
     two_same = net.spread(normed_two)
     two_all = [*net.swap_all(two_same), *two_same]
-    cot_all = [*cot_other, *cot_same]
-    *back_parts, two_rows, cot_rows, hidden, gu_grad = ffn(
-        net, me, two_all, cot_all, gu_chunk, down_rows, tokens
-    )
+    cot_rows, hidden_grad = hidden_back(net, me, [*cot_other, *cot_same], down_rows)
+    gu_chunk, hidden_grad, cot_rows, *two_all = tie(gu_chunk, hidden_grad, cot_rows, *two_all)
+    two_rows, hidden, slopes = ffn_forward(two_all, gu_chunk, tokens)
+    *back_parts, gu_grad = ffn_back(net, hidden_grad, slopes, gu_chunk, tokens)
 
     def back_one(*came):
         *_, kept["hidden"], kept["gu_grad"] = tie(*came, hidden, gu_grad)
-        kept["grad_down"] = net.rows_return(contract_first(kept["hidden"], cot_rows).astype(BF))
+        kept["grad_down"] = net.rows_return(*down_grad(net, me, kept["hidden"], cot_rows))
         return came
 
     def back_two(*moved):
-        *moved, kept["grad_down"] = tie(*moved, kept["grad_down"])
+        *moved, _ = tie(*moved, kept["grad_down"])
         gu_grad, *_ = tie(kept["gu_grad"], *moved)
-        kept["grad_gu"] = contract_first(two_rows, gu_grad).astype(BF)
+        kept["grad_gu"] = lax.dot_general(
+            two_rows, gu_grad, (((0,), (0,)), ((), ())), preferred_element_type=F32
+        ).astype(BF)
         return moved
 
     def back_three(*moved):
-        *moved, kept["grad_gu"] = tie(*moved, kept["grad_gu"])
+        down = net.z_scatter(kept["grad_down"])
+        *moved, kept["grad_gu"], kept["down"] = tie(*moved, kept["grad_gu"], down)
         return moved
 
     middle_grad, middle_low, middle_gain = middle_back(
@@ -956,7 +1122,6 @@
             back_parts[net.S :], back_parts[: net.S], (back_one, back_two, back_three)
         ),
     )
-    grad_down = net.z_scatter(kept["grad_down"])
     grad_gu = net.z_scatter(kept["grad_gu"])
 
     def middle_one(*moved):
@@ -966,25 +1131,21 @@
         kept["shares"] = done[len(moved) :]
         return done[: len(moved)]
 
-    def middle_two(*moved):
-        *moved, kept["grad_down"] = tie(*moved, grad_down)
-        return moved
-
-    middle_same = net.spread(middle_low, (middle_one, middle_two))
-    grad_down = kept["grad_down"].astype(F32)
+    middle_same = net.spread(middle_low, (middle_one,))
     middle_all = [*net.swap_all(middle_same), *middle_same]
-    heads_grad = net.exchange(out_back(net, me, out_rows, middle_all, tokens))
-    grad_out = net.rows_return(out_weight_grad(net, me, heads, middle_all))
-    heads_grad, grad_out, *shares = tie(heads_grad, grad_out, *kept["shares"])
-    grad_out = net.z_scatter(grad_out)
+    heads_grad = net.exchange_pieces(out_back(net, me, out_rows, middle_all, tokens))
+    grad_out = net.rows_return(*net.rows_parted(out_weight_grad(net, heads, middle_all)))
+    count = 2 * net.S
+    done = tie(*heads_grad, *kept["shares"], grad_out)
+    heads_grad, shares, grad_out = done[:count], done[count:-1], done[-1]
 
     def result_two(*moved):
         backs = attend_back(
-            table, order, here, query_rows, heads_grad, attended, log_total, cosine, sine, both
+            net, table, order, here, me, query_rows, heads_grad, attended, log_total, cosine,
+            sine, both,
         )
-        *moved, kept["query_pre"], kept["both_grads"], kept["grad_gu"] = tie(
-            *moved, *backs, grad_gu
-        )
+        *moved, kept["query_pre"], same, other, kept["grad_gu"] = tie(*moved, *backs, grad_gu)
+        kept["both_grads"] = same.astype(F32) + net.swap_c(other).astype(F32)
         return moved
 
     upper, upper_last, lower, lower_last = net.collect(
@@ -996,8 +1157,13 @@
             [upper + upper_last.astype(F32), lower + lower_last.astype(F32)], axis=0
         )
     ).astype(BF)
-    both_sum = lax.psum_scatter(kept["both_grads"], ("z", "c"), scatter_dimension=0, tiled=True)
-    up_parts, low_grad = up_back(net, me, kept["query_pre"], query_normed, query_low, up_pieces)
+    both_sum = net.z_scatter(kept["both_grads"])
+    up_parts, low_grad = up_back(
+        net, me, kept["query_pre"], query_normed, query_low, gain_q, up_pieces
+    )
+
+    grad_out = net.z_scatter(grad_out)
+    grad_down = kept["down"].astype(F32)
 
     def whole(parts):
         upper, upper_last, lower, lower_last = parts
@@ -1005,32 +1171,45 @@
             jnp.concatenate(
                 [upper + upper_last.astype(F32), lower + lower_last.astype(F32)], axis=0
             )
-        ).astype(F32)
-
-    up_out = whole(net.collect(*net.weight_sides(up_parts)))
-    first_parts, in_grad = project_back(
-        net, me, hidden_in, low_grad, both_sum, cosine, sine, middle_grad, gains, middle_gain,
-        first_pieces,
-    )
+        )
+
+    both_sum, *up_parts = tie(both_sum, *up_parts)
+    def up_one(*came):
+        *came, kept["both_sum"] = tie(*came, both_sum)
+        return came
+
+    def up_two(*moved):
+        first_parts, kept["in_grad"] = project_back(
+            net, me, hidden_in, low_grad, kept["both_sum"], cosine, sine, middle_grad, gains,
+            middle_gain, first_pieces,
+        )
+        done = tie(*moved, *first_parts)
+        kept["first_parts"] = done[len(moved) :]
+        return done[: len(moved)]
+
+    up_out = whole(net.collect(*net.weight_sides(up_parts), (up_one, up_two)))
 
     def first_two(*moved):
-        *moved, kept["grad_out"] = tie(*moved, grad_out)
+        *moved, kept["grad_out"], kept["grad_gu"] = tie(*moved, grad_out, kept["grad_gu"])
         return moved
 
-    first_out = whole(net.collect(*net.weight_sides(first_parts), (None, first_two)))
+    first_out = whole(
+        net.collect(*net.weight_sides(kept["first_parts"]), (None, first_two))
+    )
     grad_out = kept["grad_out"].astype(F32)
     grad_gate, grad_upward = net.cols_return(kept["grad_gu"])
+    grad_low, grad_key, grad_value, grad_gains = finish(first_out, low_rank)
     return (
         layer_out,
-        in_grad,
-        first_out[:, last],
-        first_out[:, :low_rank],
-        up_out[:, H * HD],
-        up_out[:, : H * HD],
-        first_out[:, low_rank : low_rank + HD],
-        first_out[:, low_rank + HD : last],
+        kept["in_grad"],
+        grad_gains[0],
+        grad_low,
+        up_out[:, H * HD].astype(F32),
+        up_out[:, : H * HD].astype(F32),
+        grad_key,
+        grad_value,
         grad_out,
-        first_out[:, last + 1],
+        grad_gains[1],
         grad_gate,
         grad_upward,
         grad_down,

time: 727 us -> 689 us (0.948)
  waiting for transfers between devices: 326 us -> 277 us
  Pallas kernels: 149 us -> 170 us
  starting transfers between devices: 71.1 us -> 80 us
  matrix products: 22 us -> 14 us
  local copies, waits for them, and re-layouts: 39.4 us -> 32.1 us
    ppermute x0 -> x14, waiting for transfers between devices: none -> 32.6 us  [exchange_pieces(): lax.ppermute(pieces[number], ('slot', 'c'), [(i, i ^ step) for i in range...]
    ppermute x20, waiting for transfers between devices: 149 us -> 118 us  [swap_x(): return lax.ppermute(a, 'slot', [(0, 1), (1, 0), (2, 3), (3, 2)])]
    all_to_all x4 -> x2, waiting for transfers between devices: 33.6 us -> 5.15 us  [exchange(): return lax.all_to_all(a, ('slot', 'c'), 0, 0, tiled=True)]
    pallas_call x12 -> x16, Pallas kernels: 149 us -> 170 us  [_call(): pl.pallas_call(kernel, out_shape=out_shape, in_specs=specs, out_specs=out...]
    reduce_scatter x5 -> x6, waiting for transfers between devices: 37.7 us -> 21.8 us  [z_scatter(): return lax.psum_scatter(g.astype(BF), 'z', scatter_dimension=0, tiled=True)]
    ppermute x20, waiting for transfers between devices: 80.4 us -> 69.4 us  [swap_y(): return lax.ppermute(a, 'slot', [(0, 2), (2, 0), (1, 3), (3, 1)])]
    ppermute x0 -> x14, starting transfers between devices: none -> 10.3 us  [exchange_pieces(): lax.ppermute(pieces[number], ('slot', 'c'), [(i, i ^ step) for i in range...]
    ppermute x47 -> x48, waiting for transfers between devices: 12.2 us -> 21.4 us  [swap_c(): return lax.ppermute(a, 'c', [(0, 1), (1, 0)])]
  transfers between devices with their start and end apart: 102 -> 115, of which waited for: 45 -> 58; matrix products, arithmetic and copies ran while one was open for 13% -> 13% of each run, Pallas kernels for 16% -> 19%
where the time goes in v3:
time: 689 us; the launch traced here: 679 us
  waiting for transfers between devices  277 us (40%)
  Pallas kernels  170 us (25%)
  starting transfers between devices  80 us (12%)
  other arithmetic  58.7 us (9%)
  blocking collectives  32.2 us (5%)
  local copies, waits for them, and re-layouts  32.1 us (5%)
  between operations  15.6 us (2%)
  matrix products  14 us (2%)
    pallas_call x16, Pallas kernels, _call(): pl.pallas_call(kernel, out_shape=out_shape, in_specs=specs, out_specs=out...  170 us
    ppermute x20, waiting for transfers between devices, swap_x(): return lax.ppermute(a, 'slot', [(0, 1), (1, 0), (2, 3), (3, 2)])  118 us
    ppermute x20, waiting for transfers between devices, swap_y(): return lax.ppermute(a, 'slot', [(0, 2), (2, 0), (1, 3), (3, 1)])  69.4 us
    ppermute x14, waiting for transfers between devices, exchange_pieces(): lax.ppermute(pieces[number], ('slot', 'c'), [(i, i ^ step) for i in range...  32.6 us
    all_gather x1, blocking collectives, z_gather(): return lax.all_gather(w, 'z', axis=0, tiled=True)  32.2 us
    ppermute x20, starting transfers between devices, swap_x(): return lax.ppermute(a, 'slot', [(0, 1), (1, 0), (2, 3), (3, 2)])  25.8 us
    ppermute x20, starting transfers between devices, swap_y(): return lax.ppermute(a, 'slot', [(0, 2), (2, 0), (1, 3), (3, 1)])  23.5 us
    reduce_scatter x6, waiting for transfers between devices, z_scatter(): return lax.psum_scatter(g.astype(BF), 'z', scatter_dimension=0, tiled=True)  21.8 us
  transfers between devices with their start and end apart: 115, of which 58 were waited for; matrix products, arithmetic and copies ran while one was open for 13% of the time, Pallas kernels for 19%

profile of v3, /device:TPU:0, one launch (start us, length us, event | category | flops | bytes accessed | tf_op | source)
XLA Modules:
  0.0 679.2 jit_solution(14782569668965013203)
XLA Ops:
  19.1 32.2 %all_gather.18.refs_0_ = bf16[256,1664]{1,0:T(8,128)(2,1)S(1)} all-gather(bf16[64,1664]{1,0:T(8,128)(2,1)S(1)} %pad_maximum_fusion.14), channel_id=1, replica_groups=mesh['slot'=4,'z'=4,'c'=2] {'z'}, dimensions={0}, use_global_device_ids=true | all-gather | bytes 1064960 | tf_op jit(solution)/shard_map/all_gather | solution.py:129
  55.6 16.9 %collective-permute-done.refs_1_ = bf16[256,1664]{1,0:T(8,128)(2,1)S(1)} collective-permute-done((bf16[256,1664]{1,0:T(8,128)(2,1)S(1)}, bf16[256,1664]{1,0:T(8,128)(2,1)S(1)}, u32[]{:S(2)}, u32[]{:S(2)}) %collective-permute-start) | collective-permute-done | bytes 852000 | tf_op jit(solution)/shard_map/ppermute | solution.py:46
  105.9 22.6 %collective-permute-done.9.refs_1_ = bf16[128,4096]{1,0:T(8,128)(2,1)S(1)} collective-permute-done((bf16[128,4096]{1,0:T(8,128)(2,1)}, bf16[128,4096]{1,0:T(8,128)(2,1)S(1)}, u32[]{:S(2)}, u32[]{:S(2)}) %collective-permute-start.9) | collective-permute-done | bytes 1048608 | tf_op jit(solution)/shard_map/ppermute | solution.py:46
  132.1 9.7 %collective-permute-done.10.refs_3_ = bf16[64,4096]{1,0:T(8,128)(2,1)S(1)} collective-permute-done((bf16[64,4096]{1,0:T(8,128)(2,1)S(1)}, bf16[64,4096]{1,0:T(8,128)(2,1)S(1)}, u32[]{:S(2)}, u32[]{:S(2)}) %collective-permute-start.10) | collective-permute-done | bytes 524320 | tf_op jit(solution)/shard_map/ppermute | solution.py:49
  151.1 20.9 %attend.1 = (bf16[192,512]{1,0:T(8,128)(2,1)}, bf16[192,512]{1,0:T(8,128)(2,1)}, bf16[192,512]{1,0:T(8,128)(2,1)}, bf16[192,512]{1,0:T(8,128)(2,1)}, bf16[192,51...) custom-call(s32[16]{0:T(128)} %pad_add_fusion.1.table, ...), custom_call_target="tpu_custom_call" | custom-call | flops 1 | bytes 1 | tf_op jit(solution)/shard_map/attend/pallas_call | solution.py:231
  216.8 16.5 %collective-permute-done.35 = bf16[192,2048]{1,0:T(8,128)(2,1)S(1)} collective-permute-done((bf16[192,2048]{1,0:T(8,128)(2,1)S(1)}, bf16[192,2048]{1,0:T(8,128)(2,1)S(1)}, u32[]{:S(2)}, u32[]{:S(2)}) %collective-permute-start.35) | collective-permute-done | bytes 786464 | tf_op jit(solution)/shard_map/ppermute | solution.py:49
  238.8 8.3 %collective-permute-done.34.left_last = bf16[96,2048]{1,0:T(8,128)(2,1)S(1)} collective-permute-done((bf16[96,2048]{1,0:T(8,128)(2,1)S(1)}, bf16[96,2048]{1,0:T(8,128)(2,1)S(1)}, u32[]{:S(2)}, u32[]{:S(2)}) %collective-permute-start.34) | collective-permute-done | bytes 393248 | tf_op jit(solution)/shard_map/ppermute | solution.py:49
  254.4 15.7 %collective-permute-done.43.refs_6_ = bf16[192,2048]{1,0:T(8,128)(2,1)S(1)} collective-permute-done((bf16[192,2048]{1,0:T(8,128)(2,1)}, bf16[192,2048]{1,0:T(8,128)(2,1)S(1)}, u32[]{:S(2)}, u32[]{:S(2)}) %collective-permute-start.43) | collective-permute-done | bytes 786464 | tf_op jit(solution)/shard_map/ppermute | solution.py:46
  286.0 12.7 %hidden_back.1 = (bf16[1536,2048]{1,0:T(8,128)(2,1)}, f32[1536,704]{1,0:T(8,128)}) custom-call(s32[2]{0:T(128)} %pad_add_fusion.me, bf16[1408,2048]{1,0:T(8,128)(2,1)} %all-gather.14.cloned.1.call-done.down_rows, bf16[192,2048]{1,0:T(8,128)(2,1)} %copy-done.34, bf16[192,2048]{1,0:T(8,128)(2,1)} %copy-done.35, bf16[192,2048]{1,0:T(8,128)(2,1)} %copy-done.36, ...), custom_call_target="tpu_custom_call" | custom-call | flops 1 | bytes 1 | tf_op jit(solution)/shard_map/hidden_back/pallas_call | solution.py:231
  300.2 16.3 %ffn_forward.1 = (bf16[1536,2048]{1,0:T(8,128)(2,1)}, bf16[1536,704]{1,0:T(8,128)(2,1)}, bf16[1536,1408]{1,0:T(8,128)(2,1)}) custom-call(bf16[192,2048]{1,0:T(8,128)(2,1)} %copy-done.33, bf16[192,2048]{1,0:T(8,128)(2,1)} %copy-done.37, bf16[192,2048]{1,0:T(8,128)(2,1)} %copy-done.38, bf16[96,2048]{1,0:T(8,128)(2,1)} %collective-permute-done.48.refs_3_, ...), custom_call_target="tpu_custom_call" | custom-call | flops 1 | bytes 1 | tf_op jit(solution)/shard_map/ffn_forward/pallas_call | solution.py:231
  316.5 16.2 %ffn_back.1 = (bf16[192,2048]{1,0:T(8,128)(2,1)}, bf16[192,2048]{1,0:T(8,128)(2,1)}, bf16[192,2048]{1,0:T(8,128)(2,1)}, bf16[192,2048]{1,0:T(8,128)(2,1)}, bf16[...) custom-call(f32[1536,704]{1,0:T(8,128)} %get-tuple-element.275.grad,, ...), custom_call_target="tpu_custom_call" | custom-call | flops 1 | bytes 1 | tf_op jit(solution)/shard_map/ffn_back/pallas_call | solution.py:231
  338.8 9.7 %down_grad.1 = (bf16[352,2048]{1,0:T(8,128)(2,1)}, bf16[352,2048]{1,0:T(8,128)(2,1)}) custom-call(s32[2]{0:T(128)} %pad_add_fusion.me, bf16[1536,704]{1,0:T(8,128)(2,1)} %get-tuple-element.310.hidden, bf16[1536,2048]{1,0:T(8,128)(2,1)} %get-tuple-element.299.rows), custom_call_target="tpu_custom_call" | custom-call | flops 1 | bytes 1 | tf_op jit(solution)/shard_map/down_grad/pallas_call | solution.py:231
  361.5 16.8 %collective-permute-done.54 = bf16[192,2048]{1,0:T(8,128)(2,1)S(1)} collective-permute-done((bf16[192,2048]{1,0:T(8,128)(2,1)S(1)}, bf16[192,2048]{1,0:T(8,128)(2,1)S(1)}, u32[]{:S(2)}, u32[]{:S(2)}) %collective-permute-start.54) | collective-permute-done | bytes 786464 | tf_op jit(solution)/shard_map/ppermute | solution.py:46
  383.8 14.0 %convolution_convert_fusion = bf16[2048,1408]{1,0:T(8,128)(2,1)} fusion(bf16[1536,2048]{1,0:T(8,128)(2,1)S(1)} %bitcast.45, bf16[1536,1408]{1,0:T(8,128)(2,1)} %get-tuple-element.306), kind=kOutput, calls=%fused_computation | convolution fusion | flops 8861253632 | bytes 16384000 | tf_op jit(solution)/shard_map/dot_general | solution.py:1106
  397.8 15.2 %reduce-scatter.7.cloned.1.call-done = bf16[176,2048]{1,0:T(8,128)(2,1)} async-done(((bf16[704,2048]{1,0:T(8,128)(2,1)}), bf16[176,2048]{1,0:T(8,128)(2,1)}) %reduce-scatter.7.cloned.1.call-update) | async-done | bytes 720912 | tf_op jit(solution)/shard_map/reduce_scatter | solution.py:132
  421.0 10.1 %down_share.1 = (bf16[192,2048]{1,0:T(8,128)(2,1)}, bf16[192,2048]{1,0:T(8,128)(2,1)}, bf16[192,2048]{1,0:T(8,128)(2,1)}, bf16[192,2048]{1,0:T(8,128)(2,1)}, bf1...) custom-call(s32[2]{0:T(128)} %pad_add_fusion.me, ...), custom_call_target="tpu_custom_call" | custom-call | flops 1 | bytes 1 | tf_op jit(solution)/shard_map/down_share/pallas_call | solution.py:231
  441.4 9.0 %collective-permute-done.65.refs_8_.refs_16_ = bf16[96,2048]{1,0:T(8,128)(2,1)S(1)} collective-permute-done((bf16[96,2048]{1,0:T(8,128)(2,1)S(1)}, bf16[96,2048]{1,0:T(8,128)(2,1)S(1)}, u32[]{:S(2)}, u32[]{:S(2)}) %collective-permute-start.65) | collective-permute-done | bytes 393248 | tf_op jit(solution)/shard_map/ppermute | solution.py:49
  453.8 8.1 %out_weight_grad.1 = bf16[512,2048]{1,0:T(8,128)(2,1)} custom-call(bf16[192,512]{1,0:T(8,128)(2,1)} %get-tuple-element.244.refs_0_, bf16[192,512]{1,0:T(8,128)(2,1)} %copy-done.39, bf16[192,512]{1,0:T(8,128)(2,1)} %copy-done.40, bf16[192,512]{1,0:T(8,128)(2,1)} %copy-done.41, bf16[192,512]{1,0:T(8,128)(2,1)} %copy-done.42, bf16[192,512]{1,0:T(8,128)(2,1)} %copy-done.43, ...), custom_call_target="tpu_custom_call" | custom-call | flops 1 | bytes 1 | tf_op jit(solution)/shard_map/out_weight_grad/pallas_call | solution.py:231
  463.9 8.2 %out_back.1 = (bf16[192,512]{1,0:T(8,128)(2,1)}, bf16[192,512]{1,0:T(8,128)(2,1)}, bf16[192,512]{1,0:T(8,128)(2,1)}, bf16[192,512]{1,0:T(8,128)(2,1)}, bf16[192,...) custom-call(s32[2]{0:T(128)} %pad_add_fusion.me, ...), custom_call_target="tpu_custom_call" | custom-call | flops 1 | bytes 1 | tf_op jit(solution)/shard_map/out_back/pallas_call | solution.py:231
  500.2 18.6 %attend_back.1 = (bf16[192,4096]{1,0:T(8,128)(2,1)}, bf16[768,512]{1,0:T(8,128)(2,1)}, bf16[768,512]{1,0:T(8,128)(2,1)}) custom-call(s32[16]{0:T(128)} %pad_add_fusion.1.table, s32[16]{0:T(128)} %bitcast.34, s32[2]{0:T(128)} %fusion.27.here, s32[2]{0:T(128)} %pad_add_fusion.me, bf16[192,4096]{1,0:T(8,128)(2,1)} %get-tuple-element.345.q_in, ...), custom_call_target="tpu_custom_call" | custom-call | flops 1 | bytes 1 | tf_op jit(solution)/shard_map/attend_back/pallas_call | solution.py:231
  531.4 13.6 %up_back.1 = (bf16[128,4224]{1,0:T(8,128)(2,1)}, bf16[128,4224]{1,0:T(8,128)(2,1)}, bf16[128,4224]{1,0:T(8,128)(2,1)}, bf16[128,4224]{1,0:T(8,128)(2,1)}, bf16[1...) custom-call(s32[2]{0:T(128)} %pad_add_fusion.me, ...), custom_call_target="tpu_custom_call" | custom-call | flops 1 | bytes 1 | tf_op jit(solution)/shard_map/up_back/pallas_call | solution.py:231
  564.5 11.8 %project_back.1 = (bf16[256,1664]{1,0:T(8,128)(2,1)}, bf16[256,1664]{1,0:T(8,128)(2,1)}, bf16[256,1664]{1,0:T(8,128)(2,1)}, bf16[256,1664]{1,0:T(8,128)(2,1)}, b...) custom-call(s32[2]{0:T(128)} %pad_add_fusion.me, ...), custom_call_target="tpu_custom_call" | custom-call | flops 1 | bytes 1 | tf_op jit(solution)/shard_map/project_back/pallas_call | solution.py:231
  578.3 8.3 %collective-permute-done.90 = bf16[128,4224]{1,0:T(8,128)(2,1)S(1)} collective-permute-done((bf16[128,4224]{1,0:T(8,128)(2,1)}, bf16[128,4224]{1,0:T(8,128)(2,1)S(1)}, u32[]{:S(2)}, u32[]{:S(2)}) %collective-permute-start.90) | collective-permute-done | bytes 1081376 | tf_op jit(solution)/shard_map/ppermute | solution.py:46
  610.3 16.0 %collective-permute-done.95 = bf16[256,1664]{1,0:T(8,128)(2,1)S(1)} collective-permute-done((bf16[256,1664]{1,0:T(8,128)(2,1)S(1)}, bf16[256,1664]{1,0:T(8,128)(2,1)S(1)}, u32[]{:S(2)}, u32[]{:S(2)}) %collective-permute-start.95) | collective-permute-done | bytes 852000 | tf_op jit(solution)/shard_map/ppermute | solution.py:46
  (545 shorter events, 316.2 us)
Async XLA Ops:
  7.2 71.8 %all-gather.6.cloned.1.call-start = ((), (), s32[]{:S(2)}) async-start(), calls=%async_computation.8 | async-start | bytes 1310720 | tf_op jit(solution)/shard_map/all_gather | solution.py:129
  7.9 94.3 %all-gather.8.cloned.1.call-start = ((), (), s32[]{:S(2)}) async-start(), calls=%async_computation.9 | async-start | bytes 4718592 | tf_op jit(solution)/shard_map/all_gather | solution.py:135
  13.2 38.1 %all-to-all-start = ((bf16[8,64,1408]{2,1,0:T(8,128)(2,1)}), bf16[8,64,1408]{2,1,0:T(8,128)(2,1)S(1)}, u32[]{:S(2)}, u32[]{:S(2)}) async-start(bf16[8,64,1408]{2,1,0:T(8,128)(2,1)} %maximum_bitcast_fusion), calls=%async_computation | async-start | bytes 2883584 | tf_op jit(solution)/shard_map/all_to_all | solution.py:171
  18.5 124.7 %all-gather.10.cloned.1.call-start = ((), (), s32[]{:S(2)}) async-start(), calls=%async_computation.10 | async-start | bytes 1769472 | tf_op jit(solution)/shard_map/all_gather | solution.py:135
  55.5 32.7 %collective-permute-start.4 = (bf16[256,1664]{1,0:T(8,128)(2,1)S(1)}, bf16[256,1664]{1,0:T(8,128)(2,1)}, u32[]{:S(2)}, u32[]{:S(2)}) collective-permute-start(bf16[256,1664]{1,0:T(8,128)(2,1)S(1)} %all_gather.18.refs_0_), channel_id=1, source_target_pairs={{0,1},{1,0},{2,3},{3,2},{4,5},{5,4},{6,7},{7,6},{8,9},{9,8},{10,11... | collective-permute-start | bytes 2555912 | tf_op jit(solution)/shard_map/ppermute | solution.py:43
  102.2 183.8 %all-gather.14.cloned.1.call-start = ((), (), s32[]{:S(2)}) async-start(), calls=%async_computation.12 | async-start | bytes 6488064 | tf_op jit(solution)/shard_map/all_gather | solution.py:135
  102.8 196.0 %all-gather.12.cloned.1.call-start = ((), (), s32[]{:S(2)}) async-start(), calls=%async_computation.11 | async-start | bytes 7208960 | tf_op jit(solution)/shard_map/all_gather | solution.py:129
  104.4 25.6 %collective-permute-start.11 = (bf16[128,4096]{1,0:T(8,128)(2,1)}, bf16[128,4096]{1,0:T(8,128)(2,1)S(1)}, u32[]{:S(2)}, u32[]{:S(2)}) collective-permute-start(bf16[128,4096]{1,0:T(8,128)(2,1)} %all-gather.6.cloned.1.call-done.refs_0_), channel_id=1, source_target_pairs={{0,16},{16,0},{8,24},{24,8},{1,17},{17,1},{9,25},{25,9},{2,18},{18... | collective-permute-start | bytes 3145736 | tf_op jit(solution)/shard_map/ppermute | solution.py:49
  143.8 269.3 %reduce-scatter.7.cloned.1.call-start = ((), (), s32[]{:S(2)}) async-start(), calls=%async_computation.13 | async-start | bytes 3604480 | tf_op jit(solution)/shard_map/reduce_scatter | solution.py:132
  146.2 25.8 %collective-permute-start.18 = (bf16[192,2048]{1,0:T(8,128)(2,1)S(1)}, bf16[192,2048]{1,0:T(8,128)(2,1)S(1)}, u32[]{:S(2)}, u32[]{:S(2)}) collective-permute-start(bf16[192,2048]{1,0:T(8,128)(2,1)S(1)} %multiply_convert_fusion.refs_5_.cot), channel_id=1, source_target_pairs={{0,8},{8,0},{16,24},{24,16},{1,9},{9,1},{17,25},{25,17},{2,10},{10... | collective-permute-start | bytes 2359304 | tf_op jit(solution)/shard_map/ppermute | solution.py:46
  176.4 32.5 %collective-permute-start.20 = (bf16[96,2048]{1,0:T(8,128)(2,1)}, bf16[96,2048]{1,0:T(8,128)(2,1)}, u32[]{:S(2)}, u32[]{:S(2)}) collective-permute-start(bf16[96,2048]{1,0:T(8,128)(2,1)} %slice.277), channel_id=1, source_target_pairs={{0,16},{16,0},{8,24},{24,8},{1,17},{17,1},{9,25},{25,9},{2,18},{18... | collective-permute-start | bytes 1179656 | tf_op jit(solution)/shard_map/ppermute | solution.py:49
  179.7 29.2 %collective-permute-start.21 = (bf16[96,2048]{1,0:T(8,128)(2,1)}, bf16[96,2048]{1,0:T(8,128)(2,1)}, u32[]{:S(2)}, u32[]{:S(2)}) collective-permute-start(bf16[96,2048]{1,0:T(8,128)(2,1)} %slice.278), channel_id=1, source_target_pairs={{0,8},{8,0},{16,24},{24,16},{1,9},{9,1},{17,25},{25,17},{2,10},{10... | collective-permute-start | bytes 1179656 | tf_op jit(solution)/shard_map/ppermute | solution.py:46
  272.2 26.7 %collective-permute-start.42 = (bf16[192,2048]{1,0:T(8,128)(2,1)}, bf16[192,2048]{1,0:T(8,128)(2,1)S(1)}, u32[]{:S(2)}, u32[]{:S(2)}) collective-permute-start(bf16[192,2048]{1,0:T(8,128)(2,1)} %get-tuple-element.281.refs_5_), channel_id=1, source_target_pairs={{0,1},{1,0},{2,3},{3,2},{4,5},{5,4},{6,7},{7,6},{8,9},{9,8},{10,11... | collective-permute-start | bytes 2359304 | tf_op jit(solution)/shard_map/ppermute | solution.py:43
  355.3 163.7 %reduce-scatter.9.cloned.1.call-start = ((), (), s32[]{:S(2)}) async-start(), calls=%async_computation.14 | async-start | bytes 7208960 | tf_op jit(solution)/shard_map/reduce_scatter | solution.py:132
  413.1 135.9 %reduce-scatter.11.cloned.1.call-start = ((), (), s32[]{:S(2)}) async-start(), calls=%async_computation.15 | async-start | bytes 983040 | tf_op jit(solution)/shard_map/reduce_scatter | solution.py:132
  421.0 30.7 %collective-permute-start.60 = (bf16[192,2048]{1,0:T(8,128)(2,1)}, bf16[192,2048]{1,0:T(8,128)(2,1)S(1)}, u32[]{:S(2)}, u32[]{:S(2)}) collective-permute-start(bf16[192,2048]{1,0:T(8,128)(2,1)} %get-tuple-element.309.refs_5_.refs_13_), channel_id=1, source_target_pairs={{0,1},{1,0},{2,3},{3,2},{4,5},{5,4},{6,7},{7,6},{8,9},{9,8},{10,11... | collective-permute-start | bytes 2359304 | tf_op jit(solution)/shard_map/ppermute | solution.py:43
  523.8 86.6 %reduce-scatter.13.cloned.1.call-start = ((), (), s32[]{:S(2)}) async-start(), calls=%async_computation.16 | async-start | bytes 2621440 | tf_op jit(solution)/shard_map/reduce_scatter | solution.py:132
  525.2 126.5 %reduce-scatter.17.cloned.1.call-start = ((), (), s32[]{:S(2)}) async-start(), calls=%async_computation.18 | async-start | bytes 1351680 | tf_op jit(solution)/shard_map/reduce_scatter | solution.py:132
  560.4 26.1 %collective-permute-start.90 = (bf16[128,4224]{1,0:T(8,128)(2,1)}, bf16[128,4224]{1,0:T(8,128)(2,1)S(1)}, u32[]{:S(2)}, u32[]{:S(2)}) collective-permute-start(bf16[128,4224]{1,0:T(8,128)(2,1)} %pad_maximum_fusion.2), channel_id=1, source_target_pairs={{0,8},{8,0},{16,24},{24,16},{1,9},{9,1},{17,25},{25,17},{2,10},{10... | collective-permute-start | bytes 3244040 | tf_op jit(solution)/shard_map/ppermute | solution.py:46
  563.0 25.9 %collective-permute-start.91 = (bf16[128,4224]{1,0:T(8,128)(2,1)}, bf16[128,4224]{1,0:T(8,128)(2,1)}, u32[]{:S(2)}, u32[]{:S(2)}) collective-permute-start(bf16[128,4224]{1,0:T(8,128)(2,1)} %pad_maximum_fusion.3), channel_id=1, source_target_pairs={{0,16},{16,0},{8,24},{24,8},{1,17},{17,1},{9,25},{25,9},{2,18},{18... | collective-permute-start | bytes 3244040 | tf_op jit(solution)/shard_map/ppermute | solution.py:49
  589.6 44.0 %collective-permute-start.92 = (bf16[256,1664]{1,0:T(8,128)(2,1)}, bf16[256,1664]{1,0:T(8,128)(2,1)}, u32[]{:S(2)}, u32[]{:S(2)}) collective-permute-start(bf16[256,1664]{1,0:T(8,128)(2,1)} %get-tuple-element.399), channel_id=1, source_target_pairs={{0,1},{1,0},{2,3},{3,2},{4,5},{5,4},{6,7},{7,6},{8,9},{9,8},{10,11... | collective-permute-start | bytes 2555912 | tf_op jit(solution)/shard_map/ppermute | solution.py:43
  596.3 30.1 %collective-permute-start.95 = (bf16[256,1664]{1,0:T(8,128)(2,1)S(1)}, bf16[256,1664]{1,0:T(8,128)(2,1)S(1)}, u32[]{:S(2)}, u32[]{:S(2)}) collective-permute-start(bf16[256,1664]{1,0:T(8,128)(2,1)S(1)} %pad_maximum_fusion.5), channel_id=1, source_target_pairs={{0,8},{8,0},{16,24},{24,16},{1,9},{9,1},{17,25},{25,17},{2,10},{10... | collective-permute-start | bytes 2555912 | tf_op jit(solution)/shard_map/ppermute | solution.py:46
  598.7 28.6 %collective-permute-start.97 = (bf16[256,1664]{1,0:T(8,128)(2,1)}, bf16[256,1664]{1,0:T(8,128)(2,1)}, u32[]{:S(2)}, u32[]{:S(2)}) collective-permute-start(bf16[256,1664]{1,0:T(8,128)(2,1)} %pad_maximum_fusion.6), channel_id=1, source_target_pairs={{0,16},{16,0},{8,24},{24,8},{1,17},{17,1},{9,25},{25,9},{2,18},{18... | collective-permute-start | bytes 2555912 | tf_op jit(solution)/shard_map/ppermute | solution.py:49
  640.4 29.2 %reduce-scatter.15.cloned.1.call-start = ((), (), s32[]{:S(2)}) async-start(), calls=%async_computation.17 | async-start | bytes 1064960 | tf_op jit(solution)/shard_map/reduce_scatter | solution.py:132
  (184 other events, 2028.4 us)
Sparse Core Ops, SparseCore 0:
  9.6 44.3 all-gather.5
  55.5 46.6 all-gather.7
  104.4 23.7 all-gather.9
  129.7 59.9 all-gather.13
  191.7 105.3 all-gather.11
  355.4 57.5 reduce-scatter.6
  415.3 102.0 reduce-scatter.8
  523.9 25.1 reduce-scatter.10
  551.3 43.1 reduce-scatter.12
  610.4 25.9 reduce-scatter.16
  647.6 21.8 reduce-scatter.14

commit v4 on v3

--- a/solution.py
+++ b/solution.py
@@ -134,20 +134,8 @@
     def rows_gather(self, w):
         return lax.all_gather(w, ("z", "c"), axis=0, tiled=True)
 
-    def rows_parted(self, g):
-        n = g.shape[1]
-        core = lax.axis_index("c")
-        parts = g.reshape(self.Z // 2, 2, -1, n)
-        return [
-            lax.dynamic_slice_in_dim(parts, k, 1, 1).reshape(-1, n) for k in (core, 1 - core)
-        ]
-
     def rows_return(self, mine, sent):
-        came = self.swap_c(sent)
-        first = lax.axis_index("c") == 0
-        return jnp.concatenate(
-            [jnp.where(first, mine, came), jnp.where(first, came, mine)], axis=0
-        )
+        return rows_joined(self.me(), mine, self.swap_c(sent))
 
     def cols_exchange(self, gate, up):
         r, n = gate.shape
@@ -217,7 +205,7 @@
     return (jnp.cos(angle), jnp.sin(angle))
 
 
-def _call(kernel, name, out_shape, args, scratch=(), memory=None):
+def _call(kernel, name, out_shape, args, scratch=(), memory=None, flops=1):
     specs = [
         pl.BlockSpec(
             memory_space=pltpu.SMEM
@@ -235,7 +223,7 @@
         out_specs=out_specs if many else out_specs[0],
         scratch_shapes=list(scratch),
         compiler_params=pltpu.CompilerParams(vmem_limit_bytes=VMEM_BYTES),
-        cost_estimate=pl.CostEstimate(flops=1, bytes_accessed=1, transcendentals=0),
+        cost_estimate=pl.CostEstimate(flops=flops, bytes_accessed=1, transcendentals=0),
         name=name,
     )(*args)
 
@@ -644,13 +632,7 @@
     step = 512
     for first in range(0, rows.shape[1], step):
         grad[:, first : first + step] = _tn(hidden[...], rows[:, first : first + step]).astype(BF)
-    r = wide // net.Z
-    for k in range(net.Z // 2):
-        low = grad[2 * k * r : (2 * k + 1) * r, :]
-        high = grad[(2 * k + 1) * r : (2 * k + 2) * r, :]
-        here = slice(k * r, (k + 1) * r)
-        mine[here, :] = jnp.where(me[1] == 0, low, high)
-        sent[here, :] = jnp.where(me[1] == 0, high, low)
+    _part_rows(net, me, grad, mine, sent)
 
 
 def down_grad(net, me, hidden, rows):
@@ -765,8 +747,30 @@
     )
 
 
-def out_grad_kernel(net, count, *refs):
-    heads, rows_in, grad_out = refs[: 2 * net.S], refs[2 * net.S : -1], refs[-1]
+def _part_rows(net, me, grad, mine, sent):
+    r = grad.shape[0] // net.Z
+    for k in range(net.Z // 2):
+        low = grad[2 * k * r : (2 * k + 1) * r, :]
+        high = grad[(2 * k + 1) * r : (2 * k + 2) * r, :]
+        here = slice(k * r, (k + 1) * r)
+        mine[here, :] = jnp.where(me[1] == 0, low, high)
+        sent[here, :] = jnp.where(me[1] == 0, high, low)
+
+
+def rows_joined_kernel(me, mine, came, out):
+    half = mine.shape[0]
+    out[pl.ds(pl.multiple_of(me[1] * half, half), half), :] = mine[...]
+    out[pl.ds(pl.multiple_of((1 - me[1]) * half, half), half), :] = came[...]
+
+
+def rows_joined(me, mine, came):
+    half, width = mine.shape
+    return _call(rows_joined_kernel, "rows_joined", _shape(2 * half, width), [me, mine, came])
+
+
+def out_grad_kernel(net, count, me, *refs):
+    heads, rows_in = refs[: 2 * net.S], refs[2 * net.S : -3]
+    mine, sent, grad = refs[-3:]
     group = count // 2
     total = None
     for side in range(2):
@@ -776,15 +780,19 @@
         right = jnp.concatenate([ref[...] for ref in rows_in[side * group : (side + 1) * group]], axis=0)
         part = _tn(left, right)
         total = part if total is None else total + part
-    grad_out[...] = total.astype(BF)
-
-
-def out_weight_grad(net, heads, rows):
+    grad[...] = total.astype(BF)
+    _part_rows(net, me, grad, mine, sent)
+
+
+def out_weight_grad(net, me, heads, rows):
+    size, width = heads[0].shape[1], rows[0].shape[1]
     return _call(
         functools.partial(out_grad_kernel, net, len(rows)),
         "out_weight_grad",
-        _shape(heads[0].shape[1], rows[0].shape[1]),
-        [*heads, *rows],
+        (_shape(size // 2, width), _shape(size // 2, width)),
+        [me, *heads, *rows],
+        [pltpu.VMEM((size, width), BF)],
+        flops=8 * heads[0].size * len(heads) * rows[0].shape[1],
     )
 
 
@@ -872,40 +880,48 @@
     )
 
 
-def up_back_kernel(net, count, results, me, dq, cqn, low_ref, gain_ref, *refs):
-    pieces, outs = refs[:count], refs[count : count + results]
-    low_grad_out, up_q, grad = refs[count + results :]
+def up_grad_kernel(net, me, dq, cqn, *refs):
+    outs, grad = refs[:-1], refs[-1]
+    step = 1024
+    for first in range(0, dq.shape[1], step):
+        grad[:, first : first + step] = _tn(cqn[...], dq[:, first : first + step]).astype(BF)
+    _part(net, me, grad, outs)
+
+
+def up_weight_grad(net, me, dq, cqn):
+    low_rank, wide = cqn.shape[1], dq.shape[1]
+    return _call(
+        functools.partial(up_grad_kernel, net),
+        "up_weight_grad",
+        _out_pieces(net, low_rank, wide),
+        [me, dq, cqn],
+        [pltpu.VMEM((low_rank, wide), BF)],
+    )
+
+
+def up_back_kernel(net, me, dq, low_ref, gain_ref, *refs):
+    pieces, (low_grad_out, gain_out, up_q) = refs[:-3], refs[-3:]
     _join(net, me, pieces, up_q)
-    wide = dq.shape[1]
     gain = gain_ref[...]
     upstream = _nt(dq[...], up_q[...])
     low = low_ref[...]
     scale = _mean_scale(low)
     gain_grad = jnp.sum(upstream * low * scale, axis=0, keepdims=True)
+    gain_out[...] = jnp.broadcast_to(gain_grad, gain_out.shape)
     scaled = gain * upstream
     inner = jnp.mean(scaled * low, axis=1, keepdims=True)
     low_grad_out[...] = (scale * scaled - low * (scale * scale * scale * inner)).astype(BF)
-    step = 1024
-    for first in range(0, wide, step):
-        grad[:, first : first + step] = _tn(cqn[...], dq[:, first : first + step]).astype(BF)
-    grad[:, wide:] = jnp.transpose(
-        jnp.broadcast_to(gain_grad, (128, gain_grad.shape[1]))
-    ).astype(BF)
-    _part(net, me, grad, outs)
-
-
-def up_back(net, me, dq, cqn, low, gain, pieces):
+
+
+def up_back(net, dq, low, gain, pieces, me):
     tokens, low_rank = low.shape
-    wide = H * HD + 128
-    outs = _out_pieces(net, low_rank, wide)
-    *parts, grad = _call(
-        functools.partial(up_back_kernel, net, len(pieces), len(outs)),
+    return _call(
+        functools.partial(up_back_kernel, net),
         "up_back",
-        outs + [_shape(tokens, low_rank)],
-        [me, dq, cqn, low, gain, *pieces],
-        [pltpu.VMEM((low_rank, H * HD), BF), pltpu.VMEM((low_rank, wide), BF)],
-    )
-    return parts, grad
+        [_shape(tokens, low_rank), _shape(8, low_rank, dtype=F32)],
+        [me, dq, low, gain, *pieces],
+        [pltpu.VMEM((low_rank, dq.shape[1]), BF)],
+    )
 
 
 def _out_pieces(net, rows, wide):
@@ -914,7 +930,7 @@
     return [_shape(rows, wide)]
 
 
-def project_back_kernel(net, count, results, me, x_ref, low_grad, both, cos, sin, mid_grad, gains, mid_gain, *refs):
+def project_back_kernel(net, count, results, me, x_ref, low_grad, both, cos, sin, mid_grad, gains, mid_gain, q_gain_grad, *refs):
     pieces, outs = refs[:count], refs[count : count + results]
     in_out, whole, grad = refs[count + results :]
     _join(net, me, pieces, whole)
@@ -945,14 +961,21 @@
     in_out[...] = (mid_grad[...] + scale * scaled - x * (scale * scale * scale * inner)).astype(BF)
     tall = lax.broadcasted_iota(jnp.int32, (128, width), 0)
     both_gains = jnp.where(
-        tall == 0, jnp.broadcast_to(gain_grad, (128, width)),
-        jnp.broadcast_to(mid_gain[:1, :], (128, width)),
+        tall == 0,
+        jnp.broadcast_to(gain_grad, (128, width)),
+        jnp.where(
+            tall == 1,
+            jnp.broadcast_to(mid_gain[:1, :], (128, width)),
+            jnp.broadcast_to(q_gain_grad[...], (128, width)),
+        ),
     )
     grad[:, last:] = jnp.transpose(both_gains).astype(BF)
     _part(net, me, grad, outs)
 
 
-def project_back(net, me, x, low_grad, both, cos, sin, mid_grad, gains, mid_gain, pieces):
+def project_back(
+    net, me, x, low_grad, both, cos, sin, mid_grad, gains, mid_gain, q_gain_grad, pieces
+):
     tokens, width = x.shape
     wide = pieces[0].shape[1]
     outs = _out_pieces(net, width, wide)
@@ -960,7 +983,7 @@
         functools.partial(project_back_kernel, net, len(pieces), len(outs)),
         "project_back",
         outs + [_shape(tokens, width)],
-        [me, x, low_grad, both, cos, sin, mid_grad, gains, mid_gain, *pieces],
+        [me, x, low_grad, both, cos, sin, mid_grad, gains, mid_gain, q_gain_grad, *pieces],
         [pltpu.VMEM((width, wide), BF), pltpu.VMEM((width, wide), BF)],
     )
     return parts, in_grad
@@ -1133,18 +1156,22 @@
 
     middle_same = net.spread(middle_low, (middle_one,))
     middle_all = [*net.swap_all(middle_same), *middle_same]
-    heads_grad = net.exchange_pieces(out_back(net, me, out_rows, middle_all, tokens))
-    grad_out = net.rows_return(*net.rows_parted(out_weight_grad(net, heads, middle_all)))
+    heads_grad = out_back(net, me, out_rows, middle_all, tokens)
     count = 2 * net.S
-    done = tie(*heads_grad, *kept["shares"], grad_out)
-    heads_grad, shares, grad_out = done[:count], done[count:-1], done[-1]
+    done = tie(*heads_grad, *middle_all)
+    middle_all = done[count:]
+    heads_grad = net.exchange_pieces(done[:count])
+    grad_mine, grad_sent = out_weight_grad(net, me, heads, middle_all)
+    count = 2 * net.S
+    done = tie(*heads_grad, *kept["shares"], grad_mine, grad_sent)
+    heads_grad, shares = done[:count], done[count:-2]
 
     def result_two(*moved):
         backs = attend_back(
             net, table, order, here, me, query_rows, heads_grad, attended, log_total, cosine,
             sine, both,
         )
-        *moved, kept["query_pre"], same, other, kept["grad_gu"] = tie(*moved, *backs, grad_gu)
+        *moved, kept["query_pre"], same, other = tie(*moved, *backs)
         kept["both_grads"] = same.astype(F32) + net.swap_c(other).astype(F32)
         return moved
 
@@ -1158,12 +1185,9 @@
         )
     ).astype(BF)
     both_sum = net.z_scatter(kept["both_grads"])
-    up_parts, low_grad = up_back(
-        net, me, kept["query_pre"], query_normed, query_low, gain_q, up_pieces
-    )
-
-    grad_out = net.z_scatter(grad_out)
-    grad_down = kept["down"].astype(F32)
+    up_parts = up_weight_grad(net, me, kept["query_pre"], query_normed)
+    *up_parts, kept["grad_gu"] = tie(*up_parts, grad_gu)
+    grad_out = net.z_scatter(net.rows_return(*done[-2:]))
 
     def whole(parts):
         upper, upper_last, lower, lower_last = parts
@@ -1173,15 +1197,20 @@
             )
         )
 
-    both_sum, *up_parts = tie(both_sum, *up_parts)
     def up_one(*came):
-        *came, kept["both_sum"] = tie(*came, both_sum)
+        *came, kept["query_pre"] = tie(*came, kept["query_pre"])
         return came
 
     def up_two(*moved):
+        low_grad, gain_grad = up_back(
+            net, kept["query_pre"], query_low, gain_q, up_pieces, me
+        )
+        gain_grad = jnp.pad(
+            gain_grad[0].reshape(-1, q_gain.shape[0]), ((0, 0), (0, rows - q_gain.shape[0]))
+        ).reshape(1, -1)
         first_parts, kept["in_grad"] = project_back(
-            net, me, hidden_in, low_grad, kept["both_sum"], cosine, sine, middle_grad, gains,
-            middle_gain, first_pieces,
+            net, me, hidden_in, low_grad, both_sum, cosine, sine, middle_grad, gains,
+            middle_gain, gain_grad, first_pieces,
         )
         done = tie(*moved, *first_parts)
         kept["first_parts"] = done[len(moved) :]
@@ -1190,13 +1219,16 @@
     up_out = whole(net.collect(*net.weight_sides(up_parts), (up_one, up_two)))
 
     def first_two(*moved):
-        *moved, kept["grad_out"], kept["grad_gu"] = tie(*moved, grad_out, kept["grad_gu"])
+        *moved, kept["grad_out"], kept["grad_gu"], kept["down"] = tie(
+            *moved, grad_out, kept["grad_gu"], kept["down"]
+        )
         return moved
 
     first_out = whole(
         net.collect(*net.weight_sides(kept["first_parts"]), (None, first_two))
     )
     grad_out = kept["grad_out"].astype(F32)
+    grad_down = kept["down"].astype(F32)
     grad_gate, grad_upward = net.cols_return(kept["grad_gu"])
     grad_low, grad_key, grad_value, grad_gains = finish(first_out, low_rank)
     return (
@@ -1204,8 +1236,8 @@
         kept["in_grad"],
         grad_gains[0],
         grad_low,
-        up_out[:, H * HD].astype(F32),
-        up_out[:, : H * HD].astype(F32),
+        grad_gains[2, : q_gain.shape[0]],
+        up_out.astype(F32),
         grad_key,
         grad_value,
         grad_out,

time: 689 us -> 675 us (0.980)
  waiting for transfers between devices: 277 us -> 252 us
  starting transfers between devices: 80 us -> 91.5 us
    ppermute x20, waiting for transfers between devices: 118 us -> 96.6 us  [swap_x(): return lax.ppermute(a, 'slot', [(0, 1), (1, 0), (2, 3), (3, 2)])]
    ppermute x20, waiting for transfers between devices: 69.4 us -> 83.1 us  [swap_y(): return lax.ppermute(a, 'slot', [(0, 2), (2, 0), (1, 3), (3, 1)])]
    ppermute x14, waiting for transfers between devices: 32.6 us -> 22.1 us  [exchange_pieces(): lax.ppermute(pieces[number], ('slot', 'c'), [(i, i ^ step) for i in range...]
    ppermute x20, starting transfers between devices: 23.5 us -> 31 us  [swap_y(): return lax.ppermute(a, 'slot', [(0, 2), (2, 0), (1, 3), (3, 1)])]
    unnamed x186 -> x188, local copies, waits for them, and re-layouts: 12.2 us -> 16.2 us
    pallas_call x16 -> x19, Pallas kernels: 170 us -> 169 us  [_call(): pl.pallas_call(kernel, out_shape=out_shape, in_specs=specs, out_specs=out...]
  transfers between devices with their start and end apart: 115 -> 115, of which waited for: 58 -> 52; matrix products, arithmetic and copies ran while one was open for 13% -> 13% of each run, Pallas kernels for 19% -> 18%
where the time goes in v4:
time: 675 us; the launch traced here: 665 us
  waiting for transfers between devices  252 us (37%)
  Pallas kernels  169 us (25%)
  starting transfers between devices  91.5 us (14%)
  other arithmetic  55.3 us (8%)
  local copies, waits for them, and re-layouts  35.5 us (5%)
  blocking collectives  32.2 us (5%)
  between operations  15.7 us (2%)
  matrix products  14.1 us (2%)
    pallas_call x19, Pallas kernels, _call(): pl.pallas_call(kernel, out_shape=out_shape, in_specs=specs, out_specs=out...  169 us
    ppermute x20, waiting for transfers between devices, swap_x(): return lax.ppermute(a, 'slot', [(0, 1), (1, 0), (2, 3), (3, 2)])  96.6 us
    ppermute x20, waiting for transfers between devices, swap_y(): return lax.ppermute(a, 'slot', [(0, 2), (2, 0), (1, 3), (3, 1)])  83.1 us
    all_gather x1, blocking collectives, z_gather(): return lax.all_gather(w, 'z', axis=0, tiled=True)  32.2 us
    ppermute x20, starting transfers between devices, swap_y(): return lax.ppermute(a, 'slot', [(0, 2), (2, 0), (1, 3), (3, 1)])  31 us
    ppermute x20, starting transfers between devices, swap_x(): return lax.ppermute(a, 'slot', [(0, 1), (1, 0), (2, 3), (3, 2)])  24.2 us
    ppermute x14, waiting for transfers between devices, exchange_pieces(): lax.ppermute(pieces[number], ('slot', 'c'), [(i, i ^ step) for i in range...  22.1 us
    reduce_scatter x6, waiting for transfers between devices, z_scatter(): return lax.psum_scatter(g.astype(BF), 'z', scatter_dimension=0, tiled=True)  19.5 us
  transfers between devices with their start and end apart: 115, of which 52 were waited for; matrix products, arithmetic and copies ran while one was open for 13% of the time, Pallas kernels for 18%

profile of v4, /device:TPU:0, one launch (start us, length us, event | category | flops | bytes accessed | tf_op | source)
XLA Modules:
  0.0 665.3 jit_solution(9271045267608014656)
XLA Ops:
  19.1 32.2 %all_gather.18.refs_0_ = bf16[256,1664]{1,0:T(8,128)(2,1)S(1)} all-gather(bf16[64,1664]{1,0:T(8,128)(2,1)S(1)} %pad_maximum_fusion.12), channel_id=1, replica_groups=mesh['slot'=4,'z'=4,'c'=2] {'z'}, dimensions={0}, use_global_device_ids=true | all-gather | bytes 1064960 | tf_op jit(solution)/shard_map/all_gather | solution.py:129
  55.6 16.9 %collective-permute-done.1.refs_2_ = bf16[256,1664]{1,0:T(8,128)(2,1)S(1)} collective-permute-done((bf16[256,1664]{1,0:T(8,128)(2,1)S(1)}, bf16[256,1664]{1,0:T(8,128)(2,1)S(1)}, u32[]{:S(2)}, u32[]{:S(2)}) %collective-permute-start.1) | collective-permute-done | bytes 852000 | tf_op jit(solution)/shard_map/ppermute | solution.py:49
  105.9 22.6 %collective-permute-done.11.refs_2_ = bf16[128,4096]{1,0:T(8,128)(2,1)S(1)} collective-permute-done((bf16[128,4096]{1,0:T(8,128)(2,1)}, bf16[128,4096]{1,0:T(8,128)(2,1)S(1)}, u32[]{:S(2)}, u32[]{:S(2)}) %collective-permute-start.11) | collective-permute-done | bytes 1048608 | tf_op jit(solution)/shard_map/ppermute | solution.py:49
  132.1 9.7 %collective-permute-done.12.refs_4_ = bf16[64,4096]{1,0:T(8,128)(2,1)S(1)} collective-permute-done((bf16[64,4096]{1,0:T(8,128)(2,1)S(1)}, bf16[64,4096]{1,0:T(8,128)(2,1)S(1)}, u32[]{:S(2)}, u32[]{:S(2)}) %collective-permute-start.12) | collective-permute-done | bytes 524320 | tf_op jit(solution)/shard_map/ppermute | solution.py:46
  151.0 16.3 %attend.1 = (bf16[192,512]{1,0:T(8,128)(2,1)}, bf16[192,512]{1,0:T(8,128)(2,1)}, bf16[192,512]{1,0:T(8,128)(2,1)}, bf16[192,512]{1,0:T(8,128)(2,1)}, bf16[192,51...) custom-call(s32[16]{0:T(128)} %pad_add_fusion.1.table, ...), custom_call_target="tpu_custom_call" | custom-call | flops 1 | bytes 1 | tf_op jit(solution)/shard_map/attend/pallas_call | solution.py:219
  199.0 8.0 %out_forward.1 = (bf16[192,2048]{1,0:T(8,128)(2,1)}, bf16[192,2048]{1,0:T(8,128)(2,1)}, bf16[192,2048]{1,0:T(8,128)(2,1)}, bf16[192,2048]{1,0:T(8,128)(2,1)}, bf...) custom-call(s32[2]{0:T(128)} %pad_add_fusion.me, ...), custom_call_target="tpu_custom_call" | custom-call | flops 1 | bytes 1 | tf_op jit(solution)/shard_map/out_forward/pallas_call | solution.py:219
  215.7 16.1 %collective-permute-done.32 = bf16[192,2048]{1,0:T(8,128)(2,1)S(1)} collective-permute-done((bf16[192,2048]{1,0:T(8,128)(2,1)S(1)}, bf16[192,2048]{1,0:T(8,128)(2,1)S(1)}, u32[]{:S(2)}, u32[]{:S(2)}) %collective-permute-start.32) | collective-permute-done | bytes 786464 | tf_op jit(solution)/shard_map/ppermute | solution.py:46
  237.4 8.7 %collective-permute-done.36.right_last = bf16[96,2048]{1,0:T(8,128)(2,1)S(1)} collective-permute-done((bf16[96,2048]{1,0:T(8,128)(2,1)S(1)}, bf16[96,2048]{1,0:T(8,128)(2,1)S(1)}, u32[]{:S(2)}, u32[]{:S(2)}) %collective-permute-start.36) | collective-permute-done | bytes 393248 | tf_op jit(solution)/shard_map/ppermute | solution.py:46
  254.4 15.4 %collective-permute-done.45.refs_7_ = bf16[192,2048]{1,0:T(8,128)(2,1)S(1)} collective-permute-done((bf16[192,2048]{1,0:T(8,128)(2,1)}, bf16[192,2048]{1,0:T(8,128)(2,1)S(1)}, u32[]{:S(2)}, u32[]{:S(2)}) %collective-permute-start.45) | collective-permute-done | bytes 786464 | tf_op jit(solution)/shard_map/ppermute | solution.py:49
  284.6 12.6 %hidden_back.1 = (bf16[1536,2048]{1,0:T(8,128)(2,1)}, f32[1536,704]{1,0:T(8,128)}) custom-call(s32[2]{0:T(128)} %pad_add_fusion.me, bf16[1408,2048]{1,0:T(8,128)(2,1)} %all-gather.14.cloned.1.call-done.down_rows, bf16[192,2048]{1,0:T(8,128)(2,1)} %copy-done.32, bf16[192,2048]{1,0:T(8,128)(2,1)} %copy-done.33, bf16[192,2048]{1,0:T(8,128)(2,1)} %copy-done.34, ...), custom_call_target="tpu_custom_call" | custom-call | flops 1 | bytes 1 | tf_op jit(solution)/shard_map/hidden_back/pallas_call | solution.py:219
  298.8 16.3 %ffn_forward.1 = (bf16[1536,2048]{1,0:T(8,128)(2,1)}, bf16[1536,704]{1,0:T(8,128)(2,1)}, bf16[1536,1408]{1,0:T(8,128)(2,1)}) custom-call(bf16[192,2048]{1,0:T(8,128)(2,1)} %copy-done.31, bf16[192,2048]{1,0:T(8,128)(2,1)} %copy-done.36, bf16[192,2048]{1,0:T(8,128)(2,1)} %copy-done.35, bf16[96,2048]{1,0:T(8,128)(2,1)} %collective-permute-done.48.refs_3_, ...), custom_call_target="tpu_custom_call" | custom-call | flops 1 | bytes 1 | tf_op jit(solution)/shard_map/ffn_forward/pallas_call | solution.py:219
  315.1 16.2 %ffn_back.1 = (bf16[192,2048]{1,0:T(8,128)(2,1)}, bf16[192,2048]{1,0:T(8,128)(2,1)}, bf16[192,2048]{1,0:T(8,128)(2,1)}, bf16[192,2048]{1,0:T(8,128)(2,1)}, bf16[...) custom-call(f32[1536,704]{1,0:T(8,128)} %get-tuple-element.297.grad,, ...), custom_call_target="tpu_custom_call" | custom-call | flops 1 | bytes 1 | tf_op jit(solution)/shard_map/ffn_back/pallas_call | solution.py:219
  337.3 9.7 %down_grad.1 = (bf16[352,2048]{1,0:T(8,128)(2,1)}, bf16[352,2048]{1,0:T(8,128)(2,1)}) custom-call(s32[2]{0:T(128)} %pad_add_fusion.me, bf16[1536,704]{1,0:T(8,128)(2,1)} %get-tuple-element.332.hidden, bf16[1536,2048]{1,0:T(8,128)(2,1)} %get-tuple-element.321.rows), custom_call_target="tpu_custom_call" | custom-call | flops 1 | bytes 1 | tf_op jit(solution)/shard_map/down_grad/pallas_call | solution.py:219
  361.6 16.4 %collective-permute-done.54 = bf16[192,2048]{1,0:T(8,128)(2,1)S(1)} collective-permute-done((bf16[192,2048]{1,0:T(8,128)(2,1)S(1)}, bf16[192,2048]{1,0:T(8,128)(2,1)S(1)}, u32[]{:S(2)}, u32[]{:S(2)}) %collective-permute-start.54) | collective-permute-done | bytes 786464 | tf_op jit(solution)/shard_map/ppermute | solution.py:46
  383.8 14.1 %convolution_convert_fusion = bf16[2048,1408]{1,0:T(8,128)(2,1)} fusion(bf16[1536,2048]{1,0:T(8,128)(2,1)S(1)} %bitcast.40, bf16[1536,1408]{1,0:T(8,128)(2,1)} %get-tuple-element.328), kind=kOutput, calls=%fused_computation | convolution fusion | flops 8861253632 | bytes 16384000 | tf_op jit(solution)/shard_map/dot_general | solution.py:1129
  397.8 13.3 %reduce-scatter.7.cloned.1.call-done = bf16[176,2048]{1,0:T(8,128)(2,1)} async-done(((bf16[704,2048]{1,0:T(8,128)(2,1)}), bf16[176,2048]{1,0:T(8,128)(2,1)}) %reduce-scatter.7.cloned.1.call-update) | async-done | bytes 720912 | tf_op jit(solution)/shard_map/reduce_scatter | solution.py:132
  419.2 10.2 %down_share.1 = (bf16[192,2048]{1,0:T(8,128)(2,1)}, bf16[192,2048]{1,0:T(8,128)(2,1)}, bf16[192,2048]{1,0:T(8,128)(2,1)}, bf16[192,2048]{1,0:T(8,128)(2,1)}, bf1...) custom-call(s32[2]{0:T(128)} %pad_add_fusion.me, ...), custom_call_target="tpu_custom_call" | custom-call | flops 1 | bytes 1 | tf_op jit(solution)/shard_map/down_share/pallas_call | solution.py:219
  450.5 8.2 %out_back.1 = (bf16[192,512]{1,0:T(8,128)(2,1)}, bf16[192,512]{1,0:T(8,128)(2,1)}, bf16[192,512]{1,0:T(8,128)(2,1)}, bf16[192,512]{1,0:T(8,128)(2,1)}, bf16[192,...) custom-call(s32[2]{0:T(128)} %pad_add_fusion.me, ...), custom_call_target="tpu_custom_call" | custom-call | flops 1 | bytes 1 | tf_op jit(solution)/shard_map/out_back/pallas_call | solution.py:219
  470.8 8.2 %out_weight_grad.1 = (bf16[256,2048]{1,0:T(8,128)(2,1)}, bf16[256,2048]{1,0:T(8,128)(2,1)}) custom-call(s32[2]{0:T(128)} %pad_add_fusion.me, bf16[192,512]{1,0:T(8,128)(2,1)} %get-tuple-element.266.refs_0_, bf16[192,512]{1,0:T(8,128)(2,1)} %copy-done.68, bf16[192,512]{1,0:T(8,128)(2,1)} %copy-done.69, bf16[192,512]{1,0:T(8,128)(2,1)} %collective-permute-done.24.refs_3_, ...), custom_call_target="tpu_custom_call" | custom-call | flops 12884901888 | bytes 1 | tf_op jit(solution)/shard_map/out_weight_grad/pallas_call | solution.py:219
  488.8 13.2 %attend_back.1 = (bf16[192,4096]{1,0:T(8,128)(2,1)}, bf16[768,512]{1,0:T(8,128)(2,1)}, bf16[768,512]{1,0:T(8,128)(2,1)}) custom-call(s32[16]{0:T(128)} %pad_add_fusion.1.table, s32[16]{0:T(128)} %bitcast.29, s32[2]{0:T(128)} %dynamic-slice_bitcast_fusion.here, s32[2]{0:T(128)} %pad_add_fusion.me, bf16[192,4096]{1,0:T(8,128)(2,1)} %get-tuple-element.387.q_in, ...), custom_call_target="tpu_custom_call" | custom-call | flops 1 | bytes 1 | tf_op jit(solution)/shard_map/attend_back/pallas_call | solution.py:219
  542.0 8.4 %up_back.1 = (bf16[192,1024]{1,0:T(8,128)(2,1)}, f32[8,1024]{1,0:T(8,128)}) custom-call(s32[2]{0:T(128)} %pad_add_fusion.me, bf16[192,4096]{1,0:T(8,128)(2,1)} %get-tuple-element.418.dq, f32[192,1024]{1,0:T(8,128)} %get-tuple-element.243.low.low_ref, f32[1,1024]{1,0:T(1,128)} %reshape.150.gain.gain_ref, ...), custom_call_target="tpu_custom_call" | custom-call | flops 1 | bytes 1 | tf_op jit(solution)/shard_map/up_back/pallas_call | solution.py:219
  552.0 11.7 %project_back.1 = (bf16[256,1664]{1,0:T(8,128)(2,1)}, bf16[256,1664]{1,0:T(8,128)(2,1)}, bf16[256,1664]{1,0:T(8,128)(2,1)}, bf16[256,1664]{1,0:T(8,128)(2,1)}, b...) custom-call(s32[2]{0:T(128)} %pad_add_fusion.me, ...), custom_call_target="tpu_custom_call" | custom-call | flops 1 | bytes 1 | tf_op jit(solution)/shard_map/project_back/pallas_call | solution.py:219
  576.0 9.7 %collective-permute-done.100 = bf16[64,4096]{1,0:T(8,128)(2,1)S(1)} collective-permute-done((bf16[64,4096]{1,0:T(8,128)(2,1)S(1)}, bf16[64,4096]{1,0:T(8,128)(2,1)S(1)}, u32[]{:S(2)}, u32[]{:S(2)}) %collective-permute-start.100) | collective-permute-done | bytes 524320 | tf_op jit(solution)/shard_map/ppermute | solution.py:49
  590.5 15.9 %collective-permute-done.94 = bf16[256,1664]{1,0:T(8,128)(2,1)S(1)} collective-permute-done((bf16[256,1664]{1,0:T(8,128)(2,1)}, bf16[256,1664]{1,0:T(8,128)(2,1)S(1)}, u32[]{:S(2)}, u32[]{:S(2)}) %collective-permute-start.94) | collective-permute-done | bytes 852000 | tf_op jit(solution)/shard_map/ppermute | solution.py:46
  (549 shorter events, 319.8 us)
Async XLA Ops:
  7.2 71.9 %all-gather.6.cloned.1.call-start = ((), (), s32[]{:S(2)}) async-start(), calls=%async_computation.8 | async-start | bytes 1310720 | tf_op jit(solution)/shard_map/all_gather | solution.py:129
  7.9 94.3 %all-gather.8.cloned.1.call-start = ((), (), s32[]{:S(2)}) async-start(), calls=%async_computation.9 | async-start | bytes 4718592 | tf_op jit(solution)/shard_map/all_gather | solution.py:135
  13.2 38.1 %all-to-all-start = ((bf16[8,64,1408]{2,1,0:T(8,128)(2,1)}), bf16[8,64,1408]{2,1,0:T(8,128)(2,1)S(1)}, u32[]{:S(2)}, u32[]{:S(2)}) async-start(bf16[8,64,1408]{2,1,0:T(8,128)(2,1)} %maximum_bitcast_fusion), calls=%async_computation | async-start | bytes 2883584 | tf_op jit(solution)/shard_map/all_to_all | solution.py:159
  18.5 124.7 %all-gather.10.cloned.1.call-start = ((), (), s32[]{:S(2)}) async-start(), calls=%async_computation.10 | async-start | bytes 1769472 | tf_op jit(solution)/shard_map/all_gather | solution.py:135
  55.5 32.7 %collective-permute-start.4 = (bf16[256,1664]{1,0:T(8,128)(2,1)S(1)}, bf16[256,1664]{1,0:T(8,128)(2,1)}, u32[]{:S(2)}, u32[]{:S(2)}) collective-permute-start(bf16[256,1664]{1,0:T(8,128)(2,1)S(1)} %all_gather.18.refs_0_), channel_id=1, source_target_pairs={{0,1},{1,0},{2,3},{3,2},{4,5},{5,4},{6,7},{7,6},{8,9},{9,8},{10,11... | collective-permute-start | bytes 2555912 | tf_op jit(solution)/shard_map/ppermute | solution.py:43
  102.2 182.3 %all-gather.14.cloned.1.call-start = ((), (), s32[]{:S(2)}) async-start(), calls=%async_computation.12 | async-start | bytes 6488064 | tf_op jit(solution)/shard_map/all_gather | solution.py:135
  102.8 194.4 %all-gather.12.cloned.1.call-start = ((), (), s32[]{:S(2)}) async-start(), calls=%async_computation.11 | async-start | bytes 7208960 | tf_op jit(solution)/shard_map/all_gather | solution.py:129
  102.9 25.6 %collective-permute-start.11 = (bf16[128,4096]{1,0:T(8,128)(2,1)}, bf16[128,4096]{1,0:T(8,128)(2,1)S(1)}, u32[]{:S(2)}, u32[]{:S(2)}) collective-permute-start(bf16[128,4096]{1,0:T(8,128)(2,1)} %all-gather.6.cloned.1.call-done.refs_0_), channel_id=1, source_target_pairs={{0,16},{16,0},{8,24},{24,8},{1,17},{17,1},{9,25},{25,9},{2,18},{18... | collective-permute-start | bytes 3145736 | tf_op jit(solution)/shard_map/ppermute | solution.py:49
  104.4 25.6 %collective-permute-start.9 = (bf16[128,4096]{1,0:T(8,128)(2,1)}, bf16[128,4096]{1,0:T(8,128)(2,1)S(1)}, u32[]{:S(2)}, u32[]{:S(2)}) collective-permute-start(bf16[128,4096]{1,0:T(8,128)(2,1)} %all-gather.6.cloned.1.call-done.refs_0_), channel_id=1, source_target_pairs={{0,8},{8,0},{16,24},{24,16},{1,9},{9,1},{17,25},{25,17},{2,10},{10... | collective-permute-start | bytes 3145736 | tf_op jit(solution)/shard_map/ppermute | solution.py:46
  143.8 267.4 %reduce-scatter.7.cloned.1.call-start = ((), (), s32[]{:S(2)}) async-start(), calls=%async_computation.13 | async-start | bytes 3604480 | tf_op jit(solution)/shard_map/reduce_scatter | solution.py:132
  174.4 32.6 %collective-permute-start.21 = (bf16[96,2048]{1,0:T(8,128)(2,1)S(1)}, bf16[96,2048]{1,0:T(8,128)(2,1)S(1)}, u32[]{:S(2)}, u32[]{:S(2)}) collective-permute-start(bf16[96,2048]{1,0:T(8,128)(2,1)S(1)} %slice.278), channel_id=1, source_target_pairs={{0,8},{8,0},{16,24},{24,16},{1,9},{9,1},{17,25},{25,17},{2,10},{10... | collective-permute-start | bytes 1179656 | tf_op jit(solution)/shard_map/ppermute | solution.py:46
  175.7 31.3 %collective-permute-start.20 = (bf16[96,2048]{1,0:T(8,128)(2,1)S(1)}, bf16[96,2048]{1,0:T(8,128)(2,1)S(1)}, u32[]{:S(2)}, u32[]{:S(2)}) collective-permute-start(bf16[96,2048]{1,0:T(8,128)(2,1)S(1)} %slice.277), channel_id=1, source_target_pairs={{0,16},{16,0},{8,24},{24,8},{1,17},{17,1},{9,25},{25,9},{2,18},{18... | collective-permute-start | bytes 1179656 | tf_op jit(solution)/shard_map/ppermute | solution.py:49
  272.3 25.0 %collective-permute-start.42 = (bf16[192,2048]{1,0:T(8,128)(2,1)}, bf16[192,2048]{1,0:T(8,128)(2,1)S(1)}, u32[]{:S(2)}, u32[]{:S(2)}) collective-permute-start(bf16[192,2048]{1,0:T(8,128)(2,1)} %get-tuple-element.303.refs_5_), channel_id=1, source_target_pairs={{0,1},{1,0},{2,3},{3,2},{4,5},{5,4},{6,7},{7,6},{8,9},{9,8},{10,11... | collective-permute-start | bytes 2359304 | tf_op jit(solution)/shard_map/ppermute | solution.py:43
  355.2 164.5 %reduce-scatter.9.cloned.1.call-start = ((), (), s32[]{:S(2)}) async-start(), calls=%async_computation.14 | async-start | bytes 7208960 | tf_op jit(solution)/shard_map/reduce_scatter | solution.py:132
  411.2 140.8 %reduce-scatter.11.cloned.1.call-start = ((), (), s32[]{:S(2)}) async-start(), calls=%async_computation.15 | async-start | bytes 983040 | tf_op jit(solution)/shard_map/reduce_scatter | solution.py:132
  419.2 28.5 %collective-permute-start.60 = (bf16[192,2048]{1,0:T(8,128)(2,1)}, bf16[192,2048]{1,0:T(8,128)(2,1)S(1)}, u32[]{:S(2)}, u32[]{:S(2)}) collective-permute-start(bf16[192,2048]{1,0:T(8,128)(2,1)} %get-tuple-element.372.refs_5_.refs_13_), channel_id=1, source_target_pairs={{0,1},{1,0},{2,3},{3,2},{4,5},{5,4},{6,7},{7,6},{8,9},{9,8},{10,11... | collective-permute-start | bytes 2359304 | tf_op jit(solution)/shard_map/ppermute | solution.py:43
  512.0 94.4 %reduce-scatter.13.cloned.1.call-start = ((), (), s32[]{:S(2)}) async-start(), calls=%async_computation.16 | async-start | bytes 2621440 | tf_op jit(solution)/shard_map/reduce_scatter | solution.py:132
  520.7 106.9 %collective-permute-start.76 = (bf16[192,2048]{1,0:T(8,128)(2,1)}, bf16[192,2048]{1,0:T(8,128)(2,1)}, u32[]{:S(2)}, u32[]{:S(2)}) collective-permute-start(bf16[192,2048]{1,0:T(8,128)(2,1)} %get-tuple-element.380), channel_id=1, source_target_pairs={{0,1},{1,0},{2,3},{3,2},{4,5},{5,4},{6,7},{7,6},{8,9},{9,8},{10,11... | collective-permute-start | bytes 2359304 | tf_op jit(solution)/shard_map/ppermute | solution.py:43
  523.9 111.1 %reduce-scatter.17.cloned.1.call-start = ((), (), s32[]{:S(2)}) async-start(), calls=%async_computation.18 | async-start | bytes 1310720 | tf_op jit(solution)/shard_map/reduce_scatter | solution.py:132
  529.3 100.3 %collective-permute-start.82 = (bf16[96,2048]{1,0:T(8,128)(2,1)}, bf16[96,2048]{1,0:T(8,128)(2,1)}, u32[]{:S(2)}, u32[]{:S(2)}) collective-permute-start(bf16[96,2048]{1,0:T(8,128)(2,1)} %fusion.15), channel_id=1, source_target_pairs={{0,16},{16,0},{8,24},{24,8},{1,17},{17,1},{9,25},{25,9},{2,18},{18... | collective-permute-start | bytes 1179656 | tf_op jit(solution)/shard_map/ppermute | solution.py:49
  531.0 98.6 %collective-permute-start.83 = (bf16[96,2048]{1,0:T(8,128)(2,1)}, bf16[96,2048]{1,0:T(8,128)(2,1)}, u32[]{:S(2)}, u32[]{:S(2)}) collective-permute-start(bf16[96,2048]{1,0:T(8,128)(2,1)} %fusion.13), channel_id=1, source_target_pairs={{0,8},{8,0},{16,24},{24,16},{1,9},{9,1},{17,25},{25,17},{2,10},{10... | collective-permute-start | bytes 1179656 | tf_op jit(solution)/shard_map/ppermute | solution.py:46
  540.1 25.5 %collective-permute-start.90 = (bf16[128,4096]{1,0:T(8,128)(2,1)}, bf16[128,4096]{1,0:T(8,128)(2,1)S(1)}, u32[]{:S(2)}, u32[]{:S(2)}) collective-permute-start(bf16[128,4096]{1,0:T(8,128)(2,1)} %pad_maximum_fusion.1), channel_id=1, source_target_pairs={{0,16},{16,0},{8,24},{24,8},{1,17},{17,1},{9,25},{25,9},{2,18},{18... | collective-permute-start | bytes 3145736 | tf_op jit(solution)/shard_map/ppermute | solution.py:49
  541.5 24.7 %collective-permute-start.89 = (bf16[128,4096]{1,0:T(8,128)(2,1)}, bf16[128,4096]{1,0:T(8,128)(2,1)}, u32[]{:S(2)}, u32[]{:S(2)}) collective-permute-start(bf16[128,4096]{1,0:T(8,128)(2,1)} %pad_maximum_fusion), channel_id=1, source_target_pairs={{0,8},{8,0},{16,24},{24,16},{1,9},{9,1},{17,25},{25,17},{2,10},{10... | collective-permute-start | bytes 3145736 | tf_op jit(solution)/shard_map/ppermute | solution.py:46
  621.6 32.8 %reduce-scatter.15.cloned.1.call-start = ((), (), s32[]{:S(2)}) async-start(), calls=%async_computation.17 | async-start | bytes 1064960 | tf_op jit(solution)/shard_map/reduce_scatter | solution.py:132
  (185 other events, 2049.3 us)
Sparse Core Ops, SparseCore 0:
  9.6 44.3 all-gather.5
  55.5 46.6 all-gather.7
  104.4 23.7 all-gather.9
  129.7 59.9 all-gather.13
  191.7 105.3 all-gather.11
  355.3 55.8 reduce-scatter.6
  413.5 102.0 reduce-scatter.8
  517.9 23.8 reduce-scatter.10
  544.1 43.0 reduce-scatter.12
  590.6 29.5 reduce-scatter.16
  627.7 26.7 reduce-scatter.14
